TPU v7x, 128 devices: a whole 4x4x4 slice. The times are simulated.
128 devices in a mesh: dp: 8 (over y, x_lo), seq: 8 (over z, core), pair: 2 (over x_hi).
Axes of the slice: x: 4 (x_hi: 2, x_lo: 2; x = x_hi * 2 + x_lo), y: 4, z: 4, core: 2. Of those that a mesh axis runs over, the one named last changes fastest.
Arguments:
- teacher_hidden: bfloat16 [2, 8, 2048, 5120], P('pair', 'dp', 'seq'), may hold values from -6 to 6
- student_query: bfloat16 [8, 2048, 5120], P('dp', ('seq', 'pair')), may hold values from -20 to 20
- student_key: bfloat16 [8, 2048, 5120], P('dp', ('seq', 'pair')), may hold values from -20 to 20
- student_value: bfloat16 [8, 2048, 5120], P('dp', ('seq', 'pair')), may hold values from -6 to 6
- residual: bfloat16 [8, 2048, 5120], P('dp', ('seq', 'pair')), may hold values from -6 to 6
- segment_ids: int32 [8, 2048], P('dp'), may hold values from 0 to 7, never falling along the last dimension, each value on 1 to 512 neighbouring positions
- timesteps: int32 [8, 8], P('dp'), may hold values from 0 to 999
- guide_scales: int32 [8, 8], P('dp'), may hold values from 8 to 64
- time_proj: bfloat16 [256, 10240], P(None, ('seq', 'pair')), may hold values from -0.375 to 0.375
- guide_proj: bfloat16 [256, 10240], P(None, ('seq', 'pair')), may hold values from -0.375 to 0.375
- teach_head: bfloat16 [5120, 64], replicated, may hold values from -0.078125 to 0.078125
- stud_head: bfloat16 [5120, 64], replicated, may hold values from -0.078125 to 0.078125
- out_proj: bfloat16 [5120, 5120], P('seq'), may hold values from -0.078125 to 0.078125
Outputs:
- grad_out_proj: float32 [5120, 5120], P('seq', ('dp', 'pair'))
- grad_head: float32 [5120, 64], P(('dp', 'seq', 'pair'))
- grad_guidance: float32 [256, 10240], P('dp', ('seq', 'pair'))
All inputs are finite; a program needn't handle non-finite values.
Results may differ from a plain program's by a relative error of at most 0.027.
Values may be sent and summed in bfloat16 or wider, within the bound.
No kernel may reach another device: no remote copies, remote signals or barrier semaphores. Data moves between devices by JAX's collectives and lax.ppermute only.
A program may use at most 128 MiB of HBM per device.

v0:
```python
import functools
import math

import jax
import jax.numpy as jnp
from jax import lax
from jax.experimental import pallas as pl
from jax.experimental.pallas import tpu as pltpu
from jax.sharding import PartitionSpec as P

HEAD_DIM = 128
VMEM_LIMIT = 56 * 1024 * 1024
FREE = pl.CostEstimate(flops=0, bytes_accessed=0, transcendentals=0)


def side(core):
    return 1 if core == 0 else -1


def seq_shift(value, apart):
    return lax.ppermute(value, "seq", [(i, ((i // 2 + apart) % 4) * 2 + i % 2) for i in range(8)])


def seq_ring(value):
    return lax.ppermute(value, "seq", [(i, ((i // 2 + side(i % 2)) % 4) * 2 + i % 2) for i in range(8)])


def core_swap(value):
    return lax.ppermute(value, "seq", [(i, i ^ 1) for i in range(8)])


def y_shift(value, apart):
    return lax.ppermute(value, "dp", [(i, ((i // 2 + apart) % 4) * 2 + i % 2) for i in range(8)])


def x_shift(value, apart):
    def target(index):
        data, seq, pair = index // 16, index // 2 % 8, index % 2
        x = (pair * 2 + data % 2 + side(seq % 2) * apart) % 4
        return (data // 2 * 2 + x % 2) * 16 + seq * 2 + x // 2

    return lax.ppermute(value, ("dp", "seq", "pair"), [(i, target(i)) for i in range(128)])


def pair_swap(value):
    return lax.ppermute(value, "pair", [(0, 1), (1, 0)])


def add_rows(left, right):
    return (left.astype(jnp.float32) + right.astype(jnp.float32)).astype(jnp.bfloat16)


def ring_reduce(low, high):
    totals = [seq_ring(low[0]), seq_ring(high[0])]
    for terms in zip(low[1:], high[1:]):
        totals = [seq_ring(add_rows(term, total)) for term, total in zip(terms, totals)]
    return totals


def ring_gather(block):
    blocks = [block]
    for _ in range(3):
        blocks.append(seq_ring(blocks[-1]))
    return blocks


def sinusoid(values, width):
    half = width // 2
    steps = jnp.arange(half, dtype=jnp.float32)
    freqs = jnp.exp(-math.log(10000.0) * steps / half)
    angles = values[..., None] * freqs
    return jnp.concatenate([jnp.cos(angles), jnp.sin(angles)], axis=-1)


def dot_f32(left, right, left_dim, right_dim):
    return lax.dot_general(
        left, right, (((left_dim,), (right_dim,)), ((), ())), preferred_element_type=jnp.float32
    )


def teacher_kernel(hidden_ref, hot_ref, table_ref, head_ref, out_ref):
    rows, width = hidden_ref.shape
    chunks = table_ref.shape[0] // 2
    cols = width // chunks
    hidden = hidden_ref[...].astype(jnp.float32)
    center = hidden - jnp.mean(hidden, axis=-1, keepdims=True)
    inverse = lax.rsqrt(jnp.mean(center * center, axis=-1, keepdims=True) + 1e-06)
    hot = hot_ref[...]
    total = jnp.zeros((rows, head_ref.shape[0]), jnp.float32)
    for i in range(chunks):
        part = slice(i * cols, (i + 1) * cols)
        shift = dot_f32(hot, table_ref[i], 1, 0)
        scale = dot_f32(hot, table_ref[chunks + i], 1, 0)
        normed = center[:, part] * inverse
        model_in = (normed * (1.0 + scale) + shift).astype(jnp.bfloat16)
        total += dot_f32(model_in, head_ref[:, part], 1, 1)
    out_ref[...] = total


def teacher(hidden, hot, table, head):
    rows, width = hidden.shape
    block = 128
    patch = head.shape[0]
    return pl.pallas_call(
        teacher_kernel,
        grid=(rows // block,),
        in_specs=[
            pl.BlockSpec((block, width), lambda i: (i, 0)),
            pl.BlockSpec((block, hot.shape[1]), lambda i: (i, 0)),
            pl.BlockSpec(table.shape, lambda i: (0, 0, 0)),
            pl.BlockSpec(head.shape, lambda i: (0, 0)),
        ],
        out_specs=pl.BlockSpec((block, patch), lambda i: (i, 0)),
        out_shape=jax.ShapeDtypeStruct((rows, patch), jnp.float32),
        compiler_params=pltpu.CompilerParams(vmem_limit_bytes=VMEM_LIMIT),
        cost_estimate=FREE,
        name="teacher",
    )(hidden, hot, table, head)


def pack_kernel(tensors, *refs):
    out_ref = refs[-1]
    groups = out_ref.shape[0]
    for g in range(groups):
        start = 0
        for ref in [refs[t * groups + g] for t in range(tensors)] + list(refs[tensors * groups : -1]):
            out_ref[g, start : start + ref.shape[0]] = ref[...]
            start += ref.shape[0]


def exchange(tensors, *shared):
    rows, width = tensors[0].shape
    groups, count = 8, len(tensors)
    cols = width // groups
    half = groups // 2
    height = count * rows + sum(array.shape[0] for array in shared)
    packed = pl.pallas_call(
        functools.partial(pack_kernel, count),
        grid=(2,),
        in_specs=[
            pl.BlockSpec((rows, cols), functools.partial(lambda g, i: (0, i * half + g), g))
            for _ in tensors
            for g in range(half)
        ]
        + [pl.BlockSpec(array.shape, lambda i: (0, 0)) for array in shared],
        out_specs=pl.BlockSpec((half, height, cols), lambda i: (i, 0, 0)),
        out_shape=jax.ShapeDtypeStruct((groups, height, cols), tensors[0].dtype),
        compiler_params=pltpu.CompilerParams(vmem_limit_bytes=VMEM_LIMIT),
        cost_estimate=FREE,
        name="pack",
    )(*[tensor for tensor in tensors for _ in range(half)], *shared)
    return lax.all_to_all(packed, "seq", 0, 0, tiled=True)


def rows_kernel(in_ref, out_ref):
    out_ref[...] = in_ref[...]


def take_rows(pieces, start, rows):
    blocks, _, cols = pieces.shape
    half = blocks // 2
    return pl.pallas_call(
        rows_kernel,
        grid=(2,),
        in_specs=[pl.BlockSpec((half, rows, cols), lambda i: (i, start // rows, 0))],
        out_specs=pl.BlockSpec((half, rows, cols), lambda i: (i, 0, 0)),
        out_shape=jax.ShapeDtypeStruct((blocks, rows, cols), pieces.dtype),
        compiler_params=pltpu.CompilerParams(vmem_limit_bytes=VMEM_LIMIT),
        cost_estimate=FREE,
        name="take_rows",
    )(pieces)


def attend_kernel(
    low_ref, high_ref, turn_ref, qseg_ref, kseg_ref, value_ref, first_ref, second_ref,
    out_ref, cross_ref, turned_ref, score_ref, top_ref, acc_ref,
):
    block = value_ref.shape[1]
    heads = value_ref.shape[2] // HEAD_DIM
    upper, lower = slice(0, block), slice(block, 2 * block)
    step = pl.program_id(0)
    low, high = low_ref[step], high_ref[step]
    factor = math.log2(math.e) / math.sqrt(HEAD_DIM)
    parts = [slice(h * HEAD_DIM, (h + 1) * HEAD_DIM) for h in range(heads)]
    top_ref[...] = jnp.full_like(top_ref, -1e30)
    acc_ref[...] = jnp.zeros_like(acc_ref)
    query_seg = qseg_ref[0]

    def score(index, carry):
        same = query_seg == kseg_ref[index]
        scores = [
            dot_f32(first_ref[turn_ref[step], lower, part], second_ref[index, :, part], 1, 1) for part in parts
        ]
        for h in range(heads):
            masked = jnp.where(same, scores[h] * factor, -1e30)
            score_ref[index - low, h] = masked
            pair = jnp.maximum(masked[:, :block], masked[:, block:])
            top_ref[h] = jnp.maximum(top_ref[h], pair)
        return carry

    lax.fori_loop(low, high, score, 0)
    for h in range(heads):
        top_ref[h] = jnp.broadcast_to(jnp.max(top_ref[h], axis=-1, keepdims=True), top_ref.shape[1:])
    ones = jnp.ones((2 * block, HEAD_DIM), jnp.bfloat16)

    def mix(index, carry):
        weights = []
        for h in range(heads):
            top = jnp.concatenate([top_ref[h], top_ref[h]], axis=1)
            weights.append(jnp.exp2(score_ref[index - low, h] - top).astype(jnp.bfloat16))
        for h, part in enumerate(parts):
            values = jnp.concatenate([first_ref[index, upper, part], value_ref[index, :, part]], axis=0)
            acc_ref[h] += dot_f32(weights[h], jnp.concatenate([values, ones], axis=1), 1, 0)
        return carry

    lax.fori_loop(low, high, mix, 0)
    result = jnp.concatenate(
        [acc_ref[h, :, :HEAD_DIM] / acc_ref[h, :, HEAD_DIM:] for h in range(heads)], axis=1
    )
    rounded = result.astype(jnp.bfloat16)

    @pl.when(step < 4)
    def _():
        out_ref[0] = rounded

    @pl.when(step >= 4)
    def _():
        cross_ref[0] = rounded

    turned = result.T.astype(jnp.bfloat16)
    arrival = lax.rem(8 - step, 4)
    for core in range(2):

        @pl.when(step // 4 == core)
        def _():
            turned_ref[arrival, :, core * block : (core + 1) * block] = turned


def attend(low, high, turn, query_seg, key_seg, value_other, first, second):
    blocks, block, width = value_other.shape
    chips = blocks // 2
    heads = width // HEAD_DIM

    def fixed(array):
        return pl.BlockSpec(array.shape, lambda j, *_: (0,) * array.ndim, pipeline_mode=pl.Buffered(1))

    return pl.pallas_call(
        attend_kernel,
        grid_spec=pltpu.PrefetchScalarGridSpec(
            num_scalar_prefetch=3,
            grid=(blocks,),
            in_specs=[pl.BlockSpec((1, block, 1), lambda j, *_: (j, 0, 0))]
            + [fixed(array) for array in (key_seg, value_other, first, second)],
            out_specs=[
                pl.BlockSpec((1, block, width), lambda j, *_: (jnp.minimum(j, 3), 0, 0)),
                pl.BlockSpec((1, block, width), lambda j, *_: (jnp.maximum(j - 4, 0), 0, 0)),
                pl.BlockSpec((chips, width, 2 * block), lambda j, *_: (0, 0, 0)),
            ],
            scratch_shapes=[
                pltpu.VMEM((6, heads, block, 2 * block), jnp.float32),
                pltpu.VMEM((heads, block, block), jnp.float32),
                pltpu.VMEM((heads, block, 2 * HEAD_DIM), jnp.float32),
            ],
        ),
        out_shape=[
            jax.ShapeDtypeStruct((chips, block, width), jnp.bfloat16),
            jax.ShapeDtypeStruct((chips, block, width), jnp.bfloat16),
            jax.ShapeDtypeStruct((chips, width, 2 * block), jnp.bfloat16),
        ],
        compiler_params=pltpu.CompilerParams(vmem_limit_bytes=VMEM_LIMIT),
        cost_estimate=FREE,
        name="attend",
    )(low, high, turn, query_seg, key_seg, value_other, first, second)


def project_kernel(own_ref, crossed_ref, w_own_ref, w_crossed_ref, *refs):
    outs, left_ref = refs[:-1], refs[-1]
    chips, block, depth = own_ref.shape

    @pl.when(pl.program_id(0) == 0)
    def _():
        for k in range(chips):
            take, even = slice(k * block, (k + 1) * block), depth // 256 * 256
            left_ref[take, :even] = own_ref[k, :, :even]
            left_ref[take, even : 2 * even] = crossed_ref[k, :, :even]
            left_ref[take, 2 * even : depth + even] = own_ref[k, :, even:]
            left_ref[take, depth + even :] = crossed_ref[k, :, even:]

    even = depth // 256 * 256
    rest = jnp.concatenate([w_own_ref[even:, :], w_crossed_ref[even:, :]], axis=0)
    total = dot_f32(left_ref[:, :even], w_own_ref[:even, :], 1, 0)
    total += dot_f32(left_ref[:, even : 2 * even], w_crossed_ref[:even, :], 1, 0)
    total = (total + dot_f32(left_ref[:, 2 * even :], rest, 1, 0)).astype(jnp.bfloat16)
    start = 0
    for out in outs:
        out[...] = total[start : start + out.shape[0]]
        start += out.shape[0]


def project(own, crossed, w_own, w_crossed):
    chips, block, depth = own.shape
    width = w_own.shape[1]
    tile = 1024
    heights = [block] + [block // 2] * (2 * chips - 2)
    left = pl.BlockSpec(own.shape, lambda i: (0, 0, 0))
    right = pl.BlockSpec((depth, tile), lambda i: (0, i))
    return pl.pallas_call(
        project_kernel,
        grid=(width // tile,),
        in_specs=[left, left, right, right],
        out_specs=[pl.BlockSpec((height, tile), lambda i: (0, i)) for height in heights],
        out_shape=[jax.ShapeDtypeStruct((height, width), jnp.bfloat16) for height in heights],
        scratch_shapes=[pltpu.VMEM((chips * block, 2 * depth), jnp.bfloat16)],
        compiler_params=pltpu.CompilerParams(vmem_limit_bytes=VMEM_LIMIT),
        cost_estimate=FREE,
        name="project",
    )(own, crossed, w_own, w_crossed)


def join_kernel(*refs):
    half = refs[0].shape[0] // 2
    for k, ref in enumerate(refs[:-2]):
        refs[-2][k * half : (k + 1) * half, :] = ref[:half, :]
        refs[-1][k * half : (k + 1) * half, :] = ref[half:, :]


def join(pieces):
    rows, cols = pieces[0].shape
    out = jax.ShapeDtypeStruct((len(pieces) * rows // 2, cols), pieces[0].dtype)
    return pl.pallas_call(
        join_kernel,
        out_shape=[out, out],
        compiler_params=pltpu.CompilerParams(vmem_limit_bytes=VMEM_LIMIT),
        cost_estimate=FREE,
        name="join",
    )(*pieces)


def student_kernel(
    x_ref, own_ref, la_ref, ha_ref, residual_ref, hot_ref, table_ref, head_ref, guided_ref,
    first_ref, second_ref, third_ref, fourth_ref, in_ref, kept_ref, resid_ref,
    stream_ref, normed_ref, dn_ref, dproj_ref,
):
    rows, width = residual_ref.shape
    chunks = table_ref.shape[0] // 2
    cols = width // chunks
    f32 = jnp.float32
    total = jnp.zeros((rows, 1), f32)
    for i in range(chunks):
        part = slice(i * cols, (i + 1) * cols)
        low, high = la_ref[:, part].astype(f32), ha_ref[:, part].astype(f32)
        base = residual_ref[:, part].astype(f32) + own_ref[:, part].astype(f32)
        stream = base + jnp.concatenate([low, high], axis=0)
        stream_ref[:, part] = stream
        total += jnp.sum(stream, axis=-1, keepdims=True)
    mean = total / width
    square = jnp.zeros((rows, 1), f32)
    for i in range(chunks):
        part = slice(i * cols, (i + 1) * cols)
        center = stream_ref[:, part] - mean
        square += jnp.sum(center * center, axis=-1, keepdims=True)
    inverse = lax.rsqrt(square / width + 1e-06)
    hot = hot_ref[...]
    velocity = jnp.zeros((rows, head_ref.shape[0]), f32)
    for i in range(chunks):
        part = slice(i * cols, (i + 1) * cols)
        normed = (stream_ref[:, part] - mean) * inverse
        shift = dot_f32(hot, table_ref[i], 1, 0)
        scale = 1.0 + dot_f32(hot, table_ref[chunks + i], 1, 0)
        model_in = (normed * scale + shift).astype(jnp.bfloat16)
        normed_ref[:, part] = normed
        kept_ref[:, part] = normed.astype(jnp.bfloat16)
        dn_ref[:, part] = scale
        in_ref[:, part] = model_in
        velocity += dot_f32(model_in, head_ref[:, part], 1, 1)
    scale_back = 1.0 / math.sqrt(16384)
    resid = ((velocity - guided_ref[...]) * scale_back).astype(jnp.bfloat16)
    resid_ref[...] = resid
    first = jnp.zeros((rows, 1), f32)
    second = jnp.zeros((rows, 1), f32)
    for i in range(chunks):
        part = slice(i * cols, (i + 1) * cols)
        cotangent = dot_f32(resid, head_ref[:, part], 1, 0)
        normed = normed_ref[:, part]
        dnorm = cotangent * dn_ref[:, part]
        dn_ref[:, part] = dnorm
        first += jnp.sum(dnorm, axis=-1, keepdims=True)
        second += jnp.sum(dnorm * normed, axis=-1, keepdims=True)
    first = first / width
    second = second / width

    def back(chunk):
        part = slice(chunk * cols, (chunk + 1) * cols)
        return inverse * (dn_ref[:, part] - first - normed_ref[:, part] * second)

    side = cols // 2
    for lo in range(2):
        for y in range(0, 4, 2):
            even, odd = back(2 * y + lo), back(2 * y + 2 + lo)
            for hi in range(2):
                cut = slice(hi * side, (hi + 1) * side)
                both = jnp.concatenate([even[:, cut], odd[:, cut]], axis=1)
                dproj_ref[hi * 2 + lo, :, (y // 2) * cols : (y // 2 + 1) * cols] = both.astype(jnp.bfloat16)
    for apart, ref in enumerate((first_ref, second_ref, third_ref, fourth_ref)):
        ref[...] = dproj_ref[lax.rem(x_ref[0] + 4 + x_ref[1] * apart, 4)]

def student(chip_x, own, received, residual, hot, table, head, guided):
    rows, width = residual.shape
    quarter = width // 4
    arrays = (own, *received, residual, hot, table, head, guided)
    outs = [(rows, quarter)] * 4 + [(rows, width), (rows, width), guided.shape]
    return pl.pallas_call(
        student_kernel,
        grid_spec=pltpu.PrefetchScalarGridSpec(
            num_scalar_prefetch=1,
            grid=(1,),
            in_specs=[
                pl.BlockSpec(array.shape, functools.partial(lambda dims, i, p: (0,) * dims, array.ndim))
                for array in arrays
            ],
            out_specs=[pl.BlockSpec(out, lambda i, p: (0, 0)) for out in outs],
            scratch_shapes=[
                pltpu.VMEM((rows, width), jnp.float32),
                pltpu.VMEM((rows, width), jnp.float32),
                pltpu.VMEM((rows, width), jnp.float32),
                pltpu.VMEM((4, rows, quarter), jnp.bfloat16),
            ],
        ),
        out_shape=[jax.ShapeDtypeStruct(out, jnp.bfloat16) for out in outs],
        compiler_params=pltpu.CompilerParams(vmem_limit_bytes=VMEM_LIMIT),
        cost_estimate=FREE,
        name="student",
    )(chip_x, *arrays)


def sums_kernel(
    place_ref, in_ref, normed_ref, resid_ref, hot_ref, head_ref, own_ref, cross_ref, headpart_ref, mod_ref, out_ref
):
    f32, bf16 = jnp.float32, jnp.bfloat16
    chunks, cols, patch = headpart_ref.shape
    samples = mod_ref.shape[1]
    resid = resid_ref[...]
    hot = hot_ref[:, hot_ref.shape[1] - samples :]
    for i in range(chunks):
        part = slice(i * cols, (i + 1) * cols)
        cotangent = dot_f32(resid, head_ref[:, part], 1, 0)
        headpart_ref[i] = dot_f32(in_ref[:, part], resid, 0, 0)
        mod_ref[i] = dot_f32(hot, cotangent.astype(bf16), 0, 0)
        scaled = cotangent * normed_ref[:, part].astype(f32)
        mod_ref[chunks + i] = dot_f32(hot, scaled.astype(bf16), 0, 0)
    strip = cols // (2 * chunks)
    blank = jnp.zeros((strip, cols - chunks * patch), f32)
    for i in range(2 * chunks):
        take = slice(i * strip, (i + 1) * strip)
        head_rows = jnp.concatenate([headpart_ref[k, take, :] for k in range(chunks)] + [blank], axis=1)
        out_ref[i] = jnp.concatenate([head_rows, mod_ref[i]], axis=0).astype(bf16)
    for core, ref in enumerate((own_ref, cross_ref)):
        for pair in range(2):
            for chip in range(4):
                z, c, p = lax.rem(place_ref[0] + chip, 4), lax.rem(place_ref[1] + core, 2), lax.rem(place_ref[2] + pair, 2)
                ref[pair, chip] = out_ref[z * 4 + c * 2 + p]


def local_sums(place, model_in, normed, resid, hot, head, samples, devices):
    rows, width = model_in.shape
    chunk = 2 * width // devices
    part = (chunk // devices + samples, chunk)
    arrays = (model_in, normed, resid, hot, head)
    out = (2, devices // 4) + part
    return pl.pallas_call(
        sums_kernel,
        grid_spec=pltpu.PrefetchScalarGridSpec(
            num_scalar_prefetch=1,
            grid=(1,),
            in_specs=[pl.BlockSpec(array.shape, lambda i, p: (0, 0)) for array in arrays],
            out_specs=[pl.BlockSpec(out, lambda i, p: (0, 0, 0, 0)) for _ in range(2)],
            scratch_shapes=[
                pltpu.VMEM((devices // 2, chunk, head.shape[0]), jnp.float32),
                pltpu.VMEM((devices, samples, chunk), jnp.float32),
                pltpu.VMEM((devices,) + part, jnp.bfloat16),
            ],
        ),
        out_shape=[jax.ShapeDtypeStruct(out, jnp.bfloat16) for _ in range(2)],
        compiler_params=pltpu.CompilerParams(vmem_limit_bytes=VMEM_LIMIT),
        cost_estimate=FREE,
        name="local_sums",
    )(place, *arrays)


def block_rows(refs, position):
    half = 64
    places = (position, position, 2 - position, 2 - position)
    return jnp.concatenate([ref[at * half : (at + 1) * half, :] for ref, at in zip(refs, places)], axis=0)


def early_kernel(*refs):
    out_ref, lefts, refs = refs[-1], refs[:4], refs[4:-1]
    total = jnp.zeros(out_ref.shape, jnp.float32)
    for arrival in range(4):
        rows = jnp.concatenate([refs[0][...], refs[1][...]], axis=0)
        total += dot_f32(lefts[0][arrival], rows, 1, 0)
        refs = refs[2:]
    for arrival in range(3):
        for position in range(3):
            total += dot_f32(lefts[1 + position][arrival], block_rows(refs[:4], position), 1, 0)
        refs = refs[4:]
    out_ref[...] = total


def early_product(lefts, mine, others):
    tile = 256
    flat = [part for blocks in (mine, others) for parts in blocks for part in parts]
    depth, width = lefts[0].shape[1], flat[0].shape[1]
    return pl.pallas_call(
        early_kernel,
        grid=(width // tile,),
        in_specs=[pl.BlockSpec(left.shape, lambda i: (0, 0, 0)) for left in lefts]
        + [pl.BlockSpec((part.shape[0], tile), lambda i: (0, i)) for part in flat],
        out_specs=pl.BlockSpec((depth, tile), lambda i: (0, i)),
        out_shape=jax.ShapeDtypeStruct((depth, width), jnp.float32),
        compiler_params=pltpu.CompilerParams(vmem_limit_bytes=VMEM_LIMIT),
        cost_estimate=FREE,
        name="early_product",
    )(*lefts, *flat)


def late_kernel(y_ref, first_ref, second_ref, third_ref, a_ref, b_ref, c_ref, d_ref, early_ref, *refs):
    outs, turned_ref = refs[:-1], refs[-1]
    step = pl.program_id(0)
    tile = early_ref.shape[1]
    total = early_ref[...]
    for position, left in enumerate((first_ref, second_ref, third_ref)):
        total += dot_f32(left[0], block_rows((a_ref, b_ref, c_ref, d_ref), position), 1, 0)
    turned_ref[pl.ds(pl.multiple_of(step * tile, tile), tile), :] = total.T.astype(jnp.bfloat16)

    @pl.when(step == pl.num_programs(0) - 1)
    def _():
        rows = outs[0].shape[0]
        for apart, out in enumerate(outs):
            start = pl.multiple_of(lax.rem(y_ref[0] + apart, 4) * rows, rows)
            out[...] = turned_ref[pl.ds(start, rows), :]


def late_product(chip_y, lefts, flat, early):
    depth, width = early.shape
    tile = 256
    return pl.pallas_call(
        late_kernel,
        grid_spec=pltpu.PrefetchScalarGridSpec(
            num_scalar_prefetch=1,
            grid=(width // tile,),
            in_specs=[pl.BlockSpec((1,) + left.shape[1:], lambda i, p: (3, 0, 0)) for left in lefts]
            + [pl.BlockSpec((half.shape[0], tile), lambda i, p: (0, i)) for half in flat]
            + [pl.BlockSpec((depth, tile), lambda i, p: (0, i))],
            out_specs=[pl.BlockSpec((width // 4, depth), lambda i, p: (0, 0)) for _ in range(4)],
            scratch_shapes=[pltpu.VMEM((width, depth), jnp.bfloat16)],
        ),
        out_shape=[jax.ShapeDtypeStruct((width // 4, depth), jnp.bfloat16) for _ in range(4)],
        compiler_params=pltpu.CompilerParams(vmem_limit_bytes=VMEM_LIMIT),
        cost_estimate=FREE,
        name="late_product",
    )(chip_y, *lefts, *flat, early)


def local(
    teacher_hidden,
    student_query,
    student_key,
    student_value,
    residual,
    segment_ids,
    timesteps,
    guide_scales,
    time_proj,
    guide_proj,
    teach_head,
    stud_head,
    out_proj,
):
    bf16, f32 = jnp.bfloat16, jnp.float32
    seq_pos, pair_pos, data_pos = lax.axis_index("seq"), lax.axis_index("pair"), lax.axis_index("dp")
    chip_z, core = seq_pos // 2, seq_pos % 2
    chip_y, chip_x = data_pos // 2, pair_pos * 2 + data_pos % 2
    segment = segment_ids[0]
    samples = timesteps.shape[1]
    freq = time_proj.shape[0]

    guidance = guide_scales[0].astype(f32) / 8.0
    t_emb = sinusoid(timesteps[0].astype(f32), freq).astype(bf16)
    g_emb = sinusoid(1000.0 * guidance, freq).astype(bf16)
    teach_cols = jnp.dot(t_emb, time_proj, preferred_element_type=f32)
    stud_cols = teach_cols + jnp.dot(g_emb, guide_proj, preferred_element_type=f32)
    columns = jnp.concatenate([teach_cols, stud_cols], axis=0).astype(bf16)

    stud_rows = student_query.shape[1]
    ids = jnp.arange(2 * samples, dtype=jnp.int32)[None, :]
    hidden = teacher_hidden[0, 0]
    teach_seg = lax.dynamic_slice_in_dim(segment, seq_pos * hidden.shape[0], hidden.shape[0])
    stud_seg = lax.dynamic_slice_in_dim(teach_seg, pair_pos * stud_rows, stud_rows)
    teach_hot = (teach_seg[:, None] == ids).astype(bf16)
    stud_hot = (stud_seg[:, None] == ids - samples).astype(bf16)
    guide_tok = jnp.sum(
        jnp.where(stud_seg[:, None] == ids[:, :samples], guidance[None, :], 0.0), axis=1, keepdims=True
    )

    by_block = segment.reshape(8, 2, stud_rows)
    own_seg = lax.dynamic_index_in_dim(by_block, pair_pos, 1, keepdims=False)
    other_seg = lax.dynamic_index_in_dim(by_block, 1 - pair_pos, 1, keepdims=False)
    turn = jnp.arange(8, dtype=jnp.int32)
    away = ((1 - 2 * core) * (1 - 2 * (turn // 4)) * (turn % 4) + 4) % 4
    spots = (chip_z + away) % 4 * 2 + (core + turn // 4) % 2
    query_seg = own_seg[spots]
    low = jnp.sum((segment[None, :] < query_seg[:, :1]).astype(jnp.int32), axis=1) // 256
    high = (jnp.sum((segment[None, :] <= query_seg[:, -1:]).astype(jnp.int32), axis=1) + 255) // 256
    segs = query_seg[:, :, None], jnp.concatenate([own_seg, other_seg], axis=1)[:, None, :]

    key_crossed, weights_crossed = pair_swap(student_key[0]), core_swap(out_proj)
    first = exchange([student_value[0], student_query[0]], columns)
    first, key_crossed = lax.optimization_barrier((first, key_crossed))
    table = take_rows(first, 2 * stud_rows, columns.shape[0])
    table_other = pair_swap(table)
    value_own, table_other = lax.optimization_barrier((take_rows(first, 0, stud_rows), table_other))
    value_other = pair_swap(value_own)
    second = exchange([student_key[0], key_crossed])
    lower, upper = jnp.where(pair_pos == 0, table, table_other), jnp.where(pair_pos == 0, table_other, table)
    table = jnp.stack([lower, upper], axis=1).reshape((16,) + columns.shape)
    velocity = teacher(hidden, teach_hot, table, teach_head.T)
    own_vel = lax.dynamic_slice_in_dim(velocity, pair_pos * stud_rows, stud_rows, 0)
    sent_vel = lax.dynamic_slice_in_dim(velocity, (1 - pair_pos) * stud_rows, stud_rows, 0)
    value_other, second, weights_crossed, low, high, segs, sent_vel = lax.optimization_barrier(
        (value_other, second, weights_crossed, low, high, segs, sent_vel)
    )
    attn_own, attn_cross, turned = attend(
        low, high, spots, *segs, value_other, first, second
    )

    own, *terms = project(attn_own, core_swap(attn_cross), out_proj, weights_crossed)
    received = ring_reduce(terms[4::-2], terms[5::-2])
    lefts = [turned]
    for _ in range(2):
        lefts.append(x_shift(lefts[-1], 1))
    other_vel = pair_swap(sent_vel.astype(bf16)).astype(f32)
    cond_vel = jnp.where(pair_pos == 0, own_vel, other_vel)
    uncond_vel = jnp.where(pair_pos == 0, other_vel, own_vel)
    guided = uncond_vel + guide_tok * (cond_vel - uncond_vel)
    own, lefts[1:3], guided = lax.optimization_barrier((own, lefts[1:3], guided))

    x_at = jnp.stack([chip_x, 1 - 2 * core]).astype(jnp.int32)
    y_at = jnp.reshape(chip_y, (1,)).astype(jnp.int32)
    *quarters, model_in, normed, resid = student(
        x_at, own, received, residual[0], stud_hot, table, stud_head.T, guided
    )

    from_x = [x_shift(quarters[apart], apart) for apart in (1, 2, 3)]
    mine = [quarters[0], seq_ring(quarters[0])]
    at = jnp.stack([chip_z, core, pair_pos]).astype(jnp.int32)
    kept, sent = local_sums(at, model_in, normed, resid, stud_hot, stud_head.T, samples, table.shape[0])
    from_x, kept, sent, mine[1] = lax.optimization_barrier((from_x, kept, sent, mine[1]))
    for _ in range(2):
        mine.append(seq_ring(mine[-1]))
    mine = [(block, core_swap(block)) for block in mine]
    came = core_swap(sent)
    kept, sent = add_rows(kept[0], came[0]), add_rows(kept[1], came[1])
    came = pair_swap(sent)
    came, lefts[2] = lax.optimization_barrier((came, lefts[2]))
    lefts.append(x_shift(lefts[2], 1))
    others = list(zip(*[ring_gather(half) for half in join(from_x)]))
    kept = add_rows(kept, came)
    sums = kept[0].astype(f32)
    for apart in (1, 2, 3):
        sums = sums + seq_shift(kept[apart], apart).astype(f32)
    sums = sums.astype(bf16)
    others_crossed = [tuple(core_swap(half) for half in pair) for pair in others[:3]]
    early = early_product(lefts, mine, [own + crossed for own, crossed in zip(others, others_crossed)])
    early, last = lax.optimization_barrier((early, others[3]))
    product = late_product(y_at, lefts[1:], [*last, *[core_swap(half) for half in last]], early)

    strip, patch, cols = sums.shape[0] - samples, stud_head.shape[1], sums.shape[1]
    head_sums = sums[:strip, : 8 * patch].reshape(strip, 8, patch).transpose(1, 0, 2)
    d_mod = jnp.broadcast_to(sums[None, strip:], (8, samples, cols))
    emb = g_emb.reshape(samples, 8, freq // 8).transpose(1, 0, 2)
    sent = jnp.concatenate(
        [
            jnp.pad(head_sums, ((0, 0), (0, 0), (0, 128 - patch))),
            jnp.pad(d_mod, ((0, 0), (0, strip - samples), (0, 0))),
            jnp.pad(emb, ((0, 0), (0, strip - samples), (0, 128 - freq // 8))),
        ],
        axis=2,
    )
    got = lax.all_to_all(sent, "dp", 0, 0, tiled=True)
    grad_head = jnp.sum(got[:, :, :patch].astype(f32), axis=0)
    d_mods = got[:, :samples, 128 : 128 + cols].reshape(8 * samples, cols)
    embs = got[:, :samples, 128 + cols : 128 + cols + freq // 8].reshape(8 * samples, freq // 8)
    grad_guidance = dot_f32(embs, d_mods, 0, 0)

    total = product[0].astype(f32)
    for apart in (2, 1, 3):
        total = total + y_shift(product[apart], apart).astype(f32)
    grad_out_proj = total.T
    return (grad_out_proj, grad_head, grad_guidance)


def solution(mesh):
    placed = (
        P("pair", "dp", "seq", None),
        P("dp", ("seq", "pair"), None),
        P("dp", ("seq", "pair"), None),
        P("dp", ("seq", "pair"), None),
        P("dp", ("seq", "pair"), None),
        P("dp", None),
        P("dp", None),
        P("dp", None),
        P(None, ("seq", "pair")),
        P(None, ("seq", "pair")),
        P(),
        P(),
        P("seq", None),
    )
    return jax.shard_map(
        local,
        mesh=mesh,
        in_specs=placed,
        out_specs=(
            P("seq", ("dp", "pair")),
            P(("dp", "seq", "pair"), None),
            P("dp", ("seq", "pair")),
        ),
        check_vma=False,
    )
```

profile of v0, /device:TPU:1, one launch (start us, length us, event | category | flops | bytes accessed | tf_op | source)
XLA Modules:
  0.0 307.5 jit_solution(7924888776447039298)
XLA Ops:
  5.5 3.1 %pack.2 = bf16[8,272,640]{2,1,0:T(8,128)(2,1)} custom-call(bf16[128,5120]{1,0:T(8,128)(2,1)} %bitcast.69, bf16[128,5120]{1,0:T(8,128)(2,1)} %bitcast.70, bf16[128,5120]{1,0:T(8,128)(2,1)} %bitcast.71, bf16[128,5120]{1,0:T(8,128)(2,1)} %bitcast.72, bf16[128,5120]{1,0:T(8,128)(2,1)} %bitcast.73, bf16[128,5120]{1,0:T(8,128)(2,1)} %bitcast.74, ...), custom_call_target="tpu_custom_call" | custom-call | tf_op jit(solution)/shard_map/pack/pallas_call | solution.py:137
  8.7 5.5 %all-to-all-start = ((bf16[8,272,640]{2,1,0:T(8,128)(2,1)}), bf16[8,272,640]{2,1,0:T(8,128)(2,1)S(1)}, u32[]{:S(2)}, u32[]{:S(2)}) async-start(bf16[8,272,640]{2,1,0:T(8,128)(2,1)} %pack.2), calls=%async_computation | async-start | bytes 5570560 | tf_op jit(solution)/shard_map/all_to_all | solution.py:152
  16.9 29.5 %collective-permute-done.refs_4_.refs_5_.refs_6_.refs_7_ = bf16[128,5120]{1,0:T(8,128)(2,1)} collective-permute-done((bf16[128,5120]{1,0:T(8,128)(2,1)}, bf16[128,5120]{1,0:T(8,128)(2,1)}, u32[]{:S(2)}, u32[]{:S(2)}) %collective-permute-start) | collective-permute-done | bytes 1310752 | tf_op jit(solution)/shard_map/ppermute | solution.py:46
  47.9 4.1 %pack.3 = bf16[8,256,640]{2,1,0:T(8,128)(2,1)} custom-call(bf16[128,5120]{1,0:T(8,128)(2,1)} %bitcast.78, bf16[128,5120]{1,0:T(8,128)(2,1)} %bitcast.79, bf16[128,5120]{1,0:T(8,128)(2,1)} %bitcast.80, bf16[128,5120]{1,0:T(8,128)(2,1)} %bitcast.81, bf16[128,5120]{1,0:T(8,128)(2,1)} %collective-permute-done.refs_4_.refs_5_.refs_6_.refs_7_, ...), custom_call_target="tpu_custom_call" | custom-call | tf_op jit(solution)/shard_map/pack/pallas_call | solution.py:137
  52.0 4.4 %all-to-all-start.1 = ((bf16[8,256,640]{2,1,0:T(8,128)(2,1)}), bf16[8,256,640]{2,1,0:T(8,128)(2,1)S(1)}, u32[]{:S(2)}, u32[]{:S(2)}) async-start(bf16[8,256,640]{2,1,0:T(8,128)(2,1)} %pack.3), calls=%async_computation.1 | async-start | bytes 5242880 | tf_op jit(solution)/shard_map/all_to_all | solution.py:152
  72.5 6.9 %teacher.1 = f32[256,64]{1,0:T(8,128)} custom-call(bf16[256,5120]{1,0:T(8,128)(2,1)} %bitcast.84, bf16[256,16]{1,0:T(8,128)(2,1)} %fusion.10.hot_ref, bf16[16,16,640]{2,1,0:T(8,128)(2,1)} %bitcast.82, bf16[64,5120]{1,0:T(8,128)(2,1)} %bitcast.88), custom_call_target="tpu_custom_call" | custom-call | tf_op jit(solution)/shard_map/teacher/pallas_call | solution.py:104
  80.2 16.4 %collective-permute-done.2.value_ref = bf16[8,128,640]{2,1,0:T(8,128)(2,1)} collective-permute-done((bf16[8,128,640]{2,1,0:T(8,128)(2,1)}, bf16[8,128,640]{2,1,0:T(8,128)(2,1)}, u32[]{:S(2)}, u32[]{:S(2)}) %collective-permute-start.2) | collective-permute-done | bytes 1310752 | tf_op jit(solution)/shard_map/ppermute | solution.py:46
  98.3 18.3 %attend.1 = (bf16[4,128,640]{2,1,0:T(8,128)(2,1)}, bf16[4,128,640]{2,1,0:T(8,128)(2,1)}, bf16[4,640,256]{2,1,0:T(8,128)(2,1)}) custom-call(s32[8]{0:T(128)} %get-tuple-element.59.low_ref, s32[8]{0:T(128)} %get-tuple-element.60.high_ref, s32[8]{0:T(128)} %fusion.35.turn_ref, s32[8,128,1]{2,1,0:T(8,128)} %copy.28.qseg_ref, ...), custom_call_target="tpu_custom_call" | custom-call | tf_op jit(solution)/shard_map/attend/pallas_call | solution.py:247
  118.6 5.1 %collective-permute-start.5 = (bf16[4,640,256]{2,1,0:T(8,128)(2,1)}, bf16[4,640,256]{2,1,0:T(8,128)(2,1)S(1)}, u32[]{:S(2)}, u32[]{:S(2)}) collective-permute-start(bf16[4,640,256]{2,1,0:T(8,128)(2,1)} %get-tuple-element.69.refs_0_), channel_id=1, source_target_pairs={{0,16},{1,17},{2,19},{3,18},{4,20},{5,21},{6,23},{7,22},{8,24},{9,... | collective-permute-start | bytes 3932168 | tf_op jit(solution)/shard_map/ppermute | solution.py:42
  124.6 11.8 %project.1 = (bf16[128,5120]{1,0:T(8,128)(2,1)}, bf16[64,5120]{1,0:T(8,128)(2,1)}, bf16[64,5120]{1,0:T(8,128)(2,1)}, bf16[64,5120]{1,0:T(8,128)(2,1)}, bf16[64,5...) custom-call(bf16[4,128,640]{2,1,0:T(8,128)(2,1)} %get-tuple-element.65.own_ref, ...), custom_call_target="tpu_custom_call" | custom-call | tf_op jit(solution)/shard_map/project/pallas_call | solution.py:307
  141.6 5.0 %collective-permute-done.11 = bf16[64,5120]{1,0:T(8,128)(2,1)S(1)} collective-permute-done((bf16[64,5120]{1,0:T(8,128)(2,1)}, bf16[64,5120]{1,0:T(8,128)(2,1)S(1)}, u32[]{:S(2)}, u32[]{:S(2)}) %collective-permute-start.11) | collective-permute-done | bytes 655392 | tf_op jit(solution)/shard_map/ppermute | solution.py:25
  147.9 3.4 %collective-permute-start.12 = (bf16[64,5120]{1,0:T(8,128)(2,1)S(1)}, bf16[64,5120]{1,0:T(8,128)(2,1)S(1)}, u32[]{:S(2)}, u32[]{:S(2)}) collective-permute-start(bf16[64,5120]{1,0:T(8,128)(2,1)S(1)} %add_convert_fusion.1), channel_id=1, source_target_pairs={{0,4},{2,14},{4,8},{6,2},{8,12},{10,6},{12,0},{14,10},{1,5},{3,15}... | collective-permute-start | bytes 1966088 | tf_op jit(solution)/shard_map/ppermute | solution.py:25
  153.8 3.4 %collective-permute-start.9 = (bf16[64,5120]{1,0:T(8,128)(2,1)S(1)}, bf16[64,5120]{1,0:T(8,128)(2,1)S(1)}, u32[]{:S(2)}, u32[]{:S(2)}) collective-permute-start(bf16[64,5120]{1,0:T(8,128)(2,1)S(1)} %add_convert_fusion.3), channel_id=1, source_target_pairs={{0,4},{2,14},{4,8},{6,2},{8,12},{10,6},{12,0},{14,10},{1,5},{3,15}... | collective-permute-start | bytes 1966088 | tf_op jit(solution)/shard_map/ppermute | solution.py:25
  157.2 3.4 %collective-permute-done.12 = bf16[64,5120]{1,0:T(8,128)(2,1)S(1)} collective-permute-done((bf16[64,5120]{1,0:T(8,128)(2,1)S(1)}, bf16[64,5120]{1,0:T(8,128)(2,1)S(1)}, u32[]{:S(2)}, u32[]{:S(2)}) %collective-permute-start.12) | collective-permute-done | bytes 655392 | tf_op jit(solution)/shard_map/ppermute | solution.py:25
  160.7 3.2 %collective-permute-start.13 = (bf16[64,5120]{1,0:T(8,128)(2,1)S(1)}, bf16[64,5120]{1,0:T(8,128)(2,1)S(1)}, u32[]{:S(2)}, u32[]{:S(2)}) collective-permute-start(bf16[64,5120]{1,0:T(8,128)(2,1)S(1)} %add_convert_fusion), channel_id=1, source_target_pairs={{0,4},{2,14},{4,8},{6,2},{8,12},{10,6},{12,0},{14,10},{1,5},{3,15}... | collective-permute-start | bytes 1966088 | tf_op jit(solution)/shard_map/ppermute | solution.py:25
  163.9 3.7 %collective-permute-done.9 = bf16[64,5120]{1,0:T(8,128)(2,1)S(1)} collective-permute-done((bf16[64,5120]{1,0:T(8,128)(2,1)S(1)}, bf16[64,5120]{1,0:T(8,128)(2,1)S(1)}, u32[]{:S(2)}, u32[]{:S(2)}) %collective-permute-start.9) | collective-permute-done | bytes 655392 | tf_op jit(solution)/shard_map/ppermute | solution.py:25
  167.8 3.2 %collective-permute-start.10 = (bf16[64,5120]{1,0:T(8,128)(2,1)S(1)}, bf16[64,5120]{1,0:T(8,128)(2,1)S(1)}, u32[]{:S(2)}, u32[]{:S(2)}) collective-permute-start(bf16[64,5120]{1,0:T(8,128)(2,1)S(1)} %add_convert_fusion.2), channel_id=1, source_target_pairs={{0,4},{2,14},{4,8},{6,2},{8,12},{10,6},{12,0},{14,10},{1,5},{3,15}... | collective-permute-start | bytes 1966088 | tf_op jit(solution)/shard_map/ppermute | solution.py:25
  172.3 3.7 %collective-permute-done.7 = bf16[128,64]{1,0:T(8,128)(2,1)S(1)} collective-permute-done((bf16[128,64]{1,0:T(8,128)(2,1)S(1)}, bf16[128,64]{1,0:T(8,128)(2,1)S(1)}, u32[]{:S(2)}, u32[]{:S(2)}) %collective-permute-start.7) | collective-permute-done | bytes 16416 | tf_op jit(solution)/shard_map/ppermute | solution.py:46
  176.7 5.0 %collective-permute-done.10.la_ref = bf16[64,5120]{1,0:T(8,128)(2,1)S(1)} collective-permute-done((bf16[64,5120]{1,0:T(8,128)(2,1)S(1)}, bf16[64,5120]{1,0:T(8,128)(2,1)S(1)}, u32[]{:S(2)}, u32[]{:S(2)}) %collective-permute-start.10) | collective-permute-done | bytes 655392 | tf_op jit(solution)/shard_map/ppermute | solution.py:25
  182.5 8.9 %student.1 = (bf16[128,1280]{1,0:T(8,128)(2,1)}, bf16[128,1280]{1,0:T(8,128)(2,1)}, bf16[128,1280]{1,0:T(8,128)(2,1)}, bf16[128,1280]{1,0:T(8,128)(2,1)}, bf16[1...) custom-call(s32[2]{0:T(128)} %pad_add_fusion.1.x_ref, ...), custom_call_target="tpu_custom_call" | custom-call | tf_op jit(solution)/shard_map/student/pallas_call | solution.py:412
  194.0 3.1 %collective-permute-start.17 = (bf16[128,1280]{1,0:T(8,128)(2,1)}, bf16[128,1280]{1,0:T(8,128)(2,1)S(1)}, u32[]{:S(2)}, u32[]{:S(2)}) collective-permute-start(bf16[128,1280]{1,0:T(8,128)(2,1)} %get-tuple-element.88.refs_4_), channel_id=1, source_target_pairs={{0,4},{2,14},{4,8},{6,2},{8,12},{10,6},{12,0},{14,10},{1,5},{3,15}... | collective-permute-start | bytes 983048 | tf_op jit(solution)/shard_map/ppermute | solution.py:25
  197.7 5.8 %local_sums.1 = (bf16[2,4,48,640]{3,2,1,0:T(8,128)(2,1)}, bf16[2,4,48,640]{3,2,1,0:T(8,128)(2,1)}) custom-call(s32[3]{0:T(128)} %pad_add_fusion.2.place_ref, bf16[128,5120]{1,0:T(8,128)(2,1)} %get-tuple-element.83.in_ref, bf16[128,5120]{1,0:T(8,128)(2,1)} %get-tuple-element.84.normed_ref, bf16[128,64]{1,0:T(8,128)(2,1)} %get-tuple-element.85.resid_ref, ...), custom_call_target="tpu_custom_call" | custom-call | tf_op jit(solution)/shard_map/local_sums/pallas_call | solution.py:470
  205.1 4.7 %collective-permute-done.16.refs_2_ = bf16[128,1280]{1,0:T(8,128)(2,1)S(1)} collective-permute-done((bf16[128,1280]{1,0:T(8,128)(2,1)}, bf16[128,1280]{1,0:T(8,128)(2,1)S(1)}, u32[]{:S(2)}, u32[]{:S(2)}) %collective-permute-start.16) | collective-permute-done | bytes 327712 | tf_op jit(solution)/shard_map/ppermute | solution.py:42
  221.2 7.3 %collective-permute-done.19 = bf16[4,48,640]{2,1,0:T(8,128)(2,1)S(1)} collective-permute-done((bf16[4,48,640]{2,1,0:T(8,128)(2,1)S(1)}, bf16[4,48,640]{2,1,0:T(8,128)(2,1)S(1)}, u32[]{:S(2)}, u32[]{:S(2)}) %collective-permute-start.19) | collective-permute-done | bytes 245792 | tf_op jit(solution)/shard_map/ppermute | solution.py:46
  234.8 3.7 %collective-permute-start.31 = (bf16[192,1280]{1,0:T(8,128)(2,1)S(1)}, bf16[192,1280]{1,0:T(8,128)(2,1)S(1)}, u32[]{:S(2)}, u32[]{:S(2)}) collective-permute-start(bf16[192,1280]{1,0:T(8,128)(2,1)S(1)} %collective-permute-done.29.refs_16_), channel_id=1, source_target_pairs={{0,2},{2,0},{4,6},{6,4},{8,10},{10,8},{12,14},{14,12},{1,3},{3,1},... | collective-permute-start | bytes 1474568 | tf_op jit(solution)/shard_map/ppermute | solution.py:29
  240.0 3.7 %collective-permute-start.26 = (bf16[128,1280]{1,0:T(8,128)(2,1)S(1)}, bf16[128,1280]{1,0:T(8,128)(2,1)}, u32[]{:S(2)}, u32[]{:S(2)}) collective-permute-start(bf16[128,1280]{1,0:T(8,128)(2,1)S(1)} %collective-permute-done.25.refs_10_), channel_id=1, source_target_pairs={{0,2},{2,0},{4,6},{6,4},{8,10},{10,8},{12,14},{14,12},{1,3},{3,1},... | collective-permute-start | bytes 983048 | tf_op jit(solution)/shard_map/ppermute | solution.py:29
  245.3 3.7 %collective-permute-start.35 = (bf16[192,1280]{1,0:T(8,128)(2,1)S(1)}, bf16[192,1280]{1,0:T(8,128)(2,1)S(1)}, u32[]{:S(2)}, u32[]{:S(2)}) collective-permute-start(bf16[192,1280]{1,0:T(8,128)(2,1)S(1)} %collective-permute-done.33.refs_20_), channel_id=1, source_target_pairs={{0,2},{2,0},{4,6},{6,4},{8,10},{10,8},{12,14},{14,12},{1,3},{3,1},... | collective-permute-start | bytes 1474568 | tf_op jit(solution)/shard_map/ppermute | solution.py:29
  256.2 11.5 %early_product.1.early_ref = f32[640,1280]{1,0:T(8,128)} custom-call(bf16[4,640,256]{2,1,0:T(8,128)(2,1)} %get-tuple-element.69.refs_0_, bf16[4,640,256]{2,1,0:T(8,128)(2,1)} %copy-done.4, bf16[4,640,256]{2,1,0:T(8,128)(2,1)} %copy-done.5, bf16[4,640,256]{2,1,0:T(8,128)(2,1)} %copy-done.6, bf16[128,1280]{1,0:T(8,128)(2,1)} %get-tuple-element.88.refs_4_, ...), custom_call_target="tpu_custom_call" | custom-call | tf_op jit(solution)/shard_map/early_product/pallas_call | solution.py:514
  271.3 4.2 %all-to-all-start.2 = ((bf16[8,40,896]{2,1,0:T(8,128)(2,1)}), bf16[8,40,896]{2,1,0:T(8,128)(2,1)S(1)}, u32[]{:S(2)}, u32[]{:S(2)}) async-start(bf16[8,40,896]{2,1,0:T(8,128)(2,1)} %fusion.6), calls=%async_computation.2 | async-start | bytes 1146880 | tf_op jit(solution)/shard_map/all_to_all | solution.py:690
  276.5 7.0 %late_product.1 = (bf16[320,640]{1,0:T(8,128)(2,1)}, bf16[320,640]{1,0:T(8,128)(2,1)}, bf16[320,640]{1,0:T(8,128)(2,1)}, bf16[320,640]{1,0:T(8,128)(2,1)}) custom-call(s32[1]{0:T(128)} %bitcast.y_ref, bf16[4,640,256]{2,1,0:T(8,128)(2,1)} %copy-done.4, bf16[4,640,256]{2,1,0:T(8,128)(2,1)} %copy-done.5, bf16[4,640,256]{2,1,0:T(8,128)(2,1)} %copy-done.6, ...), custom_call_target="tpu_custom_call" | custom-call | tf_op jit(solution)/shard_map/late_product/pallas_call | solution.py:547
  290.6 5.0 %collective-permute-done.41 = bf16[320,640]{1,0:T(8,128)(2,1)S(1)} collective-permute-done((bf16[320,640]{1,0:T(8,128)(2,1)}, bf16[320,640]{1,0:T(8,128)(2,1)S(1)}, u32[]{:S(2)}, u32[]{:S(2)}) %collective-permute-start.41) | collective-permute-done | bytes 409632 | tf_op jit(solution)/shard_map/ppermute | solution.py:33
  295.6 9.8 %collective-permute-done.42 = bf16[320,640]{1,0:T(8,128)(2,1)S(1)} collective-permute-done((bf16[320,640]{1,0:T(8,128)(2,1)}, bf16[320,640]{1,0:T(8,128)(2,1)S(1)}, u32[]{:S(2)}, u32[]{:S(2)}) %collective-permute-start.42) | collective-permute-done | bytes 409632 | tf_op jit(solution)/shard_map/ppermute | solution.py:33
  (211 shorter events, 89.0 us)
Async XLA Ops:
  0.6 96.0 %collective-permute-start.3 = (bf16[640,5120]{1,0:T(8,128)(2,1)}, bf16[640,5120]{1,0:T(8,128)(2,1)}, u32[]{:S(2)}, u32[]{:S(2)}) collective-permute-start(bf16[640,5120]{1,0:T(8,128)(2,1)} %w_own_ref.1), channel_id=1, source_target_pairs={{0,2},{2,0},{4,6},{6,4},{8,10},{10,8},{12,14},{14,12},{1,3},{3,1},... | collective-permute-start | bytes 19660808 | tf_op jit(solution)/shard_map/ppermute | solution.py:29
  8.7 39.2 %all-to-all-start = ((bf16[8,272,640]{2,1,0:T(8,128)(2,1)}), bf16[8,272,640]{2,1,0:T(8,128)(2,1)S(1)}, u32[]{:S(2)}, u32[]{:S(2)}) async-start(bf16[8,272,640]{2,1,0:T(8,128)(2,1)} %pack.2), calls=%async_computation | async-start | bytes 5570560 | tf_op jit(solution)/shard_map/all_to_all | solution.py:152
  14.2 32.2 %collective-permute-start = (bf16[128,5120]{1,0:T(8,128)(2,1)}, bf16[128,5120]{1,0:T(8,128)(2,1)}, u32[]{:S(2)}, u32[]{:S(2)}) collective-permute-start(bf16[128,5120]{1,0:T(8,128)(2,1)} %bitcast.77), channel_id=1, source_target_pairs={{0,1},{1,0},{2,3},{3,2},{4,5},{5,4},{6,7},{7,6},{8,9},{9,8},{10,11... | collective-permute-start | bytes 3932168 | tf_op jit(solution)/shard_map/ppermute | solution.py:46
  52.0 44.6 %all-to-all-start.1 = ((bf16[8,256,640]{2,1,0:T(8,128)(2,1)}), bf16[8,256,640]{2,1,0:T(8,128)(2,1)S(1)}, u32[]{:S(2)}, u32[]{:S(2)}) async-start(bf16[8,256,640]{2,1,0:T(8,128)(2,1)} %pack.3), calls=%async_computation.1 | async-start | bytes 5242880 | tf_op jit(solution)/shard_map/all_to_all | solution.py:152
  65.4 31.2 %collective-permute-start.2 = (bf16[8,128,640]{2,1,0:T(8,128)(2,1)}, bf16[8,128,640]{2,1,0:T(8,128)(2,1)}, u32[]{:S(2)}, u32[]{:S(2)}) collective-permute-start(bf16[8,128,640]{2,1,0:T(8,128)(2,1)} %take_rows.2), channel_id=1, source_target_pairs={{0,1},{1,0},{2,3},{3,2},{4,5},{5,4},{6,7},{7,6},{8,9},{9,8},{10,11... | collective-permute-start | bytes 3932168 | tf_op jit(solution)/shard_map/ppermute | solution.py:46
  118.6 20.9 %collective-permute-start.5 = (bf16[4,640,256]{2,1,0:T(8,128)(2,1)}, bf16[4,640,256]{2,1,0:T(8,128)(2,1)S(1)}, u32[]{:S(2)}, u32[]{:S(2)}) collective-permute-start(bf16[4,640,256]{2,1,0:T(8,128)(2,1)} %get-tuple-element.69.refs_0_), channel_id=1, source_target_pairs={{0,16},{1,17},{2,19},{3,18},{4,20},{5,21},{6,23},{7,22},{8,24},{9,... | collective-permute-start | bytes 3932168 | tf_op jit(solution)/shard_map/ppermute | solution.py:42
  139.0 14.7 %collective-permute-start.8 = (bf16[64,5120]{1,0:T(8,128)(2,1)}, bf16[64,5120]{1,0:T(8,128)(2,1)S(1)}, u32[]{:S(2)}, u32[]{:S(2)}) collective-permute-start(bf16[64,5120]{1,0:T(8,128)(2,1)} %get-tuple-element.75), channel_id=1, source_target_pairs={{0,4},{2,14},{4,8},{6,2},{8,12},{10,6},{12,0},{14,10},{1,5},{3,15}... | collective-permute-start | bytes 1966088 | tf_op jit(solution)/shard_map/ppermute | solution.py:25
  139.5 37.1 %collective-permute-start.6 = (bf16[4,640,256]{2,1,0:T(8,128)(2,1)S(1)}, bf16[4,640,256]{2,1,0:T(8,128)(2,1)S(1)}, u32[]{:S(2)}, u32[]{:S(2)}) collective-permute-start(bf16[4,640,256]{2,1,0:T(8,128)(2,1)S(1)} %collective-permute-done.5.refs_1_.first_ref), channel_id=1, source_target_pairs={{0,16},{1,17},{2,19},{3,18},{4,20},{5,21},{6,23},{7,22},{8,24},{9,... | collective-permute-start | bytes 3932168 | tf_op jit(solution)/shard_map/ppermute | solution.py:42
  147.9 12.7 %collective-permute-start.12 = (bf16[64,5120]{1,0:T(8,128)(2,1)S(1)}, bf16[64,5120]{1,0:T(8,128)(2,1)S(1)}, u32[]{:S(2)}, u32[]{:S(2)}) collective-permute-start(bf16[64,5120]{1,0:T(8,128)(2,1)S(1)} %add_convert_fusion.1), channel_id=1, source_target_pairs={{0,4},{2,14},{4,8},{6,2},{8,12},{10,6},{12,0},{14,10},{1,5},{3,15}... | collective-permute-start | bytes 1966088 | tf_op jit(solution)/shard_map/ppermute | solution.py:25
  153.8 13.8 %collective-permute-start.9 = (bf16[64,5120]{1,0:T(8,128)(2,1)S(1)}, bf16[64,5120]{1,0:T(8,128)(2,1)S(1)}, u32[]{:S(2)}, u32[]{:S(2)}) collective-permute-start(bf16[64,5120]{1,0:T(8,128)(2,1)S(1)} %add_convert_fusion.3), channel_id=1, source_target_pairs={{0,4},{2,14},{4,8},{6,2},{8,12},{10,6},{12,0},{14,10},{1,5},{3,15}... | collective-permute-start | bytes 1966088 | tf_op jit(solution)/shard_map/ppermute | solution.py:25
  160.7 15.9 %collective-permute-start.13 = (bf16[64,5120]{1,0:T(8,128)(2,1)S(1)}, bf16[64,5120]{1,0:T(8,128)(2,1)S(1)}, u32[]{:S(2)}, u32[]{:S(2)}) collective-permute-start(bf16[64,5120]{1,0:T(8,128)(2,1)S(1)} %add_convert_fusion), channel_id=1, source_target_pairs={{0,4},{2,14},{4,8},{6,2},{8,12},{10,6},{12,0},{14,10},{1,5},{3,15}... | collective-permute-start | bytes 1966088 | tf_op jit(solution)/shard_map/ppermute | solution.py:25
  167.8 13.9 %collective-permute-start.10 = (bf16[64,5120]{1,0:T(8,128)(2,1)S(1)}, bf16[64,5120]{1,0:T(8,128)(2,1)S(1)}, u32[]{:S(2)}, u32[]{:S(2)}) collective-permute-start(bf16[64,5120]{1,0:T(8,128)(2,1)S(1)} %add_convert_fusion.2), channel_id=1, source_target_pairs={{0,4},{2,14},{4,8},{6,2},{8,12},{10,6},{12,0},{14,10},{1,5},{3,15}... | collective-permute-start | bytes 1966088 | tf_op jit(solution)/shard_map/ppermute | solution.py:25
  191.4 13.7 %collective-permute-start.14 = (bf16[128,1280]{1,0:T(8,128)(2,1)}, bf16[128,1280]{1,0:T(8,128)(2,1)S(1)}, u32[]{:S(2)}, u32[]{:S(2)}) collective-permute-start(bf16[128,1280]{1,0:T(8,128)(2,1)} %get-tuple-element.80), channel_id=1, source_target_pairs={{0,16},{1,17},{2,19},{3,18},{4,20},{5,21},{6,23},{7,22},{8,24},{9,... | collective-permute-start | bytes 983048 | tf_op jit(solution)/shard_map/ppermute | solution.py:42
  193.3 11.8 %collective-permute-start.15 = (bf16[128,1280]{1,0:T(8,128)(2,1)}, bf16[128,1280]{1,0:T(8,128)(2,1)S(1)}, u32[]{:S(2)}, u32[]{:S(2)}) collective-permute-start(bf16[128,1280]{1,0:T(8,128)(2,1)} %get-tuple-element.81), channel_id=1, source_target_pairs={{0,1},{1,0},{2,3},{3,2},{4,5},{5,4},{6,7},{7,6},{8,9},{9,8},{10,11... | collective-permute-start | bytes 983048 | tf_op jit(solution)/shard_map/ppermute | solution.py:42
  193.3 16.5 %collective-permute-start.16 = (bf16[128,1280]{1,0:T(8,128)(2,1)}, bf16[128,1280]{1,0:T(8,128)(2,1)S(1)}, u32[]{:S(2)}, u32[]{:S(2)}) collective-permute-start(bf16[128,1280]{1,0:T(8,128)(2,1)} %get-tuple-element.82), channel_id=1, source_target_pairs={{0,17},{1,16},{2,18},{3,19},{4,21},{5,20},{6,22},{7,23},{8,25},{9,... | collective-permute-start | bytes 983048 | tf_op jit(solution)/shard_map/ppermute | solution.py:42
  194.0 15.8 %collective-permute-start.17 = (bf16[128,1280]{1,0:T(8,128)(2,1)}, bf16[128,1280]{1,0:T(8,128)(2,1)S(1)}, u32[]{:S(2)}, u32[]{:S(2)}) collective-permute-start(bf16[128,1280]{1,0:T(8,128)(2,1)} %get-tuple-element.88.refs_4_), channel_id=1, source_target_pairs={{0,4},{2,14},{4,8},{6,2},{8,12},{10,6},{12,0},{14,10},{1,5},{3,15}... | collective-permute-start | bytes 983048 | tf_op jit(solution)/shard_map/ppermute | solution.py:25
  216.1 12.5 %collective-permute-start.29 = (bf16[192,1280]{1,0:T(8,128)(2,1)}, bf16[192,1280]{1,0:T(8,128)(2,1)S(1)}, u32[]{:S(2)}, u32[]{:S(2)}) collective-permute-start(bf16[192,1280]{1,0:T(8,128)(2,1)} %get-tuple-element.97.refs_12_), channel_id=1, source_target_pairs={{0,4},{2,14},{4,8},{6,2},{8,12},{10,6},{12,0},{14,10},{1,5},{3,15}... | collective-permute-start | bytes 1474568 | tf_op jit(solution)/shard_map/ppermute | solution.py:25
  218.0 14.4 %collective-permute-start.27 = (bf16[192,1280]{1,0:T(8,128)(2,1)}, bf16[192,1280]{1,0:T(8,128)(2,1)S(1)}, u32[]{:S(2)}, u32[]{:S(2)}) collective-permute-start(bf16[192,1280]{1,0:T(8,128)(2,1)} %get-tuple-element.97.refs_12_), channel_id=1, source_target_pairs={{0,2},{2,0},{4,6},{6,4},{8,10},{10,8},{12,14},{14,12},{1,3},{3,1},... | collective-permute-start | bytes 1474568 | tf_op jit(solution)/shard_map/ppermute | solution.py:29
  218.0 13.1 %collective-permute-start.30 = (bf16[192,1280]{1,0:T(8,128)(2,1)}, bf16[192,1280]{1,0:T(8,128)(2,1)S(1)}, u32[]{:S(2)}, u32[]{:S(2)}) collective-permute-start(bf16[192,1280]{1,0:T(8,128)(2,1)} %get-tuple-element.98.refs_13_), channel_id=1, source_target_pairs={{0,4},{2,14},{4,8},{6,2},{8,12},{10,6},{12,0},{14,10},{1,5},{3,15}... | collective-permute-start | bytes 1474568 | tf_op jit(solution)/shard_map/ppermute | solution.py:25
  220.6 11.7 %collective-permute-start.28 = (bf16[192,1280]{1,0:T(8,128)(2,1)}, bf16[192,1280]{1,0:T(8,128)(2,1)S(1)}, u32[]{:S(2)}, u32[]{:S(2)}) collective-permute-start(bf16[192,1280]{1,0:T(8,128)(2,1)} %get-tuple-element.98.refs_13_), channel_id=1, source_target_pairs={{0,2},{2,0},{4,6},{6,4},{8,10},{10,8},{12,14},{14,12},{1,3},{3,1},... | collective-permute-start | bytes 1474568 | tf_op jit(solution)/shard_map/ppermute | solution.py:29
  228.6 25.5 %collective-permute-start.20 = (bf16[4,640,256]{2,1,0:T(8,128)(2,1)S(1)}, bf16[4,640,256]{2,1,0:T(8,128)(2,1)S(1)}, u32[]{:S(2)}, u32[]{:S(2)}) collective-permute-start(bf16[4,640,256]{2,1,0:T(8,128)(2,1)S(1)} %collective-permute-done.6.refs_2_.second_ref), channel_id=1, source_target_pairs={{0,16},{1,17},{2,19},{3,18},{4,20},{5,21},{6,23},{7,22},{8,24},{9,... | collective-permute-start | bytes 3932168 | tf_op jit(solution)/shard_map/ppermute | solution.py:42
  232.4 12.9 %collective-permute-start.34 = (bf16[192,1280]{1,0:T(8,128)(2,1)S(1)}, bf16[192,1280]{1,0:T(8,128)(2,1)S(1)}, u32[]{:S(2)}, u32[]{:S(2)}) collective-permute-start(bf16[192,1280]{1,0:T(8,128)(2,1)S(1)} %collective-permute-done.30.refs_17_), channel_id=1, source_target_pairs={{0,4},{2,14},{4,8},{6,2},{8,12},{10,6},{12,0},{14,10},{1,5},{3,15}... | collective-permute-start | bytes 1474568 | tf_op jit(solution)/shard_map/ppermute | solution.py:25
  234.8 14.3 %collective-permute-start.31 = (bf16[192,1280]{1,0:T(8,128)(2,1)S(1)}, bf16[192,1280]{1,0:T(8,128)(2,1)S(1)}, u32[]{:S(2)}, u32[]{:S(2)}) collective-permute-start(bf16[192,1280]{1,0:T(8,128)(2,1)S(1)} %collective-permute-done.29.refs_16_), channel_id=1, source_target_pairs={{0,2},{2,0},{4,6},{6,4},{8,10},{10,8},{12,14},{14,12},{1,3},{3,1},... | collective-permute-start | bytes 1474568 | tf_op jit(solution)/shard_map/ppermute | solution.py:29
  249.3 18.3 %collective-permute-start.37 = (bf16[192,1280]{1,0:T(8,128)(2,1)S(1)}, bf16[192,1280]{1,0:T(8,128)(2,1)S(1)}, u32[]{:S(2)}, u32[]{:S(2)}) collective-permute-start(bf16[192,1280]{1,0:T(8,128)(2,1)S(1)} %collective-permute-done.33.refs_20_), channel_id=1, source_target_pairs={{0,4},{2,14},{4,8},{6,2},{8,12},{10,6},{12,0},{14,10},{1,5},{3,15}... | collective-permute-start | bytes 1474568 | tf_op jit(solution)/shard_map/ppermute | solution.py:25
  249.4 18.3 %collective-permute-start.38 = (bf16[192,1280]{1,0:T(8,128)(2,1)S(1)}, bf16[192,1280]{1,0:T(8,128)(2,1)S(1)}, u32[]{:S(2)}, u32[]{:S(2)}) collective-permute-start(bf16[192,1280]{1,0:T(8,128)(2,1)S(1)} %collective-permute-done.34.refs_21_), channel_id=1, source_target_pairs={{0,4},{2,14},{4,8},{6,2},{8,12},{10,6},{12,0},{14,10},{1,5},{3,15}... | collective-permute-start | bytes 1474568 | tf_op jit(solution)/shard_map/ppermute | solution.py:25
  250.7 19.6 %collective-permute-start.44 = (bf16[48,640]{1,0:T(8,128)(2,1)S(1)}, bf16[48,640]{1,0:T(8,128)(2,1)S(1)}, u32[]{:S(2)}, u32[]{:S(2)}) collective-permute-start(bf16[48,640]{1,0:T(8,128)(2,1)S(1)} %get-tuple-element.113), channel_id=1, source_target_pairs={{0,4},{2,6},{4,8},{6,10},{8,12},{10,14},{12,0},{14,2},{1,5},{3,7},... | collective-permute-start | bytes 184328 | tf_op jit(solution)/shard_map/ppermute | solution.py:21
  252.2 18.1 %collective-permute-start.45 = (bf16[48,640]{1,0:T(8,128)(2,1)S(1)}, bf16[48,640]{1,0:T(8,128)(2,1)S(1)}, u32[]{:S(2)}, u32[]{:S(2)}) collective-permute-start(bf16[48,640]{1,0:T(8,128)(2,1)S(1)} %get-tuple-element.115), channel_id=1, source_target_pairs={{0,8},{2,10},{4,12},{6,14},{8,0},{10,2},{12,4},{14,6},{1,9},{3,11}... | collective-permute-start | bytes 184328 | tf_op jit(solution)/shard_map/ppermute | solution.py:21
  254.0 16.2 %collective-permute-start.46 = (bf16[48,640]{1,0:T(8,128)(2,1)S(1)}, bf16[48,640]{1,0:T(8,128)(2,1)S(1)}, u32[]{:S(2)}, u32[]{:S(2)}) collective-permute-start(bf16[48,640]{1,0:T(8,128)(2,1)S(1)} %get-tuple-element.114), channel_id=1, source_target_pairs={{0,12},{2,14},{4,0},{6,2},{8,4},{10,6},{12,8},{14,10},{1,13},{3,15... | collective-permute-start | bytes 184328 | tf_op jit(solution)/shard_map/ppermute | solution.py:21
  271.3 17.8 %all-to-all-start.2 = ((bf16[8,40,896]{2,1,0:T(8,128)(2,1)}), bf16[8,40,896]{2,1,0:T(8,128)(2,1)S(1)}, u32[]{:S(2)}, u32[]{:S(2)}) async-start(bf16[8,40,896]{2,1,0:T(8,128)(2,1)} %fusion.6), calls=%async_computation.2 | async-start | bytes 1146880 | tf_op jit(solution)/shard_map/all_to_all | solution.py:690
  283.5 12.1 %collective-permute-start.41 = (bf16[320,640]{1,0:T(8,128)(2,1)}, bf16[320,640]{1,0:T(8,128)(2,1)S(1)}, u32[]{:S(2)}, u32[]{:S(2)}) collective-permute-start(bf16[320,640]{1,0:T(8,128)(2,1)} %get-tuple-element.103), channel_id=1, source_target_pairs={{0,64},{16,80},{32,96},{48,112},{64,0},{80,16},{96,32},{112,48},{1... | collective-permute-start | bytes 1228808 | tf_op jit(solution)/shard_map/ppermute | solution.py:33
  286.5 18.9 %collective-permute-start.42 = (bf16[320,640]{1,0:T(8,128)(2,1)}, bf16[320,640]{1,0:T(8,128)(2,1)S(1)}, u32[]{:S(2)}, u32[]{:S(2)}) collective-permute-start(bf16[320,640]{1,0:T(8,128)(2,1)} %get-tuple-element.104), channel_id=1, source_target_pairs={{0,32},{16,48},{32,64},{48,80},{64,96},{80,112},{96,0},{112,16},{1... | collective-permute-start | bytes 1228808 | tf_op jit(solution)/shard_map/ppermute | solution.py:33
  286.7 18.6 %collective-permute-start.43 = (bf16[320,640]{1,0:T(8,128)(2,1)}, bf16[320,640]{1,0:T(8,128)(2,1)S(1)}, u32[]{:S(2)}, u32[]{:S(2)}) collective-permute-start(bf16[320,640]{1,0:T(8,128)(2,1)} %get-tuple-element.105), channel_id=1, source_target_pairs={{0,96},{16,112},{32,0},{48,16},{64,32},{80,48},{96,64},{112,80},{1... | collective-permute-start | bytes 1228808 | tf_op jit(solution)/shard_map/ppermute | solution.py:33
  (57 other events, 572.9 us)
where the time goes:
time: 309 us; the launch traced here: 307 us
  waiting for transfers between devices  104 us (34%)
  starting transfers between devices  94.1 us (30%)
  Pallas kernels  83.4 us (27%)
  other arithmetic  14.6 us (5%)
  local copies, waits for them, and re-layouts  7.65 us (2%)
    ppermute x5, waiting for transfers between devices, pair_swap(): return lax.ppermute(value, 'pair', [(0, 1), (1, 0)])  59.2 us
    ppermute x15, starting transfers between devices, seq_ring(): lax.ppermute(value, 'seq', [(i, (i // 2 + side(i % 2)) % 4 * 2 + i % 2) f...  27.2 us
    ppermute x15, waiting for transfers between devices, seq_ring(): lax.ppermute(value, 'seq', [(i, (i // 2 + side(i % 2)) % 4 * 2 + i % 2) f...  22.5 us
    ppermute x15, starting transfers between devices, core_swap(): return lax.ppermute(value, 'seq', [(i, i ^ 1) for i in range(8)])  20.9 us
    pallas_call x1, Pallas kernels, attend(): pl.pallas_call(attend_kernel, grid_spec=pltpu.PrefetchScalarGridSpec(num_...  18.3 us
    ppermute x3, waiting for transfers between devices, y_shift(): lax.ppermute(value, 'dp', [(i, (i // 2 + apart) % 4 * 2 + i % 2) for i in...  14.8 us
    ppermute x6, starting transfers between devices, x_shift(): lax.ppermute(value, ('dp', 'seq', 'pair'), [(i, target(i)) for i in range...  12.3 us
    pallas_call x1, Pallas kernels, project(): pl.pallas_call(project_kernel, grid=(width // tile,), in_specs=[left, lef...  11.8 us
  transfers between devices with their start and end apart: 50, of which 17 were waited for; matrix products, arithmetic and copies ran while one was open for 6% of the time, Pallas kernels for 18%

commit v1 on v0

--- a/solution.py
+++ b/solution.py
@@ -152,23 +152,28 @@
     return lax.all_to_all(packed, "seq", 0, 0, tiled=True)
 
 
-def rows_kernel(in_ref, out_ref):
-    out_ref[...] = in_ref[...]
-
-
-def take_rows(pieces, start, rows):
+def rows_kernel(*refs):
+    half = len(refs) // 2
+    for source, out in zip(refs[:half], refs[half:]):
+        out[...] = source[...]
+
+
+def take_rows(pieces, *spans):
     blocks, _, cols = pieces.shape
     half = blocks // 2
     return pl.pallas_call(
         rows_kernel,
         grid=(2,),
-        in_specs=[pl.BlockSpec((half, rows, cols), lambda i: (i, start // rows, 0))],
-        out_specs=pl.BlockSpec((half, rows, cols), lambda i: (i, 0, 0)),
-        out_shape=jax.ShapeDtypeStruct((blocks, rows, cols), pieces.dtype),
-        compiler_params=pltpu.CompilerParams(vmem_limit_bytes=VMEM_LIMIT),
+        in_specs=[
+            pl.BlockSpec((half, rows, cols), functools.partial(lambda at, i: (i, at, 0), start // rows))
+            for start, rows in spans
+        ],
+        out_specs=[pl.BlockSpec((half, rows, cols), lambda i: (i, 0, 0)) for _, rows in spans],
+        out_shape=[jax.ShapeDtypeStruct((blocks, rows, cols), pieces.dtype) for _, rows in spans],
+        compiler_params=pltpu.CompilerParams(vmem_limit_bytes=16 * 1024 * 1024),
         cost_estimate=FREE,
         name="take_rows",
-    )(pieces)
+    )(*[pieces for _ in spans])
 
 
 def attend_kernel(
@@ -267,7 +272,7 @@
             jax.ShapeDtypeStruct((chips, block, width), jnp.bfloat16),
             jax.ShapeDtypeStruct((chips, width, 2 * block), jnp.bfloat16),
         ],
-        compiler_params=pltpu.CompilerParams(vmem_limit_bytes=VMEM_LIMIT),
+        compiler_params=pltpu.CompilerParams(vmem_limit_bytes=24 * 1024 * 1024),
         cost_estimate=FREE,
         name="attend",
     )(low, high, turn, query_seg, key_seg, value_other, first, second)
@@ -330,7 +335,7 @@
     return pl.pallas_call(
         join_kernel,
         out_shape=[out, out],
-        compiler_params=pltpu.CompilerParams(vmem_limit_bytes=VMEM_LIMIT),
+        compiler_params=pltpu.CompilerParams(vmem_limit_bytes=16 * 1024 * 1024),
         cost_estimate=FREE,
         name="join",
     )(*pieces)
@@ -427,7 +432,7 @@
             ],
         ),
         out_shape=[jax.ShapeDtypeStruct(out, jnp.bfloat16) for out in outs],
-        compiler_params=pltpu.CompilerParams(vmem_limit_bytes=VMEM_LIMIT),
+        compiler_params=pltpu.CompilerParams(vmem_limit_bytes=40 * 1024 * 1024),
         cost_estimate=FREE,
         name="student",
     )(chip_x, *arrays)
@@ -481,7 +486,7 @@
             ],
         ),
         out_shape=[jax.ShapeDtypeStruct(out, jnp.bfloat16) for _ in range(2)],
-        compiler_params=pltpu.CompilerParams(vmem_limit_bytes=VMEM_LIMIT),
+        compiler_params=pltpu.CompilerParams(vmem_limit_bytes=24 * 1024 * 1024),
         cost_estimate=FREE,
         name="local_sums",
     )(place, *arrays)
@@ -617,9 +622,8 @@
     key_crossed, weights_crossed = pair_swap(student_key[0]), core_swap(out_proj)
     first = exchange([student_value[0], student_query[0]], columns)
     first, key_crossed = lax.optimization_barrier((first, key_crossed))
-    table = take_rows(first, 2 * stud_rows, columns.shape[0])
-    table_other = pair_swap(table)
-    value_own, table_other = lax.optimization_barrier((take_rows(first, 0, stud_rows), table_other))
+    value_own, table = take_rows(first, (0, stud_rows), (2 * stud_rows, columns.shape[0]))
+    value_own, table_other = lax.optimization_barrier((value_own, pair_swap(table)))
     value_other = pair_swap(value_own)
     second = exchange([student_key[0], key_crossed])
     lower, upper = jnp.where(pair_pos == 0, table, table_other), jnp.where(pair_pos == 0, table_other, table)

time: 309 us -> 299 us (0.968)
  Pallas kernels: 83.4 us -> 69 us
  starting transfers between devices: 94.1 us -> 101 us
  other arithmetic: 14.6 us -> 9.43 us
  waiting for transfers between devices: 104 us -> 108 us
    ppermute x15, starting transfers between devices: 27.2 us -> 32 us  [seq_ring(): lax.ppermute(value, 'seq', [(i, (i // 2 + side(i % 2)) % 4 * 2 + i % 2) f...]
    pallas_call x1, Pallas kernels: 8.9 us -> 4.88 us  [student(): pl.pallas_call(student_kernel, grid_spec=pltpu.PrefetchScalarGridSpec(num...]
  transfers between devices with their start and end apart: 50 -> 50, of which waited for: 17 -> 18; matrix products, arithmetic and copies ran while one was open for 6% -> 4% of each run, Pallas kernels for 18% -> 16%
where the time goes in v1:
time: 299 us; the launch traced here: 298 us
  waiting for transfers between devices  108 us (36%)
  starting transfers between devices  101 us (34%)
  Pallas kernels  69 us (23%)
  other arithmetic  9.43 us (3%)
  local copies, waits for them, and re-layouts  7.1 us (2%)
    ppermute x5, waiting for transfers between devices, pair_swap(): return lax.ppermute(value, 'pair', [(0, 1), (1, 0)])  57.5 us
    ppermute x15, starting transfers between devices, seq_ring(): lax.ppermute(value, 'seq', [(i, (i // 2 + side(i % 2)) % 4 * 2 + i % 2) f...  32 us
    ppermute x15, waiting for transfers between devices, seq_ring(): lax.ppermute(value, 'seq', [(i, (i // 2 + side(i % 2)) % 4 * 2 + i % 2) f...  25.4 us
    ppermute x15, starting transfers between devices, core_swap(): return lax.ppermute(value, 'seq', [(i, i ^ 1) for i in range(8)])  21.2 us
    pallas_call x1, Pallas kernels, attend(): pl.pallas_call(attend_kernel, grid_spec=pltpu.PrefetchScalarGridSpec(num_...  16.8 us
    ppermute x3, waiting for transfers between devices, y_shift(): lax.ppermute(value, 'dp', [(i, (i // 2 + apart) % 4 * 2 + i % 2) for i in...  14.8 us
    ppermute x6, starting transfers between devices, x_shift(): lax.ppermute(value, ('dp', 'seq', 'pair'), [(i, target(i)) for i in range...  11.8 us
    pallas_call x1, Pallas kernels, project(): pl.pallas_call(project_kernel, grid=(width // tile,), in_specs=[left, lef...  11.8 us
  transfers between devices with their start and end apart: 50, of which 18 were waited for; matrix products, arithmetic and copies ran while one was open for 4% of the time, Pallas kernels for 16%

profile of v1, /device:TPU:1, one launch (start us, length us, event | category | flops | bytes accessed | tf_op | source)
XLA Modules:
  0.0 298.3 jit_solution(17297397495082684463)
XLA Ops:
  5.5 3.2 %pack.2 = bf16[8,272,640]{2,1,0:T(8,128)(2,1)} custom-call(bf16[128,5120]{1,0:T(8,128)(2,1)} %bitcast.74, bf16[128,5120]{1,0:T(8,128)(2,1)} %bitcast.75, bf16[128,5120]{1,0:T(8,128)(2,1)} %bitcast.76, bf16[128,5120]{1,0:T(8,128)(2,1)} %bitcast.77, bf16[128,5120]{1,0:T(8,128)(2,1)} %bitcast.78, bf16[128,5120]{1,0:T(8,128)(2,1)} %bitcast.79, ...), custom_call_target="tpu_custom_call" | custom-call | tf_op jit(solution)/shard_map/pack/pallas_call | solution.py:137
  8.7 5.5 %all-to-all-start = ((bf16[8,272,640]{2,1,0:T(8,128)(2,1)}), bf16[8,272,640]{2,1,0:T(8,128)(2,1)S(1)}, u32[]{:S(2)}, u32[]{:S(2)}) async-start(bf16[8,272,640]{2,1,0:T(8,128)(2,1)} %pack.2), calls=%async_computation | async-start | bytes 5570560 | tf_op jit(solution)/shard_map/all_to_all | solution.py:152
  16.9 29.5 %collective-permute-done.refs_4_.refs_5_.refs_6_.refs_7_ = bf16[128,5120]{1,0:T(8,128)(2,1)} collective-permute-done((bf16[128,5120]{1,0:T(8,128)(2,1)}, bf16[128,5120]{1,0:T(8,128)(2,1)}, u32[]{:S(2)}, u32[]{:S(2)}) %collective-permute-start) | collective-permute-done | bytes 1310752 | tf_op jit(solution)/shard_map/ppermute | solution.py:46
  47.9 3.1 %pack.3 = bf16[8,256,640]{2,1,0:T(8,128)(2,1)} custom-call(bf16[128,5120]{1,0:T(8,128)(2,1)} %bitcast.83, bf16[128,5120]{1,0:T(8,128)(2,1)} %bitcast.84, bf16[128,5120]{1,0:T(8,128)(2,1)} %bitcast.85, bf16[128,5120]{1,0:T(8,128)(2,1)} %bitcast.86, bf16[128,5120]{1,0:T(8,128)(2,1)} %collective-permute-done.refs_4_.refs_5_.refs_6_.refs_7_, ...), custom_call_target="tpu_custom_call" | custom-call | tf_op jit(solution)/shard_map/pack/pallas_call | solution.py:137
  51.0 5.3 %all-to-all-start.1 = ((bf16[8,256,640]{2,1,0:T(8,128)(2,1)}), bf16[8,256,640]{2,1,0:T(8,128)(2,1)}, u32[]{:S(2)}, u32[]{:S(2)}) async-start(bf16[8,256,640]{2,1,0:T(8,128)(2,1)} %pack.3), calls=%async_computation.1 | async-start | bytes 5242880 | tf_op jit(solution)/shard_map/all_to_all | solution.py:152
  60.4 4.5 %collective-permute-done.1 = bf16[8,16,640]{2,1,0:T(8,128)(2,1)S(1)} collective-permute-done((bf16[8,16,640]{2,1,0:T(8,128)(2,1)S(1)}, bf16[8,16,640]{2,1,0:T(8,128)(2,1)S(1)}, u32[]{:S(2)}, u32[]{:S(2)}) %collective-permute-start.1) | collective-permute-done | bytes 163872 | tf_op jit(solution)/shard_map/ppermute | solution.py:46
  70.2 6.9 %teacher.1 = f32[256,64]{1,0:T(8,128)} custom-call(bf16[256,5120]{1,0:T(8,128)(2,1)} %bitcast.87, bf16[256,16]{1,0:T(8,128)(2,1)} %fusion.10.hot_ref, bf16[16,16,640]{2,1,0:T(8,128)(2,1)} %bitcast.69, bf16[64,5120]{1,0:T(8,128)(2,1)} %bitcast.88), custom_call_target="tpu_custom_call" | custom-call | tf_op jit(solution)/shard_map/teacher/pallas_call | solution.py:104
  78.0 18.2 %collective-permute-done.2.value_ref = bf16[8,128,640]{2,1,0:T(8,128)(2,1)} collective-permute-done((bf16[8,128,640]{2,1,0:T(8,128)(2,1)}, bf16[8,128,640]{2,1,0:T(8,128)(2,1)}, u32[]{:S(2)}, u32[]{:S(2)}) %collective-permute-start.2) | collective-permute-done | bytes 1310752 | tf_op jit(solution)/shard_map/ppermute | solution.py:46
  96.4 16.8 %attend.1 = (bf16[4,128,640]{2,1,0:T(8,128)(2,1)S(1)}, bf16[4,128,640]{2,1,0:T(8,128)(2,1)S(1)}, bf16[4,640,256]{2,1,0:T(8,128)(2,1)}) custom-call(s32[8]{0:T(128)S(1)} %get-tuple-element.63.low_ref, s32[8]{0:T(128)S(1)} %get-tuple-element.64.high_ref, s32[8]{0:T(128)S(1)} %fusion.35.turn_ref, s32[8,128,1]{2,1,0:T(8,128)S(1)} %copy.28.qseg_ref, ...), custom_call_target="tpu_custom_call" | custom-call | tf_op jit(solution)/shard_map/attend/pallas_call | solution.py:252
  115.8 5.1 %collective-permute-start.5 = (bf16[4,640,256]{2,1,0:T(8,128)(2,1)}, bf16[4,640,256]{2,1,0:T(8,128)(2,1)S(1)}, u32[]{:S(2)}, u32[]{:S(2)}) collective-permute-start(bf16[4,640,256]{2,1,0:T(8,128)(2,1)} %get-tuple-element.73.refs_0_), channel_id=1, source_target_pairs={{0,16},{1,17},{2,19},{3,18},{4,20},{5,21},{6,23},{7,22},{8,24},{9,... | collective-permute-start | bytes 3932168 | tf_op jit(solution)/shard_map/ppermute | solution.py:42
  121.7 11.8 %project.1 = (bf16[128,5120]{1,0:T(8,128)(2,1)}, bf16[64,5120]{1,0:T(8,128)(2,1)}, bf16[64,5120]{1,0:T(8,128)(2,1)}, bf16[64,5120]{1,0:T(8,128)(2,1)}, bf16[64,5...) custom-call(bf16[4,128,640]{2,1,0:T(8,128)(2,1)} %copy-done.6, ...), custom_call_target="tpu_custom_call" | custom-call | tf_op jit(solution)/shard_map/project/pallas_call | solution.py:312
  138.8 5.1 %collective-permute-done.11 = bf16[64,5120]{1,0:T(8,128)(2,1)} collective-permute-done((bf16[64,5120]{1,0:T(8,128)(2,1)}, bf16[64,5120]{1,0:T(8,128)(2,1)}, u32[]{:S(2)}, u32[]{:S(2)}) %collective-permute-start.11) | collective-permute-done | bytes 655392 | tf_op jit(solution)/shard_map/ppermute | solution.py:25
  145.3 3.4 %collective-permute-start.12 = (bf16[64,5120]{1,0:T(8,128)(2,1)S(1)}, bf16[64,5120]{1,0:T(8,128)(2,1)S(1)}, u32[]{:S(2)}, u32[]{:S(2)}) collective-permute-start(bf16[64,5120]{1,0:T(8,128)(2,1)S(1)} %add_convert_fusion.1), channel_id=1, source_target_pairs={{0,4},{2,14},{4,8},{6,2},{8,12},{10,6},{12,0},{14,10},{1,5},{3,15}... | collective-permute-start | bytes 1966088 | tf_op jit(solution)/shard_map/ppermute | solution.py:25
  151.0 3.4 %collective-permute-start.9 = (bf16[64,5120]{1,0:T(8,128)(2,1)S(1)}, bf16[64,5120]{1,0:T(8,128)(2,1)S(1)}, u32[]{:S(2)}, u32[]{:S(2)}) collective-permute-start(bf16[64,5120]{1,0:T(8,128)(2,1)S(1)} %add_convert_fusion.3), channel_id=1, source_target_pairs={{0,4},{2,14},{4,8},{6,2},{8,12},{10,6},{12,0},{14,10},{1,5},{3,15}... | collective-permute-start | bytes 1966088 | tf_op jit(solution)/shard_map/ppermute | solution.py:25
  154.4 3.4 %collective-permute-done.12 = bf16[64,5120]{1,0:T(8,128)(2,1)S(1)} collective-permute-done((bf16[64,5120]{1,0:T(8,128)(2,1)S(1)}, bf16[64,5120]{1,0:T(8,128)(2,1)S(1)}, u32[]{:S(2)}, u32[]{:S(2)}) %collective-permute-start.12) | collective-permute-done | bytes 655392 | tf_op jit(solution)/shard_map/ppermute | solution.py:25
  158.0 3.2 %collective-permute-start.13 = (bf16[64,5120]{1,0:T(8,128)(2,1)S(1)}, bf16[64,5120]{1,0:T(8,128)(2,1)S(1)}, u32[]{:S(2)}, u32[]{:S(2)}) collective-permute-start(bf16[64,5120]{1,0:T(8,128)(2,1)S(1)} %add_convert_fusion), channel_id=1, source_target_pairs={{0,4},{2,14},{4,8},{6,2},{8,12},{10,6},{12,0},{14,10},{1,5},{3,15}... | collective-permute-start | bytes 1966088 | tf_op jit(solution)/shard_map/ppermute | solution.py:25
  161.2 3.6 %collective-permute-done.9 = bf16[64,5120]{1,0:T(8,128)(2,1)S(1)} collective-permute-done((bf16[64,5120]{1,0:T(8,128)(2,1)S(1)}, bf16[64,5120]{1,0:T(8,128)(2,1)S(1)}, u32[]{:S(2)}, u32[]{:S(2)}) %collective-permute-start.9) | collective-permute-done | bytes 655392 | tf_op jit(solution)/shard_map/ppermute | solution.py:25
  165.0 3.2 %collective-permute-start.10 = (bf16[64,5120]{1,0:T(8,128)(2,1)S(1)}, bf16[64,5120]{1,0:T(8,128)(2,1)S(1)}, u32[]{:S(2)}, u32[]{:S(2)}) collective-permute-start(bf16[64,5120]{1,0:T(8,128)(2,1)S(1)} %add_convert_fusion.2), channel_id=1, source_target_pairs={{0,4},{2,14},{4,8},{6,2},{8,12},{10,6},{12,0},{14,10},{1,5},{3,15}... | collective-permute-start | bytes 1966088 | tf_op jit(solution)/shard_map/ppermute | solution.py:25
  172.9 6.0 %collective-permute-done.10.la_ref = bf16[64,5120]{1,0:T(8,128)(2,1)S(1)} collective-permute-done((bf16[64,5120]{1,0:T(8,128)(2,1)S(1)}, bf16[64,5120]{1,0:T(8,128)(2,1)S(1)}, u32[]{:S(2)}, u32[]{:S(2)}) %collective-permute-start.10) | collective-permute-done | bytes 655392 | tf_op jit(solution)/shard_map/ppermute | solution.py:25
  178.9 4.9 %student.1 = (bf16[128,1280]{1,0:T(8,128)(2,1)S(1)}, bf16[128,1280]{1,0:T(8,128)(2,1)S(1)}, bf16[128,1280]{1,0:T(8,128)(2,1)S(1)}, bf16[128,1280]{1,0:T(8,128)(2...) custom-call(s32[2]{0:T(128)S(1)} %pad_add_fusion.1.x_ref, ...), custom_call_target="tpu_custom_call" | custom-call | tf_op jit(solution)/shard_map/student/pallas_call | solution.py:417
  186.7 3.1 %collective-permute-start.17 = (bf16[128,1280]{1,0:T(8,128)(2,1)S(1)}, bf16[128,1280]{1,0:T(8,128)(2,1)S(1)}, u32[]{:S(2)}, u32[]{:S(2)}) collective-permute-start(bf16[128,1280]{1,0:T(8,128)(2,1)S(1)} %get-tuple-element.92.refs_4_), channel_id=1, source_target_pairs={{0,4},{2,14},{4,8},{6,2},{8,12},{10,6},{12,0},{14,10},{1,5},{3,15}... | collective-permute-start | bytes 983048 | tf_op jit(solution)/shard_map/ppermute | solution.py:25
  192.6 4.2 %collective-permute-done.14.refs_0_ = bf16[128,1280]{1,0:T(8,128)(2,1)S(1)} collective-permute-done((bf16[128,1280]{1,0:T(8,128)(2,1)S(1)}, bf16[128,1280]{1,0:T(8,128)(2,1)S(1)}, u32[]{:S(2)}, u32[]{:S(2)}) %collective-permute-start.14) | collective-permute-done | bytes 327712 | tf_op jit(solution)/shard_map/ppermute | solution.py:42
  196.8 5.0 %collective-permute-done.16.refs_2_ = bf16[128,1280]{1,0:T(8,128)(2,1)S(1)} collective-permute-done((bf16[128,1280]{1,0:T(8,128)(2,1)S(1)}, bf16[128,1280]{1,0:T(8,128)(2,1)S(1)}, u32[]{:S(2)}, u32[]{:S(2)}) %collective-permute-start.16) | collective-permute-done | bytes 327712 | tf_op jit(solution)/shard_map/ppermute | solution.py:42
  214.0 3.1 %collective-permute-done.19 = bf16[4,48,640]{2,1,0:T(8,128)(2,1)S(1)} collective-permute-done((bf16[4,48,640]{2,1,0:T(8,128)(2,1)S(1)}, bf16[4,48,640]{2,1,0:T(8,128)(2,1)S(1)}, u32[]{:S(2)}, u32[]{:S(2)}) %collective-permute-start.19) | collective-permute-done | bytes 245792 | tf_op jit(solution)/shard_map/ppermute | solution.py:46
  217.2 4.2 %collective-permute-start.25 = (bf16[128,1280]{1,0:T(8,128)(2,1)S(1)}, bf16[128,1280]{1,0:T(8,128)(2,1)S(1)}, u32[]{:S(2)}, u32[]{:S(2)}) collective-permute-start(bf16[128,1280]{1,0:T(8,128)(2,1)S(1)} %collective-permute-done.23.refs_8_), channel_id=1, source_target_pairs={{0,4},{2,14},{4,8},{6,2},{8,12},{10,6},{12,0},{14,10},{1,5},{3,15}... | collective-permute-start | bytes 983048 | tf_op jit(solution)/shard_map/ppermute | solution.py:25
  231.0 3.3 %collective-permute-start.26 = (bf16[128,1280]{1,0:T(8,128)(2,1)S(1)}, bf16[128,1280]{1,0:T(8,128)(2,1)S(1)}, u32[]{:S(2)}, u32[]{:S(2)}) collective-permute-start(bf16[128,1280]{1,0:T(8,128)(2,1)S(1)} %collective-permute-done.25.refs_10_), channel_id=1, source_target_pairs={{0,2},{2,0},{4,6},{6,4},{8,10},{10,8},{12,14},{14,12},{1,3},{3,1},... | collective-permute-start | bytes 983048 | tf_op jit(solution)/shard_map/ppermute | solution.py:29
  236.3 3.3 %collective-permute-start.35 = (bf16[192,1280]{1,0:T(8,128)(2,1)S(1)}, bf16[192,1280]{1,0:T(8,128)(2,1)S(1)}, u32[]{:S(2)}, u32[]{:S(2)}) collective-permute-start(bf16[192,1280]{1,0:T(8,128)(2,1)S(1)} %collective-permute-done.33.refs_20_), channel_id=1, source_target_pairs={{0,2},{2,0},{4,6},{6,4},{8,10},{10,8},{12,14},{14,12},{1,3},{3,1},... | collective-permute-start | bytes 1474568 | tf_op jit(solution)/shard_map/ppermute | solution.py:29
  247.0 11.4 %early_product.1.early_ref = f32[640,1280]{1,0:T(8,128)} custom-call(bf16[4,640,256]{2,1,0:T(8,128)(2,1)} %get-tuple-element.73.refs_0_, bf16[4,640,256]{2,1,0:T(8,128)(2,1)} %copy-done.10, bf16[4,640,256]{2,1,0:T(8,128)(2,1)} %copy-done.11, bf16[4,640,256]{2,1,0:T(8,128)(2,1)} %copy-done.12, bf16[128,1280]{1,0:T(8,128)(2,1)} %copy-done.9, ...), custom_call_target="tpu_custom_call" | custom-call | tf_op jit(solution)/shard_map/early_product/pallas_call | solution.py:519
  262.2 4.2 %all-to-all-start.2 = ((bf16[8,40,896]{2,1,0:T(8,128)(2,1)}), bf16[8,40,896]{2,1,0:T(8,128)(2,1)S(1)}, u32[]{:S(2)}, u32[]{:S(2)}) async-start(bf16[8,40,896]{2,1,0:T(8,128)(2,1)} %fusion.6), calls=%async_computation.2 | async-start | bytes 1146880 | tf_op jit(solution)/shard_map/all_to_all | solution.py:694
  267.3 7.0 %late_product.1 = (bf16[320,640]{1,0:T(8,128)(2,1)}, bf16[320,640]{1,0:T(8,128)(2,1)}, bf16[320,640]{1,0:T(8,128)(2,1)}, bf16[320,640]{1,0:T(8,128)(2,1)}) custom-call(s32[1]{0:T(128)} %bitcast.y_ref, bf16[4,640,256]{2,1,0:T(8,128)(2,1)} %copy-done.10, bf16[4,640,256]{2,1,0:T(8,128)(2,1)} %copy-done.11, bf16[4,640,256]{2,1,0:T(8,128)(2,1)} %copy-done.12, ...), custom_call_target="tpu_custom_call" | custom-call | tf_op jit(solution)/shard_map/late_product/pallas_call | solution.py:552
  281.4 5.0 %collective-permute-done.41 = bf16[320,640]{1,0:T(8,128)(2,1)S(1)} collective-permute-done((bf16[320,640]{1,0:T(8,128)(2,1)}, bf16[320,640]{1,0:T(8,128)(2,1)S(1)}, u32[]{:S(2)}, u32[]{:S(2)}) %collective-permute-start.41) | collective-permute-done | bytes 409632 | tf_op jit(solution)/shard_map/ppermute | solution.py:33
  286.4 9.8 %collective-permute-done.42 = bf16[320,640]{1,0:T(8,128)(2,1)S(1)} collective-permute-done((bf16[320,640]{1,0:T(8,128)(2,1)}, bf16[320,640]{1,0:T(8,128)(2,1)S(1)}, u32[]{:S(2)}, u32[]{:S(2)}) %collective-permute-start.42) | collective-permute-done | bytes 409632 | tf_op jit(solution)/shard_map/ppermute | solution.py:33
  (210 shorter events, 87.6 us)
Async XLA Ops:
  0.6 95.5 %collective-permute-start.3 = (bf16[640,5120]{1,0:T(8,128)(2,1)}, bf16[640,5120]{1,0:T(8,128)(2,1)}, u32[]{:S(2)}, u32[]{:S(2)}) collective-permute-start(bf16[640,5120]{1,0:T(8,128)(2,1)} %w_own_ref.1), channel_id=1, source_target_pairs={{0,2},{2,0},{4,6},{6,4},{8,10},{10,8},{12,14},{14,12},{1,3},{3,1},... | collective-permute-start | bytes 19660808 | tf_op jit(solution)/shard_map/ppermute | solution.py:29
  8.7 39.2 %all-to-all-start = ((bf16[8,272,640]{2,1,0:T(8,128)(2,1)}), bf16[8,272,640]{2,1,0:T(8,128)(2,1)S(1)}, u32[]{:S(2)}, u32[]{:S(2)}) async-start(bf16[8,272,640]{2,1,0:T(8,128)(2,1)} %pack.2), calls=%async_computation | async-start | bytes 5570560 | tf_op jit(solution)/shard_map/all_to_all | solution.py:152
  14.2 32.2 %collective-permute-start = (bf16[128,5120]{1,0:T(8,128)(2,1)}, bf16[128,5120]{1,0:T(8,128)(2,1)}, u32[]{:S(2)}, u32[]{:S(2)}) collective-permute-start(bf16[128,5120]{1,0:T(8,128)(2,1)} %bitcast.82), channel_id=1, source_target_pairs={{0,1},{1,0},{2,3},{3,2},{4,5},{5,4},{6,7},{7,6},{8,9},{9,8},{10,11... | collective-permute-start | bytes 3932168 | tf_op jit(solution)/shard_map/ppermute | solution.py:46
  51.0 45.2 %all-to-all-start.1 = ((bf16[8,256,640]{2,1,0:T(8,128)(2,1)}), bf16[8,256,640]{2,1,0:T(8,128)(2,1)}, u32[]{:S(2)}, u32[]{:S(2)}) async-start(bf16[8,256,640]{2,1,0:T(8,128)(2,1)} %pack.3), calls=%async_computation.1 | async-start | bytes 5242880 | tf_op jit(solution)/shard_map/all_to_all | solution.py:152
  64.9 31.3 %collective-permute-start.2 = (bf16[8,128,640]{2,1,0:T(8,128)(2,1)}, bf16[8,128,640]{2,1,0:T(8,128)(2,1)}, u32[]{:S(2)}, u32[]{:S(2)}) collective-permute-start(bf16[8,128,640]{2,1,0:T(8,128)(2,1)} %get-tuple-element.60), channel_id=1, source_target_pairs={{0,1},{1,0},{2,3},{3,2},{4,5},{5,4},{6,7},{7,6},{8,9},{9,8},{10,11... | collective-permute-start | bytes 3932168 | tf_op jit(solution)/shard_map/ppermute | solution.py:46
  115.8 20.9 %collective-permute-start.5 = (bf16[4,640,256]{2,1,0:T(8,128)(2,1)}, bf16[4,640,256]{2,1,0:T(8,128)(2,1)S(1)}, u32[]{:S(2)}, u32[]{:S(2)}) collective-permute-start(bf16[4,640,256]{2,1,0:T(8,128)(2,1)} %get-tuple-element.73.refs_0_), channel_id=1, source_target_pairs={{0,16},{1,17},{2,19},{3,18},{4,20},{5,21},{6,23},{7,22},{8,24},{9,... | collective-permute-start | bytes 3932168 | tf_op jit(solution)/shard_map/ppermute | solution.py:42
  136.2 14.7 %collective-permute-start.8 = (bf16[64,5120]{1,0:T(8,128)(2,1)}, bf16[64,5120]{1,0:T(8,128)(2,1)S(1)}, u32[]{:S(2)}, u32[]{:S(2)}) collective-permute-start(bf16[64,5120]{1,0:T(8,128)(2,1)} %get-tuple-element.79), channel_id=1, source_target_pairs={{0,4},{2,14},{4,8},{6,2},{8,12},{10,6},{12,0},{14,10},{1,5},{3,15}... | collective-permute-start | bytes 1966088 | tf_op jit(solution)/shard_map/ppermute | solution.py:25
  136.6 36.2 %collective-permute-start.6 = (bf16[4,640,256]{2,1,0:T(8,128)(2,1)S(1)}, bf16[4,640,256]{2,1,0:T(8,128)(2,1)S(1)}, u32[]{:S(2)}, u32[]{:S(2)}) collective-permute-start(bf16[4,640,256]{2,1,0:T(8,128)(2,1)S(1)} %collective-permute-done.5.refs_1_.first_ref), channel_id=1, source_target_pairs={{0,16},{1,17},{2,19},{3,18},{4,20},{5,21},{6,23},{7,22},{8,24},{9,... | collective-permute-start | bytes 3932168 | tf_op jit(solution)/shard_map/ppermute | solution.py:42
  145.3 12.5 %collective-permute-start.12 = (bf16[64,5120]{1,0:T(8,128)(2,1)S(1)}, bf16[64,5120]{1,0:T(8,128)(2,1)S(1)}, u32[]{:S(2)}, u32[]{:S(2)}) collective-permute-start(bf16[64,5120]{1,0:T(8,128)(2,1)S(1)} %add_convert_fusion.1), channel_id=1, source_target_pairs={{0,4},{2,14},{4,8},{6,2},{8,12},{10,6},{12,0},{14,10},{1,5},{3,15}... | collective-permute-start | bytes 1966088 | tf_op jit(solution)/shard_map/ppermute | solution.py:25
  151.0 13.8 %collective-permute-start.9 = (bf16[64,5120]{1,0:T(8,128)(2,1)S(1)}, bf16[64,5120]{1,0:T(8,128)(2,1)S(1)}, u32[]{:S(2)}, u32[]{:S(2)}) collective-permute-start(bf16[64,5120]{1,0:T(8,128)(2,1)S(1)} %add_convert_fusion.3), channel_id=1, source_target_pairs={{0,4},{2,14},{4,8},{6,2},{8,12},{10,6},{12,0},{14,10},{1,5},{3,15}... | collective-permute-start | bytes 1966088 | tf_op jit(solution)/shard_map/ppermute | solution.py:25
  158.0 14.9 %collective-permute-start.13 = (bf16[64,5120]{1,0:T(8,128)(2,1)S(1)}, bf16[64,5120]{1,0:T(8,128)(2,1)S(1)}, u32[]{:S(2)}, u32[]{:S(2)}) collective-permute-start(bf16[64,5120]{1,0:T(8,128)(2,1)S(1)} %add_convert_fusion), channel_id=1, source_target_pairs={{0,4},{2,14},{4,8},{6,2},{8,12},{10,6},{12,0},{14,10},{1,5},{3,15}... | collective-permute-start | bytes 1966088 | tf_op jit(solution)/shard_map/ppermute | solution.py:25
  165.0 13.9 %collective-permute-start.10 = (bf16[64,5120]{1,0:T(8,128)(2,1)S(1)}, bf16[64,5120]{1,0:T(8,128)(2,1)S(1)}, u32[]{:S(2)}, u32[]{:S(2)}) collective-permute-start(bf16[64,5120]{1,0:T(8,128)(2,1)S(1)} %add_convert_fusion.2), channel_id=1, source_target_pairs={{0,4},{2,14},{4,8},{6,2},{8,12},{10,6},{12,0},{14,10},{1,5},{3,15}... | collective-permute-start | bytes 1966088 | tf_op jit(solution)/shard_map/ppermute | solution.py:25
  183.8 13.1 %collective-permute-start.14 = (bf16[128,1280]{1,0:T(8,128)(2,1)S(1)}, bf16[128,1280]{1,0:T(8,128)(2,1)S(1)}, u32[]{:S(2)}, u32[]{:S(2)}) collective-permute-start(bf16[128,1280]{1,0:T(8,128)(2,1)S(1)} %get-tuple-element.84), channel_id=1, source_target_pairs={{0,16},{1,17},{2,19},{3,18},{4,20},{5,21},{6,23},{7,22},{8,24},{9,... | collective-permute-start | bytes 983048 | tf_op jit(solution)/shard_map/ppermute | solution.py:42
  185.5 11.3 %collective-permute-start.15 = (bf16[128,1280]{1,0:T(8,128)(2,1)S(1)}, bf16[128,1280]{1,0:T(8,128)(2,1)S(1)}, u32[]{:S(2)}, u32[]{:S(2)}) collective-permute-start(bf16[128,1280]{1,0:T(8,128)(2,1)S(1)} %get-tuple-element.85), channel_id=1, source_target_pairs={{0,1},{1,0},{2,3},{3,2},{4,5},{5,4},{6,7},{7,6},{8,9},{9,8},{10,11... | collective-permute-start | bytes 983048 | tf_op jit(solution)/shard_map/ppermute | solution.py:42
  185.9 15.9 %collective-permute-start.16 = (bf16[128,1280]{1,0:T(8,128)(2,1)S(1)}, bf16[128,1280]{1,0:T(8,128)(2,1)S(1)}, u32[]{:S(2)}, u32[]{:S(2)}) collective-permute-start(bf16[128,1280]{1,0:T(8,128)(2,1)S(1)} %get-tuple-element.86), channel_id=1, source_target_pairs={{0,17},{1,16},{2,18},{3,19},{4,21},{5,20},{6,22},{7,23},{8,25},{9,... | collective-permute-start | bytes 983048 | tf_op jit(solution)/shard_map/ppermute | solution.py:42
  186.7 15.2 %collective-permute-start.17 = (bf16[128,1280]{1,0:T(8,128)(2,1)S(1)}, bf16[128,1280]{1,0:T(8,128)(2,1)S(1)}, u32[]{:S(2)}, u32[]{:S(2)}) collective-permute-start(bf16[128,1280]{1,0:T(8,128)(2,1)S(1)} %get-tuple-element.92.refs_4_), channel_id=1, source_target_pairs={{0,4},{2,14},{4,8},{6,2},{8,12},{10,6},{12,0},{14,10},{1,5},{3,15}... | collective-permute-start | bytes 983048 | tf_op jit(solution)/shard_map/ppermute | solution.py:25
  205.8 15.5 %collective-permute-start.29 = (bf16[192,1280]{1,0:T(8,128)(2,1)S(1)}, bf16[192,1280]{1,0:T(8,128)(2,1)S(1)}, u32[]{:S(2)}, u32[]{:S(2)}) collective-permute-start(bf16[192,1280]{1,0:T(8,128)(2,1)S(1)} %get-tuple-element.101.refs_12_), channel_id=1, source_target_pairs={{0,4},{2,14},{4,8},{6,2},{8,12},{10,6},{12,0},{14,10},{1,5},{3,15}... | collective-permute-start | bytes 1474568 | tf_op jit(solution)/shard_map/ppermute | solution.py:25
  207.9 15.3 %collective-permute-start.27 = (bf16[192,1280]{1,0:T(8,128)(2,1)S(1)}, bf16[192,1280]{1,0:T(8,128)(2,1)S(1)}, u32[]{:S(2)}, u32[]{:S(2)}) collective-permute-start(bf16[192,1280]{1,0:T(8,128)(2,1)S(1)} %get-tuple-element.101.refs_12_), channel_id=1, source_target_pairs={{0,2},{2,0},{4,6},{6,4},{8,10},{10,8},{12,14},{14,12},{1,3},{3,1},... | collective-permute-start | bytes 1474568 | tf_op jit(solution)/shard_map/ppermute | solution.py:29
  207.9 15.1 %collective-permute-start.30 = (bf16[192,1280]{1,0:T(8,128)(2,1)S(1)}, bf16[192,1280]{1,0:T(8,128)(2,1)S(1)}, u32[]{:S(2)}, u32[]{:S(2)}) collective-permute-start(bf16[192,1280]{1,0:T(8,128)(2,1)S(1)} %get-tuple-element.102.refs_13_), channel_id=1, source_target_pairs={{0,4},{2,14},{4,8},{6,2},{8,12},{10,6},{12,0},{14,10},{1,5},{3,15}... | collective-permute-start | bytes 1474568 | tf_op jit(solution)/shard_map/ppermute | solution.py:25
  211.3 12.4 %collective-permute-start.28 = (bf16[192,1280]{1,0:T(8,128)(2,1)S(1)}, bf16[192,1280]{1,0:T(8,128)(2,1)S(1)}, u32[]{:S(2)}, u32[]{:S(2)}) collective-permute-start(bf16[192,1280]{1,0:T(8,128)(2,1)S(1)} %get-tuple-element.102.refs_13_), channel_id=1, source_target_pairs={{0,2},{2,0},{4,6},{6,4},{8,10},{10,8},{12,14},{14,12},{1,3},{3,1},... | collective-permute-start | bytes 1474568 | tf_op jit(solution)/shard_map/ppermute | solution.py:29
  221.4 23.5 %collective-permute-start.20 = (bf16[4,640,256]{2,1,0:T(8,128)(2,1)S(1)}, bf16[4,640,256]{2,1,0:T(8,128)(2,1)S(1)}, u32[]{:S(2)}, u32[]{:S(2)}) collective-permute-start(bf16[4,640,256]{2,1,0:T(8,128)(2,1)S(1)} %collective-permute-done.6.refs_2_.second_ref), channel_id=1, source_target_pairs={{0,16},{1,17},{2,19},{3,18},{4,20},{5,21},{6,23},{7,22},{8,24},{9,... | collective-permute-start | bytes 3932168 | tf_op jit(solution)/shard_map/ppermute | solution.py:42
  223.7 12.5 %collective-permute-start.34 = (bf16[192,1280]{1,0:T(8,128)(2,1)S(1)}, bf16[192,1280]{1,0:T(8,128)(2,1)S(1)}, u32[]{:S(2)}, u32[]{:S(2)}) collective-permute-start(bf16[192,1280]{1,0:T(8,128)(2,1)S(1)} %collective-permute-done.30.refs_17_), channel_id=1, source_target_pairs={{0,4},{2,14},{4,8},{6,2},{8,12},{10,6},{12,0},{14,10},{1,5},{3,15}... | collective-permute-start | bytes 1474568 | tf_op jit(solution)/shard_map/ppermute | solution.py:25
  226.6 13.0 %collective-permute-start.31 = (bf16[192,1280]{1,0:T(8,128)(2,1)S(1)}, bf16[192,1280]{1,0:T(8,128)(2,1)S(1)}, u32[]{:S(2)}, u32[]{:S(2)}) collective-permute-start(bf16[192,1280]{1,0:T(8,128)(2,1)S(1)} %collective-permute-done.29.refs_16_), channel_id=1, source_target_pairs={{0,2},{2,0},{4,6},{6,4},{8,10},{10,8},{12,14},{14,12},{1,3},{3,1},... | collective-permute-start | bytes 1474568 | tf_op jit(solution)/shard_map/ppermute | solution.py:29
  239.9 18.5 %collective-permute-start.37 = (bf16[192,1280]{1,0:T(8,128)(2,1)S(1)}, bf16[192,1280]{1,0:T(8,128)(2,1)S(1)}, u32[]{:S(2)}, u32[]{:S(2)}) collective-permute-start(bf16[192,1280]{1,0:T(8,128)(2,1)S(1)} %collective-permute-done.33.refs_20_), channel_id=1, source_target_pairs={{0,4},{2,14},{4,8},{6,2},{8,12},{10,6},{12,0},{14,10},{1,5},{3,15}... | collective-permute-start | bytes 1474568 | tf_op jit(solution)/shard_map/ppermute | solution.py:25
  241.4 17.1 %collective-permute-start.38 = (bf16[192,1280]{1,0:T(8,128)(2,1)S(1)}, bf16[192,1280]{1,0:T(8,128)(2,1)}, u32[]{:S(2)}, u32[]{:S(2)}) collective-permute-start(bf16[192,1280]{1,0:T(8,128)(2,1)S(1)} %collective-permute-done.34.refs_21_), channel_id=1, source_target_pairs={{0,4},{2,14},{4,8},{6,2},{8,12},{10,6},{12,0},{14,10},{1,5},{3,15}... | collective-permute-start | bytes 1474568 | tf_op jit(solution)/shard_map/ppermute | solution.py:25
  242.7 18.4 %collective-permute-start.44 = (bf16[48,640]{1,0:T(8,128)(2,1)}, bf16[48,640]{1,0:T(8,128)(2,1)S(1)}, u32[]{:S(2)}, u32[]{:S(2)}) collective-permute-start(bf16[48,640]{1,0:T(8,128)(2,1)} %get-tuple-element.117), channel_id=1, source_target_pairs={{0,4},{2,6},{4,8},{6,10},{8,12},{10,14},{12,0},{14,2},{1,5},{3,7},... | collective-permute-start | bytes 184328 | tf_op jit(solution)/shard_map/ppermute | solution.py:21
  243.6 17.4 %collective-permute-start.45 = (bf16[48,640]{1,0:T(8,128)(2,1)}, bf16[48,640]{1,0:T(8,128)(2,1)S(1)}, u32[]{:S(2)}, u32[]{:S(2)}) collective-permute-start(bf16[48,640]{1,0:T(8,128)(2,1)} %get-tuple-element.119), channel_id=1, source_target_pairs={{0,8},{2,10},{4,12},{6,14},{8,0},{10,2},{12,4},{14,6},{1,9},{3,11}... | collective-permute-start | bytes 184328 | tf_op jit(solution)/shard_map/ppermute | solution.py:21
  244.8 16.2 %collective-permute-start.46 = (bf16[48,640]{1,0:T(8,128)(2,1)S(1)}, bf16[48,640]{1,0:T(8,128)(2,1)S(1)}, u32[]{:S(2)}, u32[]{:S(2)}) collective-permute-start(bf16[48,640]{1,0:T(8,128)(2,1)S(1)} %get-tuple-element.118), channel_id=1, source_target_pairs={{0,12},{2,14},{4,0},{6,2},{8,4},{10,6},{12,8},{14,10},{1,13},{3,15... | collective-permute-start | bytes 184328 | tf_op jit(solution)/shard_map/ppermute | solution.py:21
  262.2 17.8 %all-to-all-start.2 = ((bf16[8,40,896]{2,1,0:T(8,128)(2,1)}), bf16[8,40,896]{2,1,0:T(8,128)(2,1)S(1)}, u32[]{:S(2)}, u32[]{:S(2)}) async-start(bf16[8,40,896]{2,1,0:T(8,128)(2,1)} %fusion.6), calls=%async_computation.2 | async-start | bytes 1146880 | tf_op jit(solution)/shard_map/all_to_all | solution.py:694
  274.3 12.1 %collective-permute-start.41 = (bf16[320,640]{1,0:T(8,128)(2,1)}, bf16[320,640]{1,0:T(8,128)(2,1)S(1)}, u32[]{:S(2)}, u32[]{:S(2)}) collective-permute-start(bf16[320,640]{1,0:T(8,128)(2,1)} %get-tuple-element.107), channel_id=1, source_target_pairs={{0,64},{16,80},{32,96},{48,112},{64,0},{80,16},{96,32},{112,48},{1... | collective-permute-start | bytes 1228808 | tf_op jit(solution)/shard_map/ppermute | solution.py:33
  277.3 18.9 %collective-permute-start.42 = (bf16[320,640]{1,0:T(8,128)(2,1)}, bf16[320,640]{1,0:T(8,128)(2,1)S(1)}, u32[]{:S(2)}, u32[]{:S(2)}) collective-permute-start(bf16[320,640]{1,0:T(8,128)(2,1)} %get-tuple-element.108), channel_id=1, source_target_pairs={{0,32},{16,48},{32,64},{48,80},{64,96},{80,112},{96,0},{112,16},{1... | collective-permute-start | bytes 1228808 | tf_op jit(solution)/shard_map/ppermute | solution.py:33
  277.6 18.6 %collective-permute-start.43 = (bf16[320,640]{1,0:T(8,128)(2,1)}, bf16[320,640]{1,0:T(8,128)(2,1)S(1)}, u32[]{:S(2)}, u32[]{:S(2)}) collective-permute-start(bf16[320,640]{1,0:T(8,128)(2,1)} %get-tuple-element.109), channel_id=1, source_target_pairs={{0,96},{16,112},{32,0},{48,16},{64,32},{80,48},{96,64},{112,80},{1... | collective-permute-start | bytes 1228808 | tf_op jit(solution)/shard_map/ppermute | solution.py:33
  (57 other events, 779.7 us)

commit v2 on v1

--- a/solution.py
+++ b/solution.py
@@ -523,7 +523,7 @@
         + [pl.BlockSpec((part.shape[0], tile), lambda i: (0, i)) for part in flat],
         out_specs=pl.BlockSpec((depth, tile), lambda i: (0, i)),
         out_shape=jax.ShapeDtypeStruct((depth, width), jnp.float32),
-        compiler_params=pltpu.CompilerParams(vmem_limit_bytes=VMEM_LIMIT),
+        compiler_params=pltpu.CompilerParams(vmem_limit_bytes=50 * 1024 * 1024),
         cost_estimate=FREE,
         name="early_product",
     )(*lefts, *flat)

time: 299 us -> 297 us (level)
  transfers between devices with their start and end apart: 50 -> 50, of which waited for: 18 -> 19; matrix products, arithmetic and copies ran while one was open for 4% -> 4% of each run, Pallas kernels for 16% -> 16%
where the time goes in v2:
time: 297 us
  waiting for transfers between devices  106 us (36%)
  starting transfers between devices  102 us (34%)
  Pallas kernels  70.1 us (24%)
  other arithmetic  9.43 us (3%)
  local copies, waits for them, and re-layouts  5.55 us (2%)
    ppermute x5, waiting for transfers between devices, pair_swap(): return lax.ppermute(value, 'pair', [(0, 1), (1, 0)])  55.6 us
    ppermute x15, starting transfers between devices, seq_ring(): lax.ppermute(value, 'seq', [(i, (i // 2 + side(i % 2)) % 4 * 2 + i % 2) f...  31.9 us
    ppermute x15, waiting for transfers between devices, seq_ring(): lax.ppermute(value, 'seq', [(i, (i // 2 + side(i % 2)) % 4 * 2 + i % 2) f...  24.6 us
    ppermute x15, starting transfers between devices, core_swap(): return lax.ppermute(value, 'seq', [(i, i ^ 1) for i in range(8)])  20.3 us
    pallas_call x1, Pallas kernels, attend(): pl.pallas_call(attend_kernel, grid_spec=pltpu.PrefetchScalarGridSpec(num_...  18.4 us
    ppermute x3, waiting for transfers between devices, y_shift(): lax.ppermute(value, 'dp', [(i, (i // 2 + apart) % 4 * 2 + i % 2) for i in...  14.8 us
    ppermute x5, starting transfers between devices, pair_swap(): return lax.ppermute(value, 'pair', [(0, 1), (1, 0)])  13.6 us
    pallas_call x1, Pallas kernels, project(): pl.pallas_call(project_kernel, grid=(width // tile,), in_specs=[left, lef...  11.7 us
  transfers between devices with their start and end apart: 50, of which 19 were waited for; matrix products, arithmetic and copies ran while one was open for 4% of the time, Pallas kernels for 16%

profile of v2, /device:TPU:1, one launch (start us, length us, event | category | flops | bytes accessed | tf_op | source)
XLA Modules:
  0.0 296.5 jit_solution(6288465272958878774)
XLA Ops:
  5.5 3.1 %pack.2 = bf16[8,272,640]{2,1,0:T(8,128)(2,1)} custom-call(bf16[128,5120]{1,0:T(8,128)(2,1)} %bitcast.74, bf16[128,5120]{1,0:T(8,128)(2,1)} %bitcast.75, bf16[128,5120]{1,0:T(8,128)(2,1)} %bitcast.76, bf16[128,5120]{1,0:T(8,128)(2,1)} %bitcast.77, bf16[128,5120]{1,0:T(8,128)(2,1)} %bitcast.78, bf16[128,5120]{1,0:T(8,128)(2,1)} %bitcast.79, ...), custom_call_target="tpu_custom_call" | custom-call | tf_op jit(solution)/shard_map/pack/pallas_call | solution.py:137
  8.7 5.5 %all-to-all-start = ((bf16[8,272,640]{2,1,0:T(8,128)(2,1)}), bf16[8,272,640]{2,1,0:T(8,128)(2,1)S(1)}, u32[]{:S(2)}, u32[]{:S(2)}) async-start(bf16[8,272,640]{2,1,0:T(8,128)(2,1)} %pack.2), calls=%async_computation | async-start | bytes 5570560 | tf_op jit(solution)/shard_map/all_to_all | solution.py:152
  16.9 29.5 %collective-permute-done.refs_4_.refs_5_.refs_6_.refs_7_ = bf16[128,5120]{1,0:T(8,128)(2,1)} collective-permute-done((bf16[128,5120]{1,0:T(8,128)(2,1)}, bf16[128,5120]{1,0:T(8,128)(2,1)}, u32[]{:S(2)}, u32[]{:S(2)}) %collective-permute-start) | collective-permute-done | bytes 1310752 | tf_op jit(solution)/shard_map/ppermute | solution.py:46
  47.9 3.0 %pack.3 = bf16[8,256,640]{2,1,0:T(8,128)(2,1)} custom-call(bf16[128,5120]{1,0:T(8,128)(2,1)} %bitcast.83, bf16[128,5120]{1,0:T(8,128)(2,1)} %bitcast.84, bf16[128,5120]{1,0:T(8,128)(2,1)} %bitcast.85, bf16[128,5120]{1,0:T(8,128)(2,1)} %bitcast.86, bf16[128,5120]{1,0:T(8,128)(2,1)} %collective-permute-done.refs_4_.refs_5_.refs_6_.refs_7_, ...), custom_call_target="tpu_custom_call" | custom-call | tf_op jit(solution)/shard_map/pack/pallas_call | solution.py:137
  50.9 5.3 %all-to-all-start.1 = ((bf16[8,256,640]{2,1,0:T(8,128)(2,1)}), bf16[8,256,640]{2,1,0:T(8,128)(2,1)}, u32[]{:S(2)}, u32[]{:S(2)}) async-start(bf16[8,256,640]{2,1,0:T(8,128)(2,1)} %pack.3), calls=%async_computation.1 | async-start | bytes 5242880 | tf_op jit(solution)/shard_map/all_to_all | solution.py:152
  60.3 4.5 %collective-permute-done.1 = bf16[8,16,640]{2,1,0:T(8,128)(2,1)S(1)} collective-permute-done((bf16[8,16,640]{2,1,0:T(8,128)(2,1)S(1)}, bf16[8,16,640]{2,1,0:T(8,128)(2,1)S(1)}, u32[]{:S(2)}, u32[]{:S(2)}) %collective-permute-start.1) | collective-permute-done | bytes 163872 | tf_op jit(solution)/shard_map/ppermute | solution.py:46
  70.2 6.9 %teacher.1 = f32[256,64]{1,0:T(8,128)} custom-call(bf16[256,5120]{1,0:T(8,128)(2,1)} %bitcast.87, bf16[256,16]{1,0:T(8,128)(2,1)} %fusion.10.hot_ref, bf16[16,16,640]{2,1,0:T(8,128)(2,1)} %bitcast.69, bf16[64,5120]{1,0:T(8,128)(2,1)} %bitcast.88), custom_call_target="tpu_custom_call" | custom-call | tf_op jit(solution)/shard_map/teacher/pallas_call | solution.py:104
  77.9 18.1 %collective-permute-done.2.value_ref = bf16[8,128,640]{2,1,0:T(8,128)(2,1)} collective-permute-done((bf16[8,128,640]{2,1,0:T(8,128)(2,1)}, bf16[8,128,640]{2,1,0:T(8,128)(2,1)}, u32[]{:S(2)}, u32[]{:S(2)}) %collective-permute-start.2) | collective-permute-done | bytes 1310752 | tf_op jit(solution)/shard_map/ppermute | solution.py:46
  96.3 18.4 %attend.1 = (bf16[4,128,640]{2,1,0:T(8,128)(2,1)S(1)}, bf16[4,128,640]{2,1,0:T(8,128)(2,1)S(1)}, bf16[4,640,256]{2,1,0:T(8,128)(2,1)}) custom-call(s32[8]{0:T(128)S(1)} %get-tuple-element.63.low_ref, s32[8]{0:T(128)S(1)} %get-tuple-element.64.high_ref, s32[8]{0:T(128)S(1)} %fusion.35.turn_ref, s32[8,128,1]{2,1,0:T(8,128)S(1)} %copy.28.qseg_ref, ...), custom_call_target="tpu_custom_call" | custom-call | tf_op jit(solution)/shard_map/attend/pallas_call | solution.py:252
  120.1 11.7 %project.1 = (bf16[128,5120]{1,0:T(8,128)(2,1)}, bf16[64,5120]{1,0:T(8,128)(2,1)}, bf16[64,5120]{1,0:T(8,128)(2,1)}, bf16[64,5120]{1,0:T(8,128)(2,1)}, bf16[64,5...) custom-call(bf16[4,128,640]{2,1,0:T(8,128)(2,1)} %copy-done.6, ...), custom_call_target="tpu_custom_call" | custom-call | tf_op jit(solution)/shard_map/project/pallas_call | solution.py:312
  137.2 5.0 %collective-permute-done.11 = bf16[64,5120]{1,0:T(8,128)(2,1)} collective-permute-done((bf16[64,5120]{1,0:T(8,128)(2,1)}, bf16[64,5120]{1,0:T(8,128)(2,1)}, u32[]{:S(2)}, u32[]{:S(2)}) %collective-permute-start.11) | collective-permute-done | bytes 655392 | tf_op jit(solution)/shard_map/ppermute | solution.py:25
  143.7 3.4 %collective-permute-start.12 = (bf16[64,5120]{1,0:T(8,128)(2,1)S(1)}, bf16[64,5120]{1,0:T(8,128)(2,1)S(1)}, u32[]{:S(2)}, u32[]{:S(2)}) collective-permute-start(bf16[64,5120]{1,0:T(8,128)(2,1)S(1)} %add_convert_fusion.1), channel_id=1, source_target_pairs={{0,4},{2,14},{4,8},{6,2},{8,12},{10,6},{12,0},{14,10},{1,5},{3,15}... | collective-permute-start | bytes 1966088 | tf_op jit(solution)/shard_map/ppermute | solution.py:25
  149.4 3.4 %collective-permute-start.9 = (bf16[64,5120]{1,0:T(8,128)(2,1)S(1)}, bf16[64,5120]{1,0:T(8,128)(2,1)S(1)}, u32[]{:S(2)}, u32[]{:S(2)}) collective-permute-start(bf16[64,5120]{1,0:T(8,128)(2,1)S(1)} %add_convert_fusion.3), channel_id=1, source_target_pairs={{0,4},{2,14},{4,8},{6,2},{8,12},{10,6},{12,0},{14,10},{1,5},{3,15}... | collective-permute-start | bytes 1966088 | tf_op jit(solution)/shard_map/ppermute | solution.py:25
  152.8 3.4 %collective-permute-done.12 = bf16[64,5120]{1,0:T(8,128)(2,1)S(1)} collective-permute-done((bf16[64,5120]{1,0:T(8,128)(2,1)S(1)}, bf16[64,5120]{1,0:T(8,128)(2,1)S(1)}, u32[]{:S(2)}, u32[]{:S(2)}) %collective-permute-start.12) | collective-permute-done | bytes 655392 | tf_op jit(solution)/shard_map/ppermute | solution.py:25
  156.4 3.2 %collective-permute-start.13 = (bf16[64,5120]{1,0:T(8,128)(2,1)S(1)}, bf16[64,5120]{1,0:T(8,128)(2,1)S(1)}, u32[]{:S(2)}, u32[]{:S(2)}) collective-permute-start(bf16[64,5120]{1,0:T(8,128)(2,1)S(1)} %add_convert_fusion), channel_id=1, source_target_pairs={{0,4},{2,14},{4,8},{6,2},{8,12},{10,6},{12,0},{14,10},{1,5},{3,15}... | collective-permute-start | bytes 1966088 | tf_op jit(solution)/shard_map/ppermute | solution.py:25
  159.6 3.6 %collective-permute-done.9 = bf16[64,5120]{1,0:T(8,128)(2,1)S(1)} collective-permute-done((bf16[64,5120]{1,0:T(8,128)(2,1)S(1)}, bf16[64,5120]{1,0:T(8,128)(2,1)S(1)}, u32[]{:S(2)}, u32[]{:S(2)}) %collective-permute-start.9) | collective-permute-done | bytes 655392 | tf_op jit(solution)/shard_map/ppermute | solution.py:25
  163.3 3.2 %collective-permute-start.10 = (bf16[64,5120]{1,0:T(8,128)(2,1)S(1)}, bf16[64,5120]{1,0:T(8,128)(2,1)S(1)}, u32[]{:S(2)}, u32[]{:S(2)}) collective-permute-start(bf16[64,5120]{1,0:T(8,128)(2,1)S(1)} %add_convert_fusion.2), channel_id=1, source_target_pairs={{0,4},{2,14},{4,8},{6,2},{8,12},{10,6},{12,0},{14,10},{1,5},{3,15}... | collective-permute-start | bytes 1966088 | tf_op jit(solution)/shard_map/ppermute | solution.py:25
  166.6 3.8 %collective-permute-start.7 = (bf16[128,64]{1,0:T(8,128)(2,1)S(1)}, bf16[128,64]{1,0:T(8,128)(2,1)S(1)}, u32[]{:S(2)}, u32[]{:S(2)}) collective-permute-start(bf16[128,64]{1,0:T(8,128)(2,1)S(1)} %constant_dynamic-slice_fusion.1), channel_id=1, source_target_pairs={{0,1},{1,0},{2,3},{3,2},{4,5},{5,4},{6,7},{7,6},{8,9},{9,8},{10,11... | collective-permute-start | bytes 49160 | tf_op jit(solution)/shard_map/ppermute | solution.py:46
  171.9 5.4 %collective-permute-done.10.la_ref = bf16[64,5120]{1,0:T(8,128)(2,1)S(1)} collective-permute-done((bf16[64,5120]{1,0:T(8,128)(2,1)S(1)}, bf16[64,5120]{1,0:T(8,128)(2,1)S(1)}, u32[]{:S(2)}, u32[]{:S(2)}) %collective-permute-start.10) | collective-permute-done | bytes 655392 | tf_op jit(solution)/shard_map/ppermute | solution.py:25
  177.2 4.9 %student.1 = (bf16[128,1280]{1,0:T(8,128)(2,1)S(1)}, bf16[128,1280]{1,0:T(8,128)(2,1)S(1)}, bf16[128,1280]{1,0:T(8,128)(2,1)S(1)}, bf16[128,1280]{1,0:T(8,128)(2...) custom-call(s32[2]{0:T(128)S(1)} %pad_add_fusion.1.x_ref, ...), custom_call_target="tpu_custom_call" | custom-call | tf_op jit(solution)/shard_map/student/pallas_call | solution.py:417
  186.6 3.1 %collective-permute-start.17 = (bf16[128,1280]{1,0:T(8,128)(2,1)S(1)}, bf16[128,1280]{1,0:T(8,128)(2,1)S(1)}, u32[]{:S(2)}, u32[]{:S(2)}) collective-permute-start(bf16[128,1280]{1,0:T(8,128)(2,1)S(1)} %get-tuple-element.92.refs_4_), channel_id=1, source_target_pairs={{0,4},{2,14},{4,8},{6,2},{8,12},{10,6},{12,0},{14,10},{1,5},{3,15}... | collective-permute-start | bytes 983048 | tf_op jit(solution)/shard_map/ppermute | solution.py:25
  192.5 3.6 %collective-permute-done.14.refs_0_ = bf16[128,1280]{1,0:T(8,128)(2,1)S(1)} collective-permute-done((bf16[128,1280]{1,0:T(8,128)(2,1)S(1)}, bf16[128,1280]{1,0:T(8,128)(2,1)S(1)}, u32[]{:S(2)}, u32[]{:S(2)}) %collective-permute-start.14) | collective-permute-done | bytes 327712 | tf_op jit(solution)/shard_map/ppermute | solution.py:42
  196.1 5.6 %collective-permute-done.16.refs_2_ = bf16[128,1280]{1,0:T(8,128)(2,1)S(1)} collective-permute-done((bf16[128,1280]{1,0:T(8,128)(2,1)S(1)}, bf16[128,1280]{1,0:T(8,128)(2,1)S(1)}, u32[]{:S(2)}, u32[]{:S(2)}) %collective-permute-start.16) | collective-permute-done | bytes 327712 | tf_op jit(solution)/shard_map/ppermute | solution.py:42
  215.8 4.2 %collective-permute-start.25 = (bf16[128,1280]{1,0:T(8,128)(2,1)S(1)}, bf16[128,1280]{1,0:T(8,128)(2,1)S(1)}, u32[]{:S(2)}, u32[]{:S(2)}) collective-permute-start(bf16[128,1280]{1,0:T(8,128)(2,1)S(1)} %collective-permute-done.23.refs_8_), channel_id=1, source_target_pairs={{0,4},{2,14},{4,8},{6,2},{8,12},{10,6},{12,0},{14,10},{1,5},{3,15}... | collective-permute-start | bytes 983048 | tf_op jit(solution)/shard_map/ppermute | solution.py:25
  229.6 3.4 %collective-permute-start.26 = (bf16[128,1280]{1,0:T(8,128)(2,1)S(1)}, bf16[128,1280]{1,0:T(8,128)(2,1)S(1)}, u32[]{:S(2)}, u32[]{:S(2)}) collective-permute-start(bf16[128,1280]{1,0:T(8,128)(2,1)S(1)} %collective-permute-done.25.refs_10_), channel_id=1, source_target_pairs={{0,2},{2,0},{4,6},{6,4},{8,10},{10,8},{12,14},{14,12},{1,3},{3,1},... | collective-permute-start | bytes 983048 | tf_op jit(solution)/shard_map/ppermute | solution.py:29
  234.8 3.4 %collective-permute-start.35 = (bf16[192,1280]{1,0:T(8,128)(2,1)S(1)}, bf16[192,1280]{1,0:T(8,128)(2,1)S(1)}, u32[]{:S(2)}, u32[]{:S(2)}) collective-permute-start(bf16[192,1280]{1,0:T(8,128)(2,1)S(1)} %collective-permute-done.33.refs_20_), channel_id=1, source_target_pairs={{0,2},{2,0},{4,6},{6,4},{8,10},{10,8},{12,14},{14,12},{1,3},{3,1},... | collective-permute-start | bytes 1474568 | tf_op jit(solution)/shard_map/ppermute | solution.py:29
  244.3 10.9 %early_product.1.early_ref = f32[640,1280]{1,0:T(8,128)} custom-call(bf16[4,640,256]{2,1,0:T(8,128)(2,1)} %get-tuple-element.73.refs_0_, bf16[4,640,256]{2,1,0:T(8,128)(2,1)} %copy-done.7, bf16[4,640,256]{2,1,0:T(8,128)(2,1)} %copy-done.8, bf16[4,640,256]{2,1,0:T(8,128)(2,1)} %copy-done.9, bf16[128,1280]{1,0:T(8,128)(2,1)S(1)} %get-tuple-element.92.refs_4_, ...), custom_call_target="tpu_custom_call" | custom-call | tf_op jit(solution)/shard_map/early_product/pallas_call | solution.py:519
  258.9 5.7 %all-to-all-start.2 = ((bf16[8,40,896]{2,1,0:T(8,128)(2,1)}), bf16[8,40,896]{2,1,0:T(8,128)(2,1)S(1)}, u32[]{:S(2)}, u32[]{:S(2)}) async-start(bf16[8,40,896]{2,1,0:T(8,128)(2,1)} %fusion.6), calls=%async_computation.2 | async-start | bytes 1146880 | tf_op jit(solution)/shard_map/all_to_all | solution.py:694
  265.6 7.0 %late_product.1 = (bf16[320,640]{1,0:T(8,128)(2,1)}, bf16[320,640]{1,0:T(8,128)(2,1)}, bf16[320,640]{1,0:T(8,128)(2,1)}, bf16[320,640]{1,0:T(8,128)(2,1)}) custom-call(s32[1]{0:T(128)} %bitcast.y_ref, bf16[4,640,256]{2,1,0:T(8,128)(2,1)} %copy-done.7, bf16[4,640,256]{2,1,0:T(8,128)(2,1)} %copy-done.8, bf16[4,640,256]{2,1,0:T(8,128)(2,1)} %copy-done.9, ...), custom_call_target="tpu_custom_call" | custom-call | tf_op jit(solution)/shard_map/late_product/pallas_call | solution.py:552
  272.6 3.0 collective-permute-start.41
  279.7 5.0 %collective-permute-done.41 = bf16[320,640]{1,0:T(8,128)(2,1)S(1)} collective-permute-done((bf16[320,640]{1,0:T(8,128)(2,1)}, bf16[320,640]{1,0:T(8,128)(2,1)S(1)}, u32[]{:S(2)}, u32[]{:S(2)}) %collective-permute-start.41) | collective-permute-done | bytes 409632 | tf_op jit(solution)/shard_map/ppermute | solution.py:33
  284.6 9.8 %collective-permute-done.42 = bf16[320,640]{1,0:T(8,128)(2,1)S(1)} collective-permute-done((bf16[320,640]{1,0:T(8,128)(2,1)}, bf16[320,640]{1,0:T(8,128)(2,1)S(1)}, u32[]{:S(2)}, u32[]{:S(2)}) %collective-permute-start.42) | collective-permute-done | bytes 409632 | tf_op jit(solution)/shard_map/ppermute | solution.py:33
  (188 shorter events, 85.4 us)
Async XLA Ops:
  0.6 95.4 %collective-permute-start.3 = (bf16[640,5120]{1,0:T(8,128)(2,1)}, bf16[640,5120]{1,0:T(8,128)(2,1)}, u32[]{:S(2)}, u32[]{:S(2)}) collective-permute-start(bf16[640,5120]{1,0:T(8,128)(2,1)} %w_own_ref.1), channel_id=1, source_target_pairs={{0,2},{2,0},{4,6},{6,4},{8,10},{10,8},{12,14},{14,12},{1,3},{3,1},... | collective-permute-start | bytes 19660808 | tf_op jit(solution)/shard_map/ppermute | solution.py:29
  8.7 39.2 %all-to-all-start = ((bf16[8,272,640]{2,1,0:T(8,128)(2,1)}), bf16[8,272,640]{2,1,0:T(8,128)(2,1)S(1)}, u32[]{:S(2)}, u32[]{:S(2)}) async-start(bf16[8,272,640]{2,1,0:T(8,128)(2,1)} %pack.2), calls=%async_computation | async-start | bytes 5570560 | tf_op jit(solution)/shard_map/all_to_all | solution.py:152
  14.2 32.2 %collective-permute-start = (bf16[128,5120]{1,0:T(8,128)(2,1)}, bf16[128,5120]{1,0:T(8,128)(2,1)}, u32[]{:S(2)}, u32[]{:S(2)}) collective-permute-start(bf16[128,5120]{1,0:T(8,128)(2,1)} %bitcast.82), channel_id=1, source_target_pairs={{0,1},{1,0},{2,3},{3,2},{4,5},{5,4},{6,7},{7,6},{8,9},{9,8},{10,11... | collective-permute-start | bytes 3932168 | tf_op jit(solution)/shard_map/ppermute | solution.py:46
  50.9 45.2 %all-to-all-start.1 = ((bf16[8,256,640]{2,1,0:T(8,128)(2,1)}), bf16[8,256,640]{2,1,0:T(8,128)(2,1)}, u32[]{:S(2)}, u32[]{:S(2)}) async-start(bf16[8,256,640]{2,1,0:T(8,128)(2,1)} %pack.3), calls=%async_computation.1 | async-start | bytes 5242880 | tf_op jit(solution)/shard_map/all_to_all | solution.py:152
  64.8 31.3 %collective-permute-start.2 = (bf16[8,128,640]{2,1,0:T(8,128)(2,1)}, bf16[8,128,640]{2,1,0:T(8,128)(2,1)}, u32[]{:S(2)}, u32[]{:S(2)}) collective-permute-start(bf16[8,128,640]{2,1,0:T(8,128)(2,1)} %get-tuple-element.60), channel_id=1, source_target_pairs={{0,1},{1,0},{2,3},{3,2},{4,5},{5,4},{6,7},{7,6},{8,9},{9,8},{10,11... | collective-permute-start | bytes 3932168 | tf_op jit(solution)/shard_map/ppermute | solution.py:46
  117.3 17.7 %collective-permute-start.5 = (bf16[4,640,256]{2,1,0:T(8,128)(2,1)}, bf16[4,640,256]{2,1,0:T(8,128)(2,1)S(1)}, u32[]{:S(2)}, u32[]{:S(2)}) collective-permute-start(bf16[4,640,256]{2,1,0:T(8,128)(2,1)} %get-tuple-element.73.refs_0_), channel_id=1, source_target_pairs={{0,16},{1,17},{2,19},{3,18},{4,20},{5,21},{6,23},{7,22},{8,24},{9,... | collective-permute-start | bytes 3932168 | tf_op jit(solution)/shard_map/ppermute | solution.py:42
  134.5 14.7 %collective-permute-start.8 = (bf16[64,5120]{1,0:T(8,128)(2,1)}, bf16[64,5120]{1,0:T(8,128)(2,1)S(1)}, u32[]{:S(2)}, u32[]{:S(2)}) collective-permute-start(bf16[64,5120]{1,0:T(8,128)(2,1)} %get-tuple-element.79), channel_id=1, source_target_pairs={{0,4},{2,14},{4,8},{6,2},{8,12},{10,6},{12,0},{14,10},{1,5},{3,15}... | collective-permute-start | bytes 1966088 | tf_op jit(solution)/shard_map/ppermute | solution.py:25
  135.0 36.8 %collective-permute-start.6 = (bf16[4,640,256]{2,1,0:T(8,128)(2,1)S(1)}, bf16[4,640,256]{2,1,0:T(8,128)(2,1)S(1)}, u32[]{:S(2)}, u32[]{:S(2)}) collective-permute-start(bf16[4,640,256]{2,1,0:T(8,128)(2,1)S(1)} %collective-permute-done.5.refs_1_.first_ref), channel_id=1, source_target_pairs={{0,16},{1,17},{2,19},{3,18},{4,20},{5,21},{6,23},{7,22},{8,24},{9,... | collective-permute-start | bytes 3932168 | tf_op jit(solution)/shard_map/ppermute | solution.py:42
  143.7 12.5 %collective-permute-start.12 = (bf16[64,5120]{1,0:T(8,128)(2,1)S(1)}, bf16[64,5120]{1,0:T(8,128)(2,1)S(1)}, u32[]{:S(2)}, u32[]{:S(2)}) collective-permute-start(bf16[64,5120]{1,0:T(8,128)(2,1)S(1)} %add_convert_fusion.1), channel_id=1, source_target_pairs={{0,4},{2,14},{4,8},{6,2},{8,12},{10,6},{12,0},{14,10},{1,5},{3,15}... | collective-permute-start | bytes 1966088 | tf_op jit(solution)/shard_map/ppermute | solution.py:25
  149.4 13.8 %collective-permute-start.9 = (bf16[64,5120]{1,0:T(8,128)(2,1)S(1)}, bf16[64,5120]{1,0:T(8,128)(2,1)S(1)}, u32[]{:S(2)}, u32[]{:S(2)}) collective-permute-start(bf16[64,5120]{1,0:T(8,128)(2,1)S(1)} %add_convert_fusion.3), channel_id=1, source_target_pairs={{0,4},{2,14},{4,8},{6,2},{8,12},{10,6},{12,0},{14,10},{1,5},{3,15}... | collective-permute-start | bytes 1966088 | tf_op jit(solution)/shard_map/ppermute | solution.py:25
  156.4 15.5 %collective-permute-start.13 = (bf16[64,5120]{1,0:T(8,128)(2,1)S(1)}, bf16[64,5120]{1,0:T(8,128)(2,1)S(1)}, u32[]{:S(2)}, u32[]{:S(2)}) collective-permute-start(bf16[64,5120]{1,0:T(8,128)(2,1)S(1)} %add_convert_fusion), channel_id=1, source_target_pairs={{0,4},{2,14},{4,8},{6,2},{8,12},{10,6},{12,0},{14,10},{1,5},{3,15}... | collective-permute-start | bytes 1966088 | tf_op jit(solution)/shard_map/ppermute | solution.py:25
  163.3 13.9 %collective-permute-start.10 = (bf16[64,5120]{1,0:T(8,128)(2,1)S(1)}, bf16[64,5120]{1,0:T(8,128)(2,1)S(1)}, u32[]{:S(2)}, u32[]{:S(2)}) collective-permute-start(bf16[64,5120]{1,0:T(8,128)(2,1)S(1)} %add_convert_fusion.2), channel_id=1, source_target_pairs={{0,4},{2,14},{4,8},{6,2},{8,12},{10,6},{12,0},{14,10},{1,5},{3,15}... | collective-permute-start | bytes 1966088 | tf_op jit(solution)/shard_map/ppermute | solution.py:25
  182.1 14.0 %collective-permute-start.14 = (bf16[128,1280]{1,0:T(8,128)(2,1)S(1)}, bf16[128,1280]{1,0:T(8,128)(2,1)S(1)}, u32[]{:S(2)}, u32[]{:S(2)}) collective-permute-start(bf16[128,1280]{1,0:T(8,128)(2,1)S(1)} %get-tuple-element.84), channel_id=1, source_target_pairs={{0,16},{1,17},{2,19},{3,18},{4,20},{5,21},{6,23},{7,22},{8,24},{9,... | collective-permute-start | bytes 983048 | tf_op jit(solution)/shard_map/ppermute | solution.py:42
  184.3 11.8 %collective-permute-start.15 = (bf16[128,1280]{1,0:T(8,128)(2,1)S(1)}, bf16[128,1280]{1,0:T(8,128)(2,1)S(1)}, u32[]{:S(2)}, u32[]{:S(2)}) collective-permute-start(bf16[128,1280]{1,0:T(8,128)(2,1)S(1)} %get-tuple-element.85), channel_id=1, source_target_pairs={{0,1},{1,0},{2,3},{3,2},{4,5},{5,4},{6,7},{7,6},{8,9},{9,8},{10,11... | collective-permute-start | bytes 983048 | tf_op jit(solution)/shard_map/ppermute | solution.py:42
  185.8 15.9 %collective-permute-start.16 = (bf16[128,1280]{1,0:T(8,128)(2,1)S(1)}, bf16[128,1280]{1,0:T(8,128)(2,1)S(1)}, u32[]{:S(2)}, u32[]{:S(2)}) collective-permute-start(bf16[128,1280]{1,0:T(8,128)(2,1)S(1)} %get-tuple-element.86), channel_id=1, source_target_pairs={{0,17},{1,16},{2,18},{3,19},{4,21},{5,20},{6,22},{7,23},{8,25},{9,... | collective-permute-start | bytes 983048 | tf_op jit(solution)/shard_map/ppermute | solution.py:42
  186.6 15.1 %collective-permute-start.17 = (bf16[128,1280]{1,0:T(8,128)(2,1)S(1)}, bf16[128,1280]{1,0:T(8,128)(2,1)S(1)}, u32[]{:S(2)}, u32[]{:S(2)}) collective-permute-start(bf16[128,1280]{1,0:T(8,128)(2,1)S(1)} %get-tuple-element.92.refs_4_), channel_id=1, source_target_pairs={{0,4},{2,14},{4,8},{6,2},{8,12},{10,6},{12,0},{14,10},{1,5},{3,15}... | collective-permute-start | bytes 983048 | tf_op jit(solution)/shard_map/ppermute | solution.py:25
  204.5 15.5 %collective-permute-start.29 = (bf16[192,1280]{1,0:T(8,128)(2,1)S(1)}, bf16[192,1280]{1,0:T(8,128)(2,1)S(1)}, u32[]{:S(2)}, u32[]{:S(2)}) collective-permute-start(bf16[192,1280]{1,0:T(8,128)(2,1)S(1)} %get-tuple-element.101.refs_12_), channel_id=1, source_target_pairs={{0,4},{2,14},{4,8},{6,2},{8,12},{10,6},{12,0},{14,10},{1,5},{3,15}... | collective-permute-start | bytes 1474568 | tf_op jit(solution)/shard_map/ppermute | solution.py:25
  206.6 15.3 %collective-permute-start.27 = (bf16[192,1280]{1,0:T(8,128)(2,1)S(1)}, bf16[192,1280]{1,0:T(8,128)(2,1)S(1)}, u32[]{:S(2)}, u32[]{:S(2)}) collective-permute-start(bf16[192,1280]{1,0:T(8,128)(2,1)S(1)} %get-tuple-element.101.refs_12_), channel_id=1, source_target_pairs={{0,2},{2,0},{4,6},{6,4},{8,10},{10,8},{12,14},{14,12},{1,3},{3,1},... | collective-permute-start | bytes 1474568 | tf_op jit(solution)/shard_map/ppermute | solution.py:29
  206.6 15.0 %collective-permute-start.30 = (bf16[192,1280]{1,0:T(8,128)(2,1)S(1)}, bf16[192,1280]{1,0:T(8,128)(2,1)S(1)}, u32[]{:S(2)}, u32[]{:S(2)}) collective-permute-start(bf16[192,1280]{1,0:T(8,128)(2,1)S(1)} %get-tuple-element.102.refs_13_), channel_id=1, source_target_pairs={{0,4},{2,14},{4,8},{6,2},{8,12},{10,6},{12,0},{14,10},{1,5},{3,15}... | collective-permute-start | bytes 1474568 | tf_op jit(solution)/shard_map/ppermute | solution.py:25
  210.8 11.6 %collective-permute-start.28 = (bf16[192,1280]{1,0:T(8,128)(2,1)S(1)}, bf16[192,1280]{1,0:T(8,128)(2,1)S(1)}, u32[]{:S(2)}, u32[]{:S(2)}) collective-permute-start(bf16[192,1280]{1,0:T(8,128)(2,1)S(1)} %get-tuple-element.102.refs_13_), channel_id=1, source_target_pairs={{0,2},{2,0},{4,6},{6,4},{8,10},{10,8},{12,14},{14,12},{1,3},{3,1},... | collective-permute-start | bytes 1474568 | tf_op jit(solution)/shard_map/ppermute | solution.py:29
  220.0 22.2 %collective-permute-start.20 = (bf16[4,640,256]{2,1,0:T(8,128)(2,1)S(1)}, bf16[4,640,256]{2,1,0:T(8,128)(2,1)S(1)}, u32[]{:S(2)}, u32[]{:S(2)}) collective-permute-start(bf16[4,640,256]{2,1,0:T(8,128)(2,1)S(1)} %collective-permute-done.6.refs_2_.second_ref), channel_id=1, source_target_pairs={{0,16},{1,17},{2,19},{3,18},{4,20},{5,21},{6,23},{7,22},{8,24},{9,... | collective-permute-start | bytes 3932168 | tf_op jit(solution)/shard_map/ppermute | solution.py:42
  222.4 12.4 %collective-permute-start.34 = (bf16[192,1280]{1,0:T(8,128)(2,1)S(1)}, bf16[192,1280]{1,0:T(8,128)(2,1)S(1)}, u32[]{:S(2)}, u32[]{:S(2)}) collective-permute-start(bf16[192,1280]{1,0:T(8,128)(2,1)S(1)} %collective-permute-done.30.refs_17_), channel_id=1, source_target_pairs={{0,4},{2,14},{4,8},{6,2},{8,12},{10,6},{12,0},{14,10},{1,5},{3,15}... | collective-permute-start | bytes 1474568 | tf_op jit(solution)/shard_map/ppermute | solution.py:25
  225.3 13.0 %collective-permute-start.31 = (bf16[192,1280]{1,0:T(8,128)(2,1)S(1)}, bf16[192,1280]{1,0:T(8,128)(2,1)S(1)}, u32[]{:S(2)}, u32[]{:S(2)}) collective-permute-start(bf16[192,1280]{1,0:T(8,128)(2,1)S(1)} %collective-permute-done.29.refs_16_), channel_id=1, source_target_pairs={{0,2},{2,0},{4,6},{6,4},{8,10},{10,8},{12,14},{14,12},{1,3},{3,1},... | collective-permute-start | bytes 1474568 | tf_op jit(solution)/shard_map/ppermute | solution.py:29
  238.6 16.7 %collective-permute-start.37 = (bf16[192,1280]{1,0:T(8,128)(2,1)S(1)}, bf16[192,1280]{1,0:T(8,128)(2,1)S(1)}, u32[]{:S(2)}, u32[]{:S(2)}) collective-permute-start(bf16[192,1280]{1,0:T(8,128)(2,1)S(1)} %collective-permute-done.33.refs_20_), channel_id=1, source_target_pairs={{0,4},{2,14},{4,8},{6,2},{8,12},{10,6},{12,0},{14,10},{1,5},{3,15}... | collective-permute-start | bytes 1474568 | tf_op jit(solution)/shard_map/ppermute | solution.py:25
  239.1 16.1 %collective-permute-start.38 = (bf16[192,1280]{1,0:T(8,128)(2,1)S(1)}, bf16[192,1280]{1,0:T(8,128)(2,1)}, u32[]{:S(2)}, u32[]{:S(2)}) collective-permute-start(bf16[192,1280]{1,0:T(8,128)(2,1)S(1)} %collective-permute-done.34.refs_21_), channel_id=1, source_target_pairs={{0,4},{2,14},{4,8},{6,2},{8,12},{10,6},{12,0},{14,10},{1,5},{3,15}... | collective-permute-start | bytes 1474568 | tf_op jit(solution)/shard_map/ppermute | solution.py:25
  239.8 18.0 %collective-permute-start.44 = (bf16[48,640]{1,0:T(8,128)(2,1)S(1)}, bf16[48,640]{1,0:T(8,128)(2,1)S(1)}, u32[]{:S(2)}, u32[]{:S(2)}) collective-permute-start(bf16[48,640]{1,0:T(8,128)(2,1)S(1)} %get-tuple-element.117), channel_id=1, source_target_pairs={{0,4},{2,6},{4,8},{6,10},{8,12},{10,14},{12,0},{14,2},{1,5},{3,7},... | collective-permute-start | bytes 184328 | tf_op jit(solution)/shard_map/ppermute | solution.py:21
  240.8 17.0 %collective-permute-start.45 = (bf16[48,640]{1,0:T(8,128)(2,1)S(1)}, bf16[48,640]{1,0:T(8,128)(2,1)S(1)}, u32[]{:S(2)}, u32[]{:S(2)}) collective-permute-start(bf16[48,640]{1,0:T(8,128)(2,1)S(1)} %get-tuple-element.119), channel_id=1, source_target_pairs={{0,8},{2,10},{4,12},{6,14},{8,0},{10,2},{12,4},{14,6},{1,9},{3,11}... | collective-permute-start | bytes 184328 | tf_op jit(solution)/shard_map/ppermute | solution.py:21
  242.2 15.6 %collective-permute-start.46 = (bf16[48,640]{1,0:T(8,128)(2,1)S(1)}, bf16[48,640]{1,0:T(8,128)(2,1)S(1)}, u32[]{:S(2)}, u32[]{:S(2)}) collective-permute-start(bf16[48,640]{1,0:T(8,128)(2,1)S(1)} %get-tuple-element.118), channel_id=1, source_target_pairs={{0,12},{2,14},{4,0},{6,2},{8,4},{10,6},{12,8},{14,10},{1,13},{3,15... | collective-permute-start | bytes 184328 | tf_op jit(solution)/shard_map/ppermute | solution.py:21
  258.9 19.3 %all-to-all-start.2 = ((bf16[8,40,896]{2,1,0:T(8,128)(2,1)}), bf16[8,40,896]{2,1,0:T(8,128)(2,1)S(1)}, u32[]{:S(2)}, u32[]{:S(2)}) async-start(bf16[8,40,896]{2,1,0:T(8,128)(2,1)} %fusion.6), calls=%async_computation.2 | async-start | bytes 1146880 | tf_op jit(solution)/shard_map/all_to_all | solution.py:694
  272.6 12.1 %collective-permute-start.41 = (bf16[320,640]{1,0:T(8,128)(2,1)}, bf16[320,640]{1,0:T(8,128)(2,1)S(1)}, u32[]{:S(2)}, u32[]{:S(2)}) collective-permute-start(bf16[320,640]{1,0:T(8,128)(2,1)} %get-tuple-element.107), channel_id=1, source_target_pairs={{0,64},{16,80},{32,96},{48,112},{64,0},{80,16},{96,32},{112,48},{1... | collective-permute-start | bytes 1228808 | tf_op jit(solution)/shard_map/ppermute | solution.py:33
  275.5 18.9 %collective-permute-start.42 = (bf16[320,640]{1,0:T(8,128)(2,1)}, bf16[320,640]{1,0:T(8,128)(2,1)S(1)}, u32[]{:S(2)}, u32[]{:S(2)}) collective-permute-start(bf16[320,640]{1,0:T(8,128)(2,1)} %get-tuple-element.108), channel_id=1, source_target_pairs={{0,32},{16,48},{32,64},{48,80},{64,96},{80,112},{96,0},{112,16},{1... | collective-permute-start | bytes 1228808 | tf_op jit(solution)/shard_map/ppermute | solution.py:33
  275.8 18.6 %collective-permute-start.43 = (bf16[320,640]{1,0:T(8,128)(2,1)}, bf16[320,640]{1,0:T(8,128)(2,1)S(1)}, u32[]{:S(2)}, u32[]{:S(2)}) collective-permute-start(bf16[320,640]{1,0:T(8,128)(2,1)} %get-tuple-element.109), channel_id=1, source_target_pairs={{0,96},{16,112},{32,0},{48,16},{64,32},{80,48},{96,64},{112,80},{1... | collective-permute-start | bytes 1228808 | tf_op jit(solution)/shard_map/ppermute | solution.py:33
  (46 other events, 475.4 us)

commit v3 on v2

--- a/solution.py
+++ b/solution.py
@@ -145,7 +145,7 @@
         + [pl.BlockSpec(array.shape, lambda i: (0, 0)) for array in shared],
         out_specs=pl.BlockSpec((half, height, cols), lambda i: (i, 0, 0)),
         out_shape=jax.ShapeDtypeStruct((groups, height, cols), tensors[0].dtype),
-        compiler_params=pltpu.CompilerParams(vmem_limit_bytes=VMEM_LIMIT),
+        compiler_params=pltpu.CompilerParams(vmem_limit_bytes=24 * 1024 * 1024),
         cost_estimate=FREE,
         name="pack",
     )(*[tensor for tensor in tensors for _ in range(half)], *shared)

time: 297 us -> 302 us (1.017)
  local copies, waits for them, and re-layouts: 5.55 us -> 16.9 us
  Pallas kernels: 70.1 us -> 63.4 us
  waiting for transfers between devices: 106 us -> 111 us
  starting transfers between devices: 102 us -> 97.7 us
    unnamed x56 -> x74, local copies, waits for them, and re-layouts: 2.72 us -> 13.2 us
    ppermute x5, starting transfers between devices: 13.6 us -> 8.5 us  [pair_swap(): return lax.ppermute(value, 'pair', [(0, 1), (1, 0)])]
    pallas_call x2, Pallas kernels: 6.16 us -> 1.2 us  [exchange(): pl.pallas_call(functools.partial(pack_kernel, count), grid=(2,), in_specs...]
    ppermute x5, waiting for transfers between devices: 55.6 us -> 60.1 us  [pair_swap(): return lax.ppermute(value, 'pair', [(0, 1), (1, 0)])]
  transfers between devices with their start and end apart: 50 -> 50, of which waited for: 19 -> 19; matrix products, arithmetic and copies ran while one was open for 4% -> 4% of each run, Pallas kernels for 16% -> 14%
where the time goes in v3:
time: 302 us; the launch traced here: 300 us
  waiting for transfers between devices  111 us (37%)
  starting transfers between devices  97.7 us (32%)
  Pallas kernels  63.4 us (21%)
  local copies, waits for them, and re-layouts  16.9 us (6%)
  other arithmetic  8.6 us (3%)
    ppermute x5, waiting for transfers between devices, pair_swap(): return lax.ppermute(value, 'pair', [(0, 1), (1, 0)])  60.1 us
    ppermute x15, starting transfers between devices, seq_ring(): lax.ppermute(value, 'seq', [(i, (i // 2 + side(i % 2)) % 4 * 2 + i % 2) f...  31.8 us
    ppermute x15, waiting for transfers between devices, seq_ring(): lax.ppermute(value, 'seq', [(i, (i // 2 + side(i % 2)) % 4 * 2 + i % 2) f...  25.4 us
    ppermute x15, starting transfers between devices, core_swap(): return lax.ppermute(value, 'seq', [(i, i ^ 1) for i in range(8)])  21.4 us
    pallas_call x1, Pallas kernels, attend(): pl.pallas_call(attend_kernel, grid_spec=pltpu.PrefetchScalarGridSpec(num_...  16.8 us
    ppermute x3, waiting for transfers between devices, y_shift(): lax.ppermute(value, 'dp', [(i, (i // 2 + apart) % 4 * 2 + i % 2) for i in...  14.8 us
    unnamed x74, local copies, waits for them, and re-layouts  13.2 us
    pallas_call x1, Pallas kernels, project(): pl.pallas_call(project_kernel, grid=(width // tile,), in_specs=[left, lef...  11.8 us
  transfers between devices with their start and end apart: 50, of which 19 were waited for; matrix products, arithmetic and copies ran while one was open for 4% of the time, Pallas kernels for 14%

profile of v3, /device:TPU:1, one launch (start us, length us, event | category | flops | bytes accessed | tf_op | source)
XLA Modules:
  0.0 300.5 jit_solution(6259300381868214557)
XLA Ops:
  9.8 5.5 %all-to-all-start = ((bf16[8,272,640]{2,1,0:T(8,128)(2,1)}), bf16[8,272,640]{2,1,0:T(8,128)(2,1)S(1)}, u32[]{:S(2)}, u32[]{:S(2)}) async-start(bf16[8,272,640]{2,1,0:T(8,128)(2,1)} %copy-done.7), calls=%async_computation | async-start | bytes 5570560 | tf_op jit(solution)/shard_map/all_to_all | solution.py:152
  18.1 29.4 %collective-permute-done.refs_4_.refs_5_.refs_6_.refs_7_ = bf16[128,5120]{1,0:T(8,128)(2,1)S(1)} collective-permute-done((bf16[128,5120]{1,0:T(8,128)(2,1)}, bf16[128,5120]{1,0:T(8,128)(2,1)S(1)}, u32[]{:S(2)}, u32[]{:S(2)}) %collective-permute-start) | collective-permute-done | bytes 1310752 | tf_op jit(solution)/shard_map/ppermute | solution.py:46
  53.8 5.3 %all-to-all-start.1 = ((bf16[8,256,640]{2,1,0:T(8,128)(2,1)}), bf16[8,256,640]{2,1,0:T(8,128)(2,1)}, u32[]{:S(2)}, u32[]{:S(2)}) async-start(bf16[8,256,640]{2,1,0:T(8,128)(2,1)} %copy-done.8), calls=%async_computation.1 | async-start | bytes 5242880 | tf_op jit(solution)/shard_map/all_to_all | solution.py:152
  63.2 4.5 %collective-permute-done.1 = bf16[8,16,640]{2,1,0:T(8,128)(2,1)S(1)} collective-permute-done((bf16[8,16,640]{2,1,0:T(8,128)(2,1)S(1)}, bf16[8,16,640]{2,1,0:T(8,128)(2,1)S(1)}, u32[]{:S(2)}, u32[]{:S(2)}) %collective-permute-start.1) | collective-permute-done | bytes 163872 | tf_op jit(solution)/shard_map/ppermute | solution.py:46
  73.1 6.9 %teacher.1 = f32[256,64]{1,0:T(8,128)} custom-call(bf16[256,5120]{1,0:T(8,128)(2,1)} %bitcast.87, bf16[256,16]{1,0:T(8,128)(2,1)} %fusion.10.hot_ref, bf16[16,16,640]{2,1,0:T(8,128)(2,1)} %bitcast.82, bf16[64,5120]{1,0:T(8,128)(2,1)} %bitcast.88), custom_call_target="tpu_custom_call" | custom-call | tf_op jit(solution)/shard_map/teacher/pallas_call | solution.py:104
  80.8 18.2 %collective-permute-done.2.value_ref = bf16[8,128,640]{2,1,0:T(8,128)(2,1)} collective-permute-done((bf16[8,128,640]{2,1,0:T(8,128)(2,1)}, bf16[8,128,640]{2,1,0:T(8,128)(2,1)}, u32[]{:S(2)}, u32[]{:S(2)}) %collective-permute-start.2) | collective-permute-done | bytes 1310752 | tf_op jit(solution)/shard_map/ppermute | solution.py:46
  101.0 16.8 %attend.1 = (bf16[4,128,640]{2,1,0:T(8,128)(2,1)S(1)}, bf16[4,128,640]{2,1,0:T(8,128)(2,1)S(1)}, bf16[4,640,256]{2,1,0:T(8,128)(2,1)}) custom-call(s32[8]{0:T(128)S(1)} %get-tuple-element.63.low_ref, s32[8]{0:T(128)S(1)} %get-tuple-element.64.high_ref, s32[8]{0:T(128)S(1)} %fusion.35.turn_ref, s32[8,128,1]{2,1,0:T(8,128)S(1)} %copy-done.11, ...), custom_call_target="tpu_custom_call" | custom-call | tf_op jit(solution)/shard_map/attend/pallas_call | solution.py:252
  120.5 4.6 %collective-permute-start.5 = (bf16[4,640,256]{2,1,0:T(8,128)(2,1)}, bf16[4,640,256]{2,1,0:T(8,128)(2,1)S(1)}, u32[]{:S(2)}, u32[]{:S(2)}) collective-permute-start(bf16[4,640,256]{2,1,0:T(8,128)(2,1)} %get-tuple-element.73.refs_0_), channel_id=1, source_target_pairs={{0,16},{1,17},{2,19},{3,18},{4,20},{5,21},{6,23},{7,22},{8,24},{9,... | collective-permute-start | bytes 3932168 | tf_op jit(solution)/shard_map/ppermute | solution.py:42
  125.9 11.8 %project.1 = (bf16[128,5120]{1,0:T(8,128)(2,1)}, bf16[64,5120]{1,0:T(8,128)(2,1)}, bf16[64,5120]{1,0:T(8,128)(2,1)}, bf16[64,5120]{1,0:T(8,128)(2,1)}, bf16[64,5...) custom-call(bf16[4,128,640]{2,1,0:T(8,128)(2,1)} %copy-done.14, ...), custom_call_target="tpu_custom_call" | custom-call | tf_op jit(solution)/shard_map/project/pallas_call | solution.py:312
  142.9 5.0 %collective-permute-done.11 = bf16[64,5120]{1,0:T(8,128)(2,1)S(1)} collective-permute-done((bf16[64,5120]{1,0:T(8,128)(2,1)}, bf16[64,5120]{1,0:T(8,128)(2,1)S(1)}, u32[]{:S(2)}, u32[]{:S(2)}) %collective-permute-start.11) | collective-permute-done | bytes 655392 | tf_op jit(solution)/shard_map/ppermute | solution.py:25
  149.2 3.4 %collective-permute-start.12 = (bf16[64,5120]{1,0:T(8,128)(2,1)S(1)}, bf16[64,5120]{1,0:T(8,128)(2,1)S(1)}, u32[]{:S(2)}, u32[]{:S(2)}) collective-permute-start(bf16[64,5120]{1,0:T(8,128)(2,1)S(1)} %add_convert_fusion.1), channel_id=1, source_target_pairs={{0,4},{2,14},{4,8},{6,2},{8,12},{10,6},{12,0},{14,10},{1,5},{3,15}... | collective-permute-start | bytes 1966088 | tf_op jit(solution)/shard_map/ppermute | solution.py:25
  155.1 3.4 %collective-permute-start.9 = (bf16[64,5120]{1,0:T(8,128)(2,1)S(1)}, bf16[64,5120]{1,0:T(8,128)(2,1)S(1)}, u32[]{:S(2)}, u32[]{:S(2)}) collective-permute-start(bf16[64,5120]{1,0:T(8,128)(2,1)S(1)} %add_convert_fusion.3), channel_id=1, source_target_pairs={{0,4},{2,14},{4,8},{6,2},{8,12},{10,6},{12,0},{14,10},{1,5},{3,15}... | collective-permute-start | bytes 1966088 | tf_op jit(solution)/shard_map/ppermute | solution.py:25
  158.5 3.4 %collective-permute-done.12 = bf16[64,5120]{1,0:T(8,128)(2,1)S(1)} collective-permute-done((bf16[64,5120]{1,0:T(8,128)(2,1)S(1)}, bf16[64,5120]{1,0:T(8,128)(2,1)S(1)}, u32[]{:S(2)}, u32[]{:S(2)}) %collective-permute-start.12) | collective-permute-done | bytes 655392 | tf_op jit(solution)/shard_map/ppermute | solution.py:25
  162.1 3.2 %collective-permute-start.13 = (bf16[64,5120]{1,0:T(8,128)(2,1)S(1)}, bf16[64,5120]{1,0:T(8,128)(2,1)S(1)}, u32[]{:S(2)}, u32[]{:S(2)}) collective-permute-start(bf16[64,5120]{1,0:T(8,128)(2,1)S(1)} %add_convert_fusion), channel_id=1, source_target_pairs={{0,4},{2,14},{4,8},{6,2},{8,12},{10,6},{12,0},{14,10},{1,5},{3,15}... | collective-permute-start | bytes 1966088 | tf_op jit(solution)/shard_map/ppermute | solution.py:25
  165.3 3.6 %collective-permute-done.9 = bf16[64,5120]{1,0:T(8,128)(2,1)S(1)} collective-permute-done((bf16[64,5120]{1,0:T(8,128)(2,1)S(1)}, bf16[64,5120]{1,0:T(8,128)(2,1)S(1)}, u32[]{:S(2)}, u32[]{:S(2)}) %collective-permute-start.9) | collective-permute-done | bytes 655392 | tf_op jit(solution)/shard_map/ppermute | solution.py:25
  169.1 3.2 %collective-permute-start.10 = (bf16[64,5120]{1,0:T(8,128)(2,1)S(1)}, bf16[64,5120]{1,0:T(8,128)(2,1)S(1)}, u32[]{:S(2)}, u32[]{:S(2)}) collective-permute-start(bf16[64,5120]{1,0:T(8,128)(2,1)S(1)} %add_convert_fusion.2), channel_id=1, source_target_pairs={{0,4},{2,14},{4,8},{6,2},{8,12},{10,6},{12,0},{14,10},{1,5},{3,15}... | collective-permute-start | bytes 1966088 | tf_op jit(solution)/shard_map/ppermute | solution.py:25
  172.7 4.2 %collective-permute-done.7 = bf16[128,64]{1,0:T(8,128)(2,1)S(1)} collective-permute-done((bf16[128,64]{1,0:T(8,128)(2,1)S(1)}, bf16[128,64]{1,0:T(8,128)(2,1)S(1)}, u32[]{:S(2)}, u32[]{:S(2)}) %collective-permute-start.7) | collective-permute-done | bytes 16416 | tf_op jit(solution)/shard_map/ppermute | solution.py:46
  177.0 6.0 %collective-permute-done.10.la_ref = bf16[64,5120]{1,0:T(8,128)(2,1)S(1)} collective-permute-done((bf16[64,5120]{1,0:T(8,128)(2,1)S(1)}, bf16[64,5120]{1,0:T(8,128)(2,1)S(1)}, u32[]{:S(2)}, u32[]{:S(2)}) %collective-permute-start.10) | collective-permute-done | bytes 655392 | tf_op jit(solution)/shard_map/ppermute | solution.py:25
  183.0 4.8 %student.1 = (bf16[128,1280]{1,0:T(8,128)(2,1)S(1)}, bf16[128,1280]{1,0:T(8,128)(2,1)S(1)}, bf16[128,1280]{1,0:T(8,128)(2,1)S(1)}, bf16[128,1280]{1,0:T(8,128)(2...) custom-call(s32[2]{0:T(128)S(1)} %pad_add_fusion.1.x_ref, ...), custom_call_target="tpu_custom_call" | custom-call | tf_op jit(solution)/shard_map/student/pallas_call | solution.py:417
  190.3 3.1 %collective-permute-start.17 = (bf16[128,1280]{1,0:T(8,128)(2,1)S(1)}, bf16[128,1280]{1,0:T(8,128)(2,1)S(1)}, u32[]{:S(2)}, u32[]{:S(2)}) collective-permute-start(bf16[128,1280]{1,0:T(8,128)(2,1)S(1)} %get-tuple-element.92.refs_4_), channel_id=1, source_target_pairs={{0,4},{2,14},{4,8},{6,2},{8,12},{10,6},{12,0},{14,10},{1,5},{3,15}... | collective-permute-start | bytes 983048 | tf_op jit(solution)/shard_map/ppermute | solution.py:25
  196.1 4.7 %collective-permute-done.14.refs_0_ = bf16[128,1280]{1,0:T(8,128)(2,1)S(1)} collective-permute-done((bf16[128,1280]{1,0:T(8,128)(2,1)S(1)}, bf16[128,1280]{1,0:T(8,128)(2,1)S(1)}, u32[]{:S(2)}, u32[]{:S(2)}) %collective-permute-start.14) | collective-permute-done | bytes 327712 | tf_op jit(solution)/shard_map/ppermute | solution.py:42
  200.8 5.0 %collective-permute-done.16.refs_2_ = bf16[128,1280]{1,0:T(8,128)(2,1)S(1)} collective-permute-done((bf16[128,1280]{1,0:T(8,128)(2,1)S(1)}, bf16[128,1280]{1,0:T(8,128)(2,1)S(1)}, u32[]{:S(2)}, u32[]{:S(2)}) %collective-permute-start.16) | collective-permute-done | bytes 327712 | tf_op jit(solution)/shard_map/ppermute | solution.py:42
  217.3 3.9 %collective-permute-done.19 = bf16[4,48,640]{2,1,0:T(8,128)(2,1)S(1)} collective-permute-done((bf16[4,48,640]{2,1,0:T(8,128)(2,1)S(1)}, bf16[4,48,640]{2,1,0:T(8,128)(2,1)S(1)}, u32[]{:S(2)}, u32[]{:S(2)}) %collective-permute-start.19) | collective-permute-done | bytes 245792 | tf_op jit(solution)/shard_map/ppermute | solution.py:46
  221.1 4.1 %collective-permute-start.25 = (bf16[128,1280]{1,0:T(8,128)(2,1)S(1)}, bf16[128,1280]{1,0:T(8,128)(2,1)S(1)}, u32[]{:S(2)}, u32[]{:S(2)}) collective-permute-start(bf16[128,1280]{1,0:T(8,128)(2,1)S(1)} %collective-permute-done.23.refs_8_), channel_id=1, source_target_pairs={{0,4},{2,14},{4,8},{6,2},{8,12},{10,6},{12,0},{14,10},{1,5},{3,15}... | collective-permute-start | bytes 983048 | tf_op jit(solution)/shard_map/ppermute | solution.py:25
  234.9 3.5 %collective-permute-start.26 = (bf16[128,1280]{1,0:T(8,128)(2,1)S(1)}, bf16[128,1280]{1,0:T(8,128)(2,1)S(1)}, u32[]{:S(2)}, u32[]{:S(2)}) collective-permute-start(bf16[128,1280]{1,0:T(8,128)(2,1)S(1)} %collective-permute-done.25.refs_10_), channel_id=1, source_target_pairs={{0,2},{2,0},{4,6},{6,4},{8,10},{10,8},{12,14},{14,12},{1,3},{3,1},... | collective-permute-start | bytes 983048 | tf_op jit(solution)/shard_map/ppermute | solution.py:29
  240.1 3.5 %collective-permute-start.35 = (bf16[192,1280]{1,0:T(8,128)(2,1)S(1)}, bf16[192,1280]{1,0:T(8,128)(2,1)S(1)}, u32[]{:S(2)}, u32[]{:S(2)}) collective-permute-start(bf16[192,1280]{1,0:T(8,128)(2,1)S(1)} %collective-permute-done.33.refs_20_), channel_id=1, source_target_pairs={{0,2},{2,0},{4,6},{6,4},{8,10},{10,8},{12,14},{14,12},{1,3},{3,1},... | collective-permute-start | bytes 1474568 | tf_op jit(solution)/shard_map/ppermute | solution.py:29
  249.6 10.9 %early_product.1.early_ref = f32[640,1280]{1,0:T(8,128)} custom-call(bf16[4,640,256]{2,1,0:T(8,128)(2,1)} %get-tuple-element.73.refs_0_, bf16[4,640,256]{2,1,0:T(8,128)(2,1)} %copy-done.15, bf16[4,640,256]{2,1,0:T(8,128)(2,1)} %copy-done.16, bf16[4,640,256]{2,1,0:T(8,128)(2,1)} %copy-done.17, bf16[128,1280]{1,0:T(8,128)(2,1)S(1)} %get-tuple-element.92.refs_4_, ...), custom_call_target="tpu_custom_call" | custom-call | tf_op jit(solution)/shard_map/early_product/pallas_call | solution.py:519
  264.2 4.4 %all-to-all-start.2 = ((bf16[8,40,896]{2,1,0:T(8,128)(2,1)}), bf16[8,40,896]{2,1,0:T(8,128)(2,1)S(1)}, u32[]{:S(2)}, u32[]{:S(2)}) async-start(bf16[8,40,896]{2,1,0:T(8,128)(2,1)} %fusion.6), calls=%async_computation.2 | async-start | bytes 1146880 | tf_op jit(solution)/shard_map/all_to_all | solution.py:694
  269.5 7.0 %late_product.1 = (bf16[320,640]{1,0:T(8,128)(2,1)}, bf16[320,640]{1,0:T(8,128)(2,1)}, bf16[320,640]{1,0:T(8,128)(2,1)}, bf16[320,640]{1,0:T(8,128)(2,1)}) custom-call(s32[1]{0:T(128)} %bitcast.y_ref, bf16[4,640,256]{2,1,0:T(8,128)(2,1)} %copy-done.15, bf16[4,640,256]{2,1,0:T(8,128)(2,1)} %copy-done.16, bf16[4,640,256]{2,1,0:T(8,128)(2,1)} %copy-done.17, ...), custom_call_target="tpu_custom_call" | custom-call | tf_op jit(solution)/shard_map/late_product/pallas_call | solution.py:552
  276.5 3.0 collective-permute-start.41
  283.6 5.0 %collective-permute-done.41 = bf16[320,640]{1,0:T(8,128)(2,1)S(1)} collective-permute-done((bf16[320,640]{1,0:T(8,128)(2,1)}, bf16[320,640]{1,0:T(8,128)(2,1)S(1)}, u32[]{:S(2)}, u32[]{:S(2)}) %collective-permute-start.41) | collective-permute-done | bytes 409632 | tf_op jit(solution)/shard_map/ppermute | solution.py:33
  288.6 9.8 %collective-permute-done.42 = bf16[320,640]{1,0:T(8,128)(2,1)S(1)} collective-permute-done((bf16[320,640]{1,0:T(8,128)(2,1)}, bf16[320,640]{1,0:T(8,128)(2,1)S(1)}, u32[]{:S(2)}, u32[]{:S(2)}) %collective-permute-start.42) | collective-permute-done | bytes 409632 | tf_op jit(solution)/shard_map/ppermute | solution.py:33
  (206 shorter events, 88.5 us)
Async XLA Ops:
  0.6 98.3 %collective-permute-start.3 = (bf16[640,5120]{1,0:T(8,128)(2,1)}, bf16[640,5120]{1,0:T(8,128)(2,1)}, u32[]{:S(2)}, u32[]{:S(2)}) collective-permute-start(bf16[640,5120]{1,0:T(8,128)(2,1)} %w_own_ref.1), channel_id=1, source_target_pairs={{0,2},{2,0},{4,6},{6,4},{8,10},{10,8},{12,14},{14,12},{1,3},{3,1},... | collective-permute-start | bytes 19660808 | tf_op jit(solution)/shard_map/ppermute | solution.py:29
  9.8 39.2 %all-to-all-start = ((bf16[8,272,640]{2,1,0:T(8,128)(2,1)}), bf16[8,272,640]{2,1,0:T(8,128)(2,1)S(1)}, u32[]{:S(2)}, u32[]{:S(2)}) async-start(bf16[8,272,640]{2,1,0:T(8,128)(2,1)} %copy-done.7), calls=%async_computation | async-start | bytes 5570560 | tf_op jit(solution)/shard_map/all_to_all | solution.py:152
  15.3 32.1 %collective-permute-start = (bf16[128,5120]{1,0:T(8,128)(2,1)}, bf16[128,5120]{1,0:T(8,128)(2,1)S(1)}, u32[]{:S(2)}, u32[]{:S(2)}) collective-permute-start(bf16[128,5120]{1,0:T(8,128)(2,1)} %bitcast.77), channel_id=1, source_target_pairs={{0,1},{1,0},{2,3},{3,2},{4,5},{5,4},{6,7},{7,6},{8,9},{9,8},{10,11... | collective-permute-start | bytes 3932168 | tf_op jit(solution)/shard_map/ppermute | solution.py:46
  53.8 45.2 %all-to-all-start.1 = ((bf16[8,256,640]{2,1,0:T(8,128)(2,1)}), bf16[8,256,640]{2,1,0:T(8,128)(2,1)}, u32[]{:S(2)}, u32[]{:S(2)}) async-start(bf16[8,256,640]{2,1,0:T(8,128)(2,1)} %copy-done.8), calls=%async_computation.1 | async-start | bytes 5242880 | tf_op jit(solution)/shard_map/all_to_all | solution.py:152
  67.7 31.3 %collective-permute-start.2 = (bf16[8,128,640]{2,1,0:T(8,128)(2,1)}, bf16[8,128,640]{2,1,0:T(8,128)(2,1)}, u32[]{:S(2)}, u32[]{:S(2)}) collective-permute-start(bf16[8,128,640]{2,1,0:T(8,128)(2,1)} %get-tuple-element.60), channel_id=1, source_target_pairs={{0,1},{1,0},{2,3},{3,2},{4,5},{5,4},{6,7},{7,6},{8,9},{9,8},{10,11... | collective-permute-start | bytes 3932168 | tf_op jit(solution)/shard_map/ppermute | solution.py:46
  120.5 20.3 %collective-permute-start.5 = (bf16[4,640,256]{2,1,0:T(8,128)(2,1)}, bf16[4,640,256]{2,1,0:T(8,128)(2,1)S(1)}, u32[]{:S(2)}, u32[]{:S(2)}) collective-permute-start(bf16[4,640,256]{2,1,0:T(8,128)(2,1)} %get-tuple-element.73.refs_0_), channel_id=1, source_target_pairs={{0,16},{1,17},{2,19},{3,18},{4,20},{5,21},{6,23},{7,22},{8,24},{9,... | collective-permute-start | bytes 3932168 | tf_op jit(solution)/shard_map/ppermute | solution.py:42
  140.3 14.7 %collective-permute-start.8 = (bf16[64,5120]{1,0:T(8,128)(2,1)}, bf16[64,5120]{1,0:T(8,128)(2,1)S(1)}, u32[]{:S(2)}, u32[]{:S(2)}) collective-permute-start(bf16[64,5120]{1,0:T(8,128)(2,1)} %get-tuple-element.79), channel_id=1, source_target_pairs={{0,4},{2,14},{4,8},{6,2},{8,12},{10,6},{12,0},{14,10},{1,5},{3,15}... | collective-permute-start | bytes 1966088 | tf_op jit(solution)/shard_map/ppermute | solution.py:25
  140.7 36.2 %collective-permute-start.6 = (bf16[4,640,256]{2,1,0:T(8,128)(2,1)S(1)}, bf16[4,640,256]{2,1,0:T(8,128)(2,1)S(1)}, u32[]{:S(2)}, u32[]{:S(2)}) collective-permute-start(bf16[4,640,256]{2,1,0:T(8,128)(2,1)S(1)} %collective-permute-done.5.refs_1_.first_ref), channel_id=1, source_target_pairs={{0,16},{1,17},{2,19},{3,18},{4,20},{5,21},{6,23},{7,22},{8,24},{9,... | collective-permute-start | bytes 3932168 | tf_op jit(solution)/shard_map/ppermute | solution.py:42
  149.2 12.7 %collective-permute-start.12 = (bf16[64,5120]{1,0:T(8,128)(2,1)S(1)}, bf16[64,5120]{1,0:T(8,128)(2,1)S(1)}, u32[]{:S(2)}, u32[]{:S(2)}) collective-permute-start(bf16[64,5120]{1,0:T(8,128)(2,1)S(1)} %add_convert_fusion.1), channel_id=1, source_target_pairs={{0,4},{2,14},{4,8},{6,2},{8,12},{10,6},{12,0},{14,10},{1,5},{3,15}... | collective-permute-start | bytes 1966088 | tf_op jit(solution)/shard_map/ppermute | solution.py:25
  155.1 13.8 %collective-permute-start.9 = (bf16[64,5120]{1,0:T(8,128)(2,1)S(1)}, bf16[64,5120]{1,0:T(8,128)(2,1)S(1)}, u32[]{:S(2)}, u32[]{:S(2)}) collective-permute-start(bf16[64,5120]{1,0:T(8,128)(2,1)S(1)} %add_convert_fusion.3), channel_id=1, source_target_pairs={{0,4},{2,14},{4,8},{6,2},{8,12},{10,6},{12,0},{14,10},{1,5},{3,15}... | collective-permute-start | bytes 1966088 | tf_op jit(solution)/shard_map/ppermute | solution.py:25
  162.1 14.9 %collective-permute-start.13 = (bf16[64,5120]{1,0:T(8,128)(2,1)S(1)}, bf16[64,5120]{1,0:T(8,128)(2,1)S(1)}, u32[]{:S(2)}, u32[]{:S(2)}) collective-permute-start(bf16[64,5120]{1,0:T(8,128)(2,1)S(1)} %add_convert_fusion), channel_id=1, source_target_pairs={{0,4},{2,14},{4,8},{6,2},{8,12},{10,6},{12,0},{14,10},{1,5},{3,15}... | collective-permute-start | bytes 1966088 | tf_op jit(solution)/shard_map/ppermute | solution.py:25
  169.1 13.9 %collective-permute-start.10 = (bf16[64,5120]{1,0:T(8,128)(2,1)S(1)}, bf16[64,5120]{1,0:T(8,128)(2,1)S(1)}, u32[]{:S(2)}, u32[]{:S(2)}) collective-permute-start(bf16[64,5120]{1,0:T(8,128)(2,1)S(1)} %add_convert_fusion.2), channel_id=1, source_target_pairs={{0,4},{2,14},{4,8},{6,2},{8,12},{10,6},{12,0},{14,10},{1,5},{3,15}... | collective-permute-start | bytes 1966088 | tf_op jit(solution)/shard_map/ppermute | solution.py:25
  187.8 13.1 %collective-permute-start.14 = (bf16[128,1280]{1,0:T(8,128)(2,1)S(1)}, bf16[128,1280]{1,0:T(8,128)(2,1)S(1)}, u32[]{:S(2)}, u32[]{:S(2)}) collective-permute-start(bf16[128,1280]{1,0:T(8,128)(2,1)S(1)} %get-tuple-element.84), channel_id=1, source_target_pairs={{0,16},{1,17},{2,19},{3,18},{4,20},{5,21},{6,23},{7,22},{8,24},{9,... | collective-permute-start | bytes 983048 | tf_op jit(solution)/shard_map/ppermute | solution.py:42
  189.6 11.3 %collective-permute-start.15 = (bf16[128,1280]{1,0:T(8,128)(2,1)S(1)}, bf16[128,1280]{1,0:T(8,128)(2,1)S(1)}, u32[]{:S(2)}, u32[]{:S(2)}) collective-permute-start(bf16[128,1280]{1,0:T(8,128)(2,1)S(1)} %get-tuple-element.85), channel_id=1, source_target_pairs={{0,1},{1,0},{2,3},{3,2},{4,5},{5,4},{6,7},{7,6},{8,9},{9,8},{10,11... | collective-permute-start | bytes 983048 | tf_op jit(solution)/shard_map/ppermute | solution.py:42
  189.6 16.2 %collective-permute-start.16 = (bf16[128,1280]{1,0:T(8,128)(2,1)S(1)}, bf16[128,1280]{1,0:T(8,128)(2,1)S(1)}, u32[]{:S(2)}, u32[]{:S(2)}) collective-permute-start(bf16[128,1280]{1,0:T(8,128)(2,1)S(1)} %get-tuple-element.86), channel_id=1, source_target_pairs={{0,17},{1,16},{2,18},{3,19},{4,21},{5,20},{6,22},{7,23},{8,25},{9,... | collective-permute-start | bytes 983048 | tf_op jit(solution)/shard_map/ppermute | solution.py:42
  190.3 15.6 %collective-permute-start.17 = (bf16[128,1280]{1,0:T(8,128)(2,1)S(1)}, bf16[128,1280]{1,0:T(8,128)(2,1)S(1)}, u32[]{:S(2)}, u32[]{:S(2)}) collective-permute-start(bf16[128,1280]{1,0:T(8,128)(2,1)S(1)} %get-tuple-element.92.refs_4_), channel_id=1, source_target_pairs={{0,4},{2,14},{4,8},{6,2},{8,12},{10,6},{12,0},{14,10},{1,5},{3,15}... | collective-permute-start | bytes 983048 | tf_op jit(solution)/shard_map/ppermute | solution.py:25
  209.8 15.5 %collective-permute-start.29 = (bf16[192,1280]{1,0:T(8,128)(2,1)S(1)}, bf16[192,1280]{1,0:T(8,128)(2,1)S(1)}, u32[]{:S(2)}, u32[]{:S(2)}) collective-permute-start(bf16[192,1280]{1,0:T(8,128)(2,1)S(1)} %get-tuple-element.101.refs_12_), channel_id=1, source_target_pairs={{0,4},{2,14},{4,8},{6,2},{8,12},{10,6},{12,0},{14,10},{1,5},{3,15}... | collective-permute-start | bytes 1474568 | tf_op jit(solution)/shard_map/ppermute | solution.py:25
  211.9 15.2 %collective-permute-start.27 = (bf16[192,1280]{1,0:T(8,128)(2,1)S(1)}, bf16[192,1280]{1,0:T(8,128)(2,1)S(1)}, u32[]{:S(2)}, u32[]{:S(2)}) collective-permute-start(bf16[192,1280]{1,0:T(8,128)(2,1)S(1)} %get-tuple-element.101.refs_12_), channel_id=1, source_target_pairs={{0,2},{2,0},{4,6},{6,4},{8,10},{10,8},{12,14},{14,12},{1,3},{3,1},... | collective-permute-start | bytes 1474568 | tf_op jit(solution)/shard_map/ppermute | solution.py:29
  211.9 15.0 %collective-permute-start.30 = (bf16[192,1280]{1,0:T(8,128)(2,1)S(1)}, bf16[192,1280]{1,0:T(8,128)(2,1)S(1)}, u32[]{:S(2)}, u32[]{:S(2)}) collective-permute-start(bf16[192,1280]{1,0:T(8,128)(2,1)S(1)} %get-tuple-element.102.refs_13_), channel_id=1, source_target_pairs={{0,4},{2,14},{4,8},{6,2},{8,12},{10,6},{12,0},{14,10},{1,5},{3,15}... | collective-permute-start | bytes 1474568 | tf_op jit(solution)/shard_map/ppermute | solution.py:25
  214.6 13.1 %collective-permute-start.28 = (bf16[192,1280]{1,0:T(8,128)(2,1)S(1)}, bf16[192,1280]{1,0:T(8,128)(2,1)S(1)}, u32[]{:S(2)}, u32[]{:S(2)}) collective-permute-start(bf16[192,1280]{1,0:T(8,128)(2,1)S(1)} %get-tuple-element.102.refs_13_), channel_id=1, source_target_pairs={{0,2},{2,0},{4,6},{6,4},{8,10},{10,8},{12,14},{14,12},{1,3},{3,1},... | collective-permute-start | bytes 1474568 | tf_op jit(solution)/shard_map/ppermute | solution.py:29
  225.3 22.2 %collective-permute-start.20 = (bf16[4,640,256]{2,1,0:T(8,128)(2,1)S(1)}, bf16[4,640,256]{2,1,0:T(8,128)(2,1)S(1)}, u32[]{:S(2)}, u32[]{:S(2)}) collective-permute-start(bf16[4,640,256]{2,1,0:T(8,128)(2,1)S(1)} %collective-permute-done.6.refs_2_.second_ref), channel_id=1, source_target_pairs={{0,16},{1,17},{2,19},{3,18},{4,20},{5,21},{6,23},{7,22},{8,24},{9,... | collective-permute-start | bytes 3932168 | tf_op jit(solution)/shard_map/ppermute | solution.py:42
  227.7 12.4 %collective-permute-start.34 = (bf16[192,1280]{1,0:T(8,128)(2,1)S(1)}, bf16[192,1280]{1,0:T(8,128)(2,1)S(1)}, u32[]{:S(2)}, u32[]{:S(2)}) collective-permute-start(bf16[192,1280]{1,0:T(8,128)(2,1)S(1)} %collective-permute-done.30.refs_17_), channel_id=1, source_target_pairs={{0,4},{2,14},{4,8},{6,2},{8,12},{10,6},{12,0},{14,10},{1,5},{3,15}... | collective-permute-start | bytes 1474568 | tf_op jit(solution)/shard_map/ppermute | solution.py:25
  230.6 13.0 %collective-permute-start.31 = (bf16[192,1280]{1,0:T(8,128)(2,1)S(1)}, bf16[192,1280]{1,0:T(8,128)(2,1)S(1)}, u32[]{:S(2)}, u32[]{:S(2)}) collective-permute-start(bf16[192,1280]{1,0:T(8,128)(2,1)S(1)} %collective-permute-done.29.refs_16_), channel_id=1, source_target_pairs={{0,2},{2,0},{4,6},{6,4},{8,10},{10,8},{12,14},{14,12},{1,3},{3,1},... | collective-permute-start | bytes 1474568 | tf_op jit(solution)/shard_map/ppermute | solution.py:29
  243.9 16.6 %collective-permute-start.37 = (bf16[192,1280]{1,0:T(8,128)(2,1)S(1)}, bf16[192,1280]{1,0:T(8,128)(2,1)S(1)}, u32[]{:S(2)}, u32[]{:S(2)}) collective-permute-start(bf16[192,1280]{1,0:T(8,128)(2,1)S(1)} %collective-permute-done.33.refs_20_), channel_id=1, source_target_pairs={{0,4},{2,14},{4,8},{6,2},{8,12},{10,6},{12,0},{14,10},{1,5},{3,15}... | collective-permute-start | bytes 1474568 | tf_op jit(solution)/shard_map/ppermute | solution.py:25
  244.4 16.1 %collective-permute-start.38 = (bf16[192,1280]{1,0:T(8,128)(2,1)S(1)}, bf16[192,1280]{1,0:T(8,128)(2,1)S(1)}, u32[]{:S(2)}, u32[]{:S(2)}) collective-permute-start(bf16[192,1280]{1,0:T(8,128)(2,1)S(1)} %collective-permute-done.34.refs_21_), channel_id=1, source_target_pairs={{0,4},{2,14},{4,8},{6,2},{8,12},{10,6},{12,0},{14,10},{1,5},{3,15}... | collective-permute-start | bytes 1474568 | tf_op jit(solution)/shard_map/ppermute | solution.py:25
  245.1 18.0 %collective-permute-start.44 = (bf16[48,640]{1,0:T(8,128)(2,1)S(1)}, bf16[48,640]{1,0:T(8,128)(2,1)S(1)}, u32[]{:S(2)}, u32[]{:S(2)}) collective-permute-start(bf16[48,640]{1,0:T(8,128)(2,1)S(1)} %get-tuple-element.117), channel_id=1, source_target_pairs={{0,4},{2,6},{4,8},{6,10},{8,12},{10,14},{12,0},{14,2},{1,5},{3,7},... | collective-permute-start | bytes 184328 | tf_op jit(solution)/shard_map/ppermute | solution.py:21
  246.1 17.0 %collective-permute-start.45 = (bf16[48,640]{1,0:T(8,128)(2,1)S(1)}, bf16[48,640]{1,0:T(8,128)(2,1)S(1)}, u32[]{:S(2)}, u32[]{:S(2)}) collective-permute-start(bf16[48,640]{1,0:T(8,128)(2,1)S(1)} %get-tuple-element.119), channel_id=1, source_target_pairs={{0,8},{2,10},{4,12},{6,14},{8,0},{10,2},{12,4},{14,6},{1,9},{3,11}... | collective-permute-start | bytes 184328 | tf_op jit(solution)/shard_map/ppermute | solution.py:21
  247.5 15.6 %collective-permute-start.46 = (bf16[48,640]{1,0:T(8,128)(2,1)S(1)}, bf16[48,640]{1,0:T(8,128)(2,1)S(1)}, u32[]{:S(2)}, u32[]{:S(2)}) collective-permute-start(bf16[48,640]{1,0:T(8,128)(2,1)S(1)} %get-tuple-element.118), channel_id=1, source_target_pairs={{0,12},{2,14},{4,0},{6,2},{8,4},{10,6},{12,8},{14,10},{1,13},{3,15... | collective-permute-start | bytes 184328 | tf_op jit(solution)/shard_map/ppermute | solution.py:21
  264.2 18.0 %all-to-all-start.2 = ((bf16[8,40,896]{2,1,0:T(8,128)(2,1)}), bf16[8,40,896]{2,1,0:T(8,128)(2,1)S(1)}, u32[]{:S(2)}, u32[]{:S(2)}) async-start(bf16[8,40,896]{2,1,0:T(8,128)(2,1)} %fusion.6), calls=%async_computation.2 | async-start | bytes 1146880 | tf_op jit(solution)/shard_map/all_to_all | solution.py:694
  276.5 12.1 %collective-permute-start.41 = (bf16[320,640]{1,0:T(8,128)(2,1)}, bf16[320,640]{1,0:T(8,128)(2,1)S(1)}, u32[]{:S(2)}, u32[]{:S(2)}) collective-permute-start(bf16[320,640]{1,0:T(8,128)(2,1)} %get-tuple-element.107), channel_id=1, source_target_pairs={{0,64},{16,80},{32,96},{48,112},{64,0},{80,16},{96,32},{112,48},{1... | collective-permute-start | bytes 1228808 | tf_op jit(solution)/shard_map/ppermute | solution.py:33
  279.5 18.9 %collective-permute-start.42 = (bf16[320,640]{1,0:T(8,128)(2,1)}, bf16[320,640]{1,0:T(8,128)(2,1)S(1)}, u32[]{:S(2)}, u32[]{:S(2)}) collective-permute-start(bf16[320,640]{1,0:T(8,128)(2,1)} %get-tuple-element.108), channel_id=1, source_target_pairs={{0,32},{16,48},{32,64},{48,80},{64,96},{80,112},{96,0},{112,16},{1... | collective-permute-start | bytes 1228808 | tf_op jit(solution)/shard_map/ppermute | solution.py:33
  279.8 18.6 %collective-permute-start.43 = (bf16[320,640]{1,0:T(8,128)(2,1)}, bf16[320,640]{1,0:T(8,128)(2,1)S(1)}, u32[]{:S(2)}, u32[]{:S(2)}) collective-permute-start(bf16[320,640]{1,0:T(8,128)(2,1)} %get-tuple-element.109), channel_id=1, source_target_pairs={{0,96},{16,112},{32,0},{48,16},{64,32},{80,48},{96,64},{112,80},{1... | collective-permute-start | bytes 1228808 | tf_op jit(solution)/shard_map/ppermute | solution.py:33
  (55 other events, 486.1 us)
